TPU v7x, 32 devices: a whole 2x2x4 slice. The times are simulated.
32 devices in a mesh: rep: 8 (over z, y), grp: 4 (over x, core).
Axes of the slice: x: 2, y: 2, z: 4, core: 2. Of those that a mesh axis runs over, the one named last changes fastest.
Arguments:
- inputs: bfloat16 [4096, 2048], P(('rep', 'grp')), may hold values from -6 to 6
- cotangent: bfloat16 [4096, 2048], P(('rep', 'grp')), may hold values from -6 to 6
- segment_ids: int32 [4096], P(('rep', 'grp')), may hold values from 0 to 127, never falling along the last dimension, each value on 1 to 96 neighbouring positions
- weights: bfloat16 [2048, 33408], P(('grp', 'rep')), may hold values from -5 to 3
- master: float32 [2048, 33408], P(('grp', 'rep')), may hold values from -5 to 3
- moment_one: float32 [2048, 33408], P(('grp', 'rep')), may hold values from -6 to 6
- moment_two: float32 [2048, 33408], P(('grp', 'rep')), may hold values from 0.5 to 50
- step: int32 [1], replicated, may hold values from 1 to 8
- learn_rate: float32 [1], replicated, may hold values from 0.05 to 0.3
- beta_one: float32 [1], replicated, may hold values from 0.8 to 0.95
- beta_two: float32 [1], replicated, may hold values from 0.95 to 0.999
Outputs:
- output: bfloat16 [4096, 2048], P(('rep', 'grp'))
- input_grad: bfloat16 [4096, 2048], P(('rep', 'grp'))
- grads: float32 [2048, 33408], P(('grp', 'rep'))
- moment_one_new: float32 [2048, 33408], P(('grp', 'rep'))
- moment_two_new: float32 [2048, 33408], P(('grp', 'rep'))
- master_new: float32 [2048, 33408], P(('grp', 'rep'))
- new_weights: bfloat16 [2048, 33408], P(('grp', 'rep'))
- gain_grads: float32 [2048, 2], P(('grp', 'rep'))
Inputs may be any that keep to these rules, and one draw needn't show every extreme that they name: `segment_ids`: never falls from token to token; each document has 1 to 96 tokens, one exactly 96.
All inputs are finite; a program needn't handle non-finite values.
Results may differ from a plain program's by a relative error of at most 0.014.
The roundings to bfloat16 on the way count: a program that leaves them out, or rounds other values in their place, can miss the bound.
Values may be sent and summed in bfloat16 or wider, within the bound.
A program may use at most 768 MiB of HBM per device.

v0:
```python
import jax
import jax.numpy as jnp
from jax import lax
from jax.sharding import PartitionSpec as P

D = 2048
H = 16
DK = 128
DV = 256
FF = 5632
CONV = 4
SPAN = 64
EXTRA = 128
KD = 2048
VD = 4096


EPS_NORM = 1e-06
EPS_GATED = 1e-05
EPS_ADAM = 1e-08
DECAY_WEIGHT = 0.1
HIGH_PRECISION = lax.Precision.HIGHEST


def norm_scale(values, epsilon):
    return lax.rsqrt(jnp.mean(values * values, axis=-1, keepdims=True) + epsilon)


def document_starts(segments):
    leading = jnp.ones(segments.shape[:-1] + (1,), jnp.int32)
    changes = (segments[..., 1:] != segments[..., :-1]).astype(jnp.int32)
    return jnp.concatenate([leading, changes], axis=-1)


def short_conv(channels, kernel, doc_ids):
    summed = channels * kernel[CONV - 1]
    for offset in range(1, CONV):
        shifted = jnp.concatenate(
            [jnp.zeros_like(channels[..., :offset, :]), channels[..., :-offset, :]], axis=-2
        )
        shifted_docs = jnp.concatenate(
            [jnp.full_like(doc_ids[..., :offset], -1), doc_ids[..., :-offset]], axis=-1
        )
        same_doc = (shifted_docs == doc_ids).astype(jnp.float32)
        summed = summed + shifted * same_doc[..., None] * kernel[CONV - 1 - offset]
    return summed


def unit_lower_inverse(lower):
    identity = jnp.eye(SPAN, dtype=jnp.float32)
    powered = -lower
    result = identity + powered
    reached = 2
    while reached < SPAN:
        powered = jnp.einsum("...ij,...jk->...ik", powered, powered, precision=HIGH_PRECISION)
        result = jnp.einsum(
            "...ij,...jk->...ik", result, identity + powered, precision=HIGH_PRECISION
        )
        reached = reached * 2
    return result


def span_delta(query_vecs, key_vecs, value_vecs, beta_gate, log_decay, starts):
    length = query_vecs.shape[0]
    blocks = length // SPAN

    def arrange(member):
        shaped = member.reshape((blocks, SPAN) + member.shape[1:])
        return jnp.swapaxes(shaped, 1, 2)

    query_blk = arrange(query_vecs)
    key_blk = arrange(key_vecs)
    value_blk = arrange(value_vecs)
    beta_blk = arrange(beta_gate)
    cumul = jnp.cumsum(arrange(log_decay), axis=-1)
    doc_blk = jnp.cumsum(starts.reshape(blocks, SPAN), axis=1)
    alive = (doc_blk == 0).astype(jnp.float32)
    position = jnp.arange(SPAN)
    same_doc = doc_blk[:, :, None] == doc_blk[:, None, :]
    mask_incl = (same_doc & (position[:, None] >= position[None, :]))[:, None]
    mask_strict = (same_doc & (position[:, None] > position[None, :]))[:, None]
    gap_decay = cumul[..., :, None] - cumul[..., None, :]
    pair_incl = jnp.where(mask_incl, jnp.exp(jnp.where(mask_incl, gap_decay, 0.0)), 0.0)
    pair_strict = jnp.where(mask_strict, pair_incl, 0.0)
    key_key = jnp.einsum("nhtk,nhsk->nhts", key_blk, key_blk, precision=HIGH_PRECISION)
    query_key = jnp.einsum("nhtk,nhsk->nhts", query_blk, key_blk, precision=HIGH_PRECISION)
    inverse = unit_lower_inverse(beta_blk[..., :, None] * pair_strict * key_key)
    head_decay = jnp.exp(cumul) * alive[:, None, :]
    from_values = jnp.einsum(
        "nhts,nhsv->nhtv", inverse, beta_blk[..., None] * value_blk, precision=HIGH_PRECISION
    )
    from_state = jnp.einsum(
        "nhts,nhsk->nhtk",
        inverse,
        (beta_blk * head_decay)[..., None] * key_blk,
        precision=HIGH_PRECISION,
    )
    query_state = head_decay[..., None] * query_blk
    query_pairs = pair_incl * query_key
    mask_end = mask_incl[:, :, SPAN - 1, :]
    last_cum = cumul[..., SPAN - 1 :]
    end_weight = jnp.where(mask_end, jnp.exp(jnp.where(mask_end, last_cum - cumul, 0.0)), 0.0)
    key_end = end_weight[..., None] * key_blk
    state_keep = jnp.exp(cumul[..., SPAN - 1]) * alive[:, SPAN - 1][:, None]

    def carry_step(running_memory, pieces):
        value_portion, state_portion, query_portion, pairs_part, final_piece_part, keep_part = (
            pieces
        )
        state_update = value_portion - jnp.einsum(
            "nzu,nui->nzi", state_portion, running_memory, precision=HIGH_PRECISION
        )
        emitted_output = jnp.einsum(
            "nzu,nui->nzi", query_portion, running_memory, precision=HIGH_PRECISION
        ) + jnp.einsum("hts,hsv->htv", pairs_part, state_update, precision=HIGH_PRECISION)
        running_memory = keep_part[:, None, None] * running_memory + jnp.einsum(
            "zqy,zql->zyl", final_piece_part, state_update, precision=HIGH_PRECISION
        )
        return (running_memory, emitted_output)

    initial = jnp.zeros((H, DK, DV), jnp.float32)
    final_memory, emitted_output = lax.scan(
        carry_step,
        initial,
        (from_values, from_state, query_state, query_pairs, key_end, state_keep),
    )
    return jnp.swapaxes(emitted_output, 1, 2).reshape(length, H, DV)


def mixer_core(mixed, gate_pair, extra, starts):
    conv_cols = CONV * (2 * KD + VD) // D
    kernel = extra[:, 2 * H + 2 : 2 * H + 2 + conv_cols].reshape(CONV, 2 * KD + VD)
    column = extra[:, 2 * H + 2 + conv_cols]
    a_log = column[0:H]
    dt_bias = column[H : 2 * H]
    out_gain = column[2 * H : 2 * H + DV]
    doc_ids = jnp.cumsum(starts, axis=-1)
    convolved = jax.nn.silu(short_conv(mixed[:, : 2 * KD + VD], kernel, doc_ids))
    length = mixed.shape[0]
    query_vecs = convolved[:, :KD].reshape(length, H, DK)
    key_vecs = convolved[:, KD : 2 * KD].reshape(length, H, DK)
    value_vecs = convolved[:, 2 * KD :].reshape(length, H, DV)
    query_vecs = (
        query_vecs
        * lax.rsqrt(jnp.sum(query_vecs * query_vecs, axis=-1, keepdims=True) + EPS_NORM)
        * DK ** (-0.5)
    )
    key_vecs = key_vecs * lax.rsqrt(jnp.sum(key_vecs * key_vecs, axis=-1, keepdims=True) + EPS_NORM)
    beta_gate = jax.nn.sigmoid(gate_pair[:, H:])
    log_decay = -jnp.exp(a_log) * jax.nn.softplus(gate_pair[:, :H] + dt_bias)
    outputs = span_delta(query_vecs, key_vecs, value_vecs, beta_gate, log_decay, starts)
    out_gate = mixed[:, 2 * KD + VD :].reshape(length, H, DV)
    normed = outputs * norm_scale(outputs, EPS_GATED) * out_gain * jax.nn.silu(out_gate)
    return normed.reshape(length, VD)


def contract_rows(left, right):
    return lax.dot_general(
        left, right, (((0,), (0,)), ((), ())), preferred_element_type=jnp.float32
    )


def contract_cols(left, right):
    return lax.dot_general(
        left, right, (((1,), (1,)), ((), ())), preferred_element_type=jnp.float32
    )


def on_device(
    inputs,
    cotangent,
    segment_ids,
    weights,
    master,
    moment_one,
    moment_two,
    step,
    learn_rate,
    beta_one,
    beta_two,
):
    width = inputs.shape[1]
    mixer_end = 2 * KD + 2 * VD
    ffn_start = mixer_end + VD
    down_start = ffn_start + 2 * FF
    extra_start = down_start + FF
    group_rows = lax.all_gather(weights, "rep", axis=0, tiled=True)
    full_weights = lax.all_gather(group_rows, "grp", axis=0, tiled=True)
    extra = full_weights[:, extra_start:].astype(jnp.float32)
    gain_one = extra[:, 2 * H]
    gain_two = extra[:, 2 * H + 1]
    starts = document_starts(segment_ids)
    tokens = inputs.astype(jnp.float32)
    scale_one = norm_scale(tokens, EPS_NORM)
    unit_one = tokens * scale_one
    normed = (unit_one * gain_one).astype(jnp.bfloat16)
    mixed = jnp.dot(normed, full_weights[:, :mixer_end], preferred_element_type=jnp.float32)
    gate_pair = jnp.dot(
        normed,
        full_weights[:, extra_start : extra_start + 2 * H],
        preferred_element_type=jnp.float32,
    )

    def core_call(mixed_in, pair_in, extra_in):
        return mixer_core(mixed_in, pair_in, extra_in, starts)

    core_out, core_pull = jax.vjp(core_call, mixed, gate_pair, extra)
    gated = core_out.astype(jnp.bfloat16)
    hidden = tokens + contract_cols(gated, full_weights[:, mixer_end:ffn_start])
    scale_two = norm_scale(hidden, EPS_NORM)
    unit_two = hidden * scale_two
    normed_two = (unit_two * gain_two).astype(jnp.bfloat16)
    gate_up = jnp.dot(
        normed_two, full_weights[:, ffn_start:down_start], preferred_element_type=jnp.float32
    )
    gate_part = gate_up[:, :FF]
    up_part = gate_up[:, FF:]
    sigmoid_gate = jax.nn.sigmoid(gate_part)
    activated = (gate_part * sigmoid_gate * up_part).astype(jnp.bfloat16)
    output = (hidden + contract_cols(activated, full_weights[:, down_start:extra_start])).astype(
        jnp.bfloat16
    )
    d_act = jnp.dot(
        cotangent, full_weights[:, down_start:extra_start], preferred_element_type=jnp.float32
    )
    d_gate = d_act * up_part * sigmoid_gate * (1 + gate_part * (1 - sigmoid_gate))
    d_up = d_act * gate_part * sigmoid_gate
    d_gate_up = jnp.concatenate([d_gate, d_up], axis=1).astype(jnp.bfloat16)
    d_normed_two = contract_cols(d_gate_up, full_weights[:, ffn_start:down_start])
    gain_two_grad = jnp.sum(d_normed_two * unit_two, axis=0)
    scaled_two = d_normed_two * gain_two
    d_hidden = cotangent.astype(jnp.float32) + scale_two * (
        scaled_two - unit_two * jnp.mean(scaled_two * unit_two, axis=1, keepdims=True)
    )
    d_branch = d_hidden.astype(jnp.bfloat16)
    d_gated = jnp.dot(
        d_branch, full_weights[:, mixer_end:ffn_start], preferred_element_type=jnp.float32
    )
    d_mixed, d_pair, extra_core_grad = core_pull(d_gated)
    d_mixed_low = d_mixed.astype(jnp.bfloat16)
    d_pair_low = d_pair.astype(jnp.bfloat16)
    d_normed = contract_cols(d_mixed_low, full_weights[:, :mixer_end]) + contract_cols(
        d_pair_low, full_weights[:, extra_start : extra_start + 2 * H]
    )
    gain_one_grad = jnp.sum(d_normed * unit_one, axis=0)
    scaled_one = d_normed * gain_one
    d_input = d_hidden + scale_one * (
        scaled_one - unit_one * jnp.mean(scaled_one * unit_one, axis=1, keepdims=True)
    )
    input_grad = d_input.astype(jnp.bfloat16)
    pair_grad = contract_rows(normed, d_pair_low)
    extra_grad = extra_core_grad + jnp.concatenate(
        [
            pair_grad,
            gain_one_grad[:, None],
            gain_two_grad[:, None],
            jnp.zeros((width, EXTRA - 2 * H - 2), jnp.float32),
        ],
        axis=1,
    )
    group_size = lax.axis_size("grp")
    replica_size = lax.axis_size("rep")
    piece_rows = width // (group_size * replica_size)
    ordered = jnp.arange(piece_rows * lax.axis_size(("rep", "grp")))
    rep_of = ordered // (group_size * piece_rows)
    grp_of = ordered // piece_rows % group_size
    within = ordered % piece_rows
    source = grp_of * (width // group_size) + rep_of * piece_rows + within

    def take_cols(matrix):
        return jnp.take(matrix, source, axis=1)

    grads = lax.psum_scatter(
        jnp.concatenate(
            [
                contract_rows(take_cols(normed), d_mixed_low),
                contract_rows(take_cols(d_branch), gated),
                contract_rows(take_cols(normed_two), d_gate_up),
                contract_rows(take_cols(cotangent), activated),
                jnp.take(extra_grad, source, axis=0),
            ],
            axis=1,
        ),
        ("rep", "grp"),
        scatter_dimension=0,
        tiled=True,
    )
    gain_grads = grads[:, extra_start + 2 * H : extra_start + 2 * H + 2]
    step_size = learn_rate[0]
    first_beta = beta_one[0]
    second_beta = beta_two[0]
    step_float = step[0].astype(jnp.float32)
    moment_one_new = first_beta * moment_one + (1 - first_beta) * grads
    moment_two_new = second_beta * moment_two + (1 - second_beta) * grads * grads
    first_hat = moment_one_new / (1 - first_beta**step_float)
    second_hat = moment_two_new / (1 - second_beta**step_float)
    master_new = master - step_size * (
        first_hat / (jnp.sqrt(second_hat) + EPS_ADAM) + DECAY_WEIGHT * master
    )
    new_weights = master_new.astype(jnp.bfloat16)
    return (
        output,
        input_grad,
        grads,
        moment_one_new,
        moment_two_new,
        master_new,
        new_weights,
        gain_grads,
    )


def solution(mesh):
    return jax.shard_map(
        on_device,
        mesh=mesh,
        in_specs=(
            P(("rep", "grp"), None),
            P(("rep", "grp"), None),
            P(("rep", "grp")),
            P(("grp", "rep"), None),
            P(("grp", "rep"), None),
            P(("grp", "rep"), None),
            P(("grp", "rep"), None),
            P(),
            P(),
            P(),
            P(),
        ),
        out_specs=(
            P(("rep", "grp"), None),
            P(("rep", "grp"), None),
            P(("grp", "rep"), None),
            P(("grp", "rep"), None),
            P(("grp", "rep"), None),
            P(("grp", "rep"), None),
            P(("grp", "rep"), None),
            P(("grp", "rep"), None),
        ),
        check_vma=False,
    )
```

profile of v0, /device:TPU:0, one launch (start us, length us, event | category | flops | bytes accessed | tf_op | source)
XLA Modules:
  0.0 4419.3 jit_solution(1948961002648886083)
XLA Ops:
  7.9 654.3 %all-gather.3.cloned.1.call-done = bf16[512,33408]{1,0:T(8,128)(2,1)} async-done(((bf16[64,33408]{1,0:T(8,128)(2,1)}), bf16[512,33408]{1,0:T(8,128)(2,1)}) %all-gather.3.cloned.1.call-update) | async-done | bytes 34209808 | tf_op jit(solution)/shard_map/all_gather | solution.py:187
  668.3 8.0 gather_fusion.4
  678.6 777.4 %all-gather.5.cloned.1.call-done = bf16[2048,33408]{1,0:T(8,128)(2,1)} async-done(((bf16[512,33408]{1,0:T(8,128)(2,1)}), bf16[2048,33408]{1,0:T(8,128)(2,1)}) %all-gather.5.cloned.1.call-update) | async-done | bytes 136839184 | tf_op jit(solution)/shard_map/all_gather | solution.py:188
  1460.1 20.3 fusion.110
  1480.5 4.8 slice.206
  1494.1 8.7 fusion.130
  1510.4 3.8 fusion.311
  1516.8 3.8 fusion.320
  1523.1 3.9 fusion.321
  1529.5 3.7 fusion.322
  1541.5 3.5 convolution_add_fusion.15
  1545.1 3.9 fusion.201
  1550.6 14.3 fusion.197
  1572.4 4.3 fusion.145
  1579.3 3.4 fusion.181
  1588.1 19.3 while.46
  1617.3 3.2 multiply_convert_fusion.3
  1620.5 12.1 multiply_reduce_fusion.12
  1632.8 19.0 fusion.114
  1651.8 13.7 multiply_convert_fusion.1
  1665.6 22.3 multiply_reduce_fusion.7
  1689.6 7.3 fusion.120
  1697.0 4.0 fusion.141
  1702.3 3.5 multiply_reduce_fusion.4
  1713.6 42.8 while.47
  1756.4 3.6 fusion.185
  1760.1 4.9 fusion.152
  1770.2 5.7 bitcast_multiply_fusion.1
  1779.7 5.2 fusion.174
  1785.7 3.8 broadcast_multiply_fusion
  1822.5 3.9 multiply_select_fusion
  1844.2 4.7 add_add_fusion.3
  1848.9 8.1 multiply_reduce_fusion.3
  1866.3 3.5 fusion.143
  1871.0 8.0 gather_fusion.1
  1879.0 8.0 gather_fusion.2
  1887.0 8.0 gather_fusion.3
  1897.8 9.4 multiply_add_fusion.2
  1907.3 24.4 fusion.108
  1931.7 3.4 fusion.162
  1939.4 37.1 convolution_dynamic-update-slice_fusion
  1976.5 14.4 convolution_dynamic-update-slice_fusion.3
  1990.8 34.0 convolution_dynamic-update-slice_fusion.1
  2027.9 5.5 gather_fusion
  2033.3 19.3 convolution_dynamic-update-slice_fusion.2
  2059.9 15.1 fusion.137
  2075.0 2312.3 %reduce-scatter.2.cloned.1.call-done = f32[64,33408]{1,0:T(8,128)} async-done(((f32[2048,33408]{1,0:T(8,128)}), f32[64,33408]{1,0:T(8,128)}) %reduce-scatter.2.cloned.1.call-update) | async-done | bytes 8552464 | tf_op jit(solution)/shard_map/reduce_scatter | solution.py:273
  4388.8 23.4 fusion.313
  (657 shorter events, 229.2 us)
Async XLA Ops:
  7.2 655.1 %all-gather.3.cloned.1.call-start = ((), (), s32[]{:S(2)}) async-start(), calls=%async_computation.1 | async-start | bytes 38486016 | tf_op jit(solution)/shard_map/all_gather | solution.py:187
  7.9 1448.1 %all-gather.5.cloned.1.call-start = ((), (), s32[]{:S(2)}) async-start(), calls=%async_computation.2 | async-start | bytes 171048960 | tf_op jit(solution)/shard_map/all_gather | solution.py:188
  662.3 3725.1 %reduce-scatter.2.cloned.1.call-start = ((), (), s32[]{:S(2)}) async-start(), calls=%async_computation.3 | async-start | bytes 282230784 | tf_op jit(solution)/shard_map/reduce_scatter | solution.py:273
  664.4 829.7 %copy-start.166 = (f32[128]{0:T(128)}, f32[128]{0:T(128)S(1)}, u32[]{:S(2)}) copy-start(f32[128]{0:T(128)S(1)} %get-tuple-element.753) | copy-start | bytes 1540
  664.4 829.7 %copy-start.168 = (f32[128]{0:T(128)}, f32[128]{0:T(128)S(1)}, u32[]{:S(2)}) copy-start(f32[128]{0:T(128)S(1)} %get-tuple-element.754) | copy-start | bytes 1540
  666.2 11.9 copy-start.80
  668.3 788.8 %copy-start.135 = (s32[2048]{0:T(1024)}, s32[2048]{0:T(1024)S(1)}, u32[]{:S(2)}) copy-start(s32[2048]{0:T(1024)S(1)} %get-tuple-element.773) | copy-start | bytes 24580
  677.4 859.1 %copy-start.155 = (f32[2,64]{1,0:T(2,128)}, f32[2,64]{1,0:T(2,128)S(1)}, u32[]{:S(2)}) copy-start(f32[2,64]{1,0:T(2,128)S(1)} %compare_convert_fusion.3) | copy-start | bytes 1540
  678.1 889.5 %copy-start.99 = (f32[64,64]{0,1:T(8,128)}, f32[64,64]{0,1:T(8,128)S(1)}, u32[]{:S(2)}) copy-start(f32[64,64]{0,1:T(8,128)S(1)} %fusion.261) | copy-start | bytes 49156
  678.4 781.6 %copy-start.159 = (f32[128]{0:T(128)}, f32[128]{0:T(128)S(1)}, u32[]{:S(2)}) copy-start(f32[128]{0:T(128)S(1)} %add_rsqrt_fusion.3) | copy-start | bytes 1540
  678.4 858.1 %copy-start.157 = (pred[2,64]{1,0:T(4,128)(4,1)}, pred[2,64]{1,0:T(4,128)(4,1)S(1)}, u32[]{:S(2)}) copy-start(pred[2,64]{1,0:T(4,128)(4,1)S(1)} %and_bitcast_fusion) | copy-start | bytes 388
  678.5 866.5 %copy-start.117 = (pred[2,64,64]{1,2,0:T(8,128)(4,1)}, pred[2,64,64]{1,2,0:T(8,128)(4,1)S(1)}, u32[]{:S(2)}) copy-start(pred[2,64,64]{1,2,0:T(8,128)(4,1)S(1)} %get-tuple-element.751) | copy-start | bytes 24580
  678.5 900.8 %copy-start.109 = (pred[2,64,64]{1,2,0:T(8,128)(4,1)}, pred[2,64,64]{1,2,0:T(8,128)(4,1)S(1)}, u32[]{:S(2)}) copy-start(pred[2,64,64]{1,2,0:T(8,128)(4,1)S(1)} %get-tuple-element.752) | copy-start | bytes 24580
  1458.5 22.0 copy-start.143
  1458.5 229.4 %copy-start.141 = (f32[2048]{0:T(1024)}, f32[2048]{0:T(1024)S(1)}, u32[]{:S(2)}) copy-start(f32[2048]{0:T(1024)S(1)} %get-tuple-element.649) | copy-start | bytes 24580
  1458.7 31.2 copy-start.184
  1458.7 32.6 copy-start.164
  1460.1 29.8 copy-start.83
  1492.3 87.0 %copy-start.86 = (f32[2,16,64]{2,1,0:T(8,128)}, f32[2,16,64]{2,1,0:T(8,128)S(1)}, u32[]{:S(2)}) copy-start(f32[2,16,64]{2,1,0:T(8,128)S(1)} %reduce_window_sum.40) | copy-start | bytes 24580
  1492.5 44.1 copy-start.152
  1492.6 44.0 copy-start.133
  1505.3 77.5 %copy-start.3 = (f32[16,8,16,128]{3,2,1,0:T(8,128)}, f32[16,8,16,128]{3,2,1,0:T(8,128)S(1)}, u32[]{:S(2)}) copy-start(f32[16,8,16,128]{3,2,1,0:T(8,128)S(1)} %copy.415) | copy-start | bytes 3145732
  1507.0 75.8 %copy-start.105 = (f32[2,64,16]{1,2,0:T(8,128)}, f32[2,64,16]{1,2,0:T(8,128)S(1)}, u32[]{:S(2)}) copy-start(f32[2,64,16]{1,2,0:T(8,128)S(1)} %copy.246) | copy-start | bytes 24580
  1507.0 65.4 %copy-start.111 = (f32[2,64,16]{1,2,0:T(8,128)}, f32[2,64,16]{1,2,0:T(8,128)S(1)}, u32[]{:S(2)}) copy-start(f32[2,64,16]{1,2,0:T(8,128)S(1)} %copy.507) | copy-start | bytes 24580
  1536.6 40.1 copy-start.129
  1536.6 46.1 %copy-start.131 = (f32[2,16,64]{2,1,0:T(8,128)}, f32[2,16,64]{2,1,0:T(8,128)S(1)}, u32[]{:S(2)}) copy-start(f32[2,16,64]{2,1,0:T(8,128)S(1)} %get-tuple-element.718) | copy-start | bytes 24580
  1536.7 46.1 %copy-start.137 = (f32[2,16,64]{2,1,0:T(8,128)}, f32[2,16,64]{2,1,0:T(8,128)S(1)}, u32[]{:S(2)}) copy-start(f32[2,16,64]{2,1,0:T(8,128)S(1)} %get-tuple-element.746) | copy-start | bytes 24580
  1539.0 43.8 copy-start.119
  1545.1 25.4 copy-start.44
  1549.0 15.9 copy-start.93
  1549.0 16.8 copy-start.50
  1550.6 21.8 copy-start.30
  1550.6 18.1 copy-start.52
  1632.6 55.3 %copy-start.67 = (f32[128,2048]{1,0:T(8,128)}, f32[128,2048]{1,0:T(8,128)S(1)}, u32[]{:S(2)}) copy-start(f32[128,2048]{1,0:T(8,128)S(1)} %get-tuple-element.761) | copy-start | bytes 3145732
  1632.6 55.3 %copy-start.162 = (f32[128]{0:T(128)}, f32[128]{0:T(128)S(1)}, u32[]{:S(2)}) copy-start(f32[128]{0:T(128)S(1)} %add_rsqrt_fusion.2) | copy-start | bytes 1540
  1632.8 19.1 copy-start.103
  1632.8 19.0 copy-start.88
  1707.5 48.9 %copy-start.130 = (f32[2,16,64]{2,1,0:T(8,128)S(1)}, f32[2,16,64]{2,1,0:T(8,128)}, u32[]{:S(2)}) copy-start(f32[2,16,64]{2,1,0:T(8,128)} %copy-done.129) | copy-start | bytes 24580
  1713.6 42.9 copy-start.4
  1713.6 42.9 copy-start.106
  1907.2 24.5 copy-start.81
  1907.2 24.5 copy-start.144
  1907.3 24.5 copy-start.160
  1939.4 37.1 copy-start.98
  1976.5 14.4 copy-start.102
  1990.8 34.0 copy-start.91
  1990.8 34.0 copy-start.92
  1990.8 34.0 copy-start.179
  (170 other events, 641.3 us)
Sparse Core Ops, SparseCore 0:
  9.5 652.7 all-gather.2
  663.9 792.0 all-gather.4
  2054.3 2333.0 reduce-scatter.1
where the time goes:
time: 4430 us; the launch traced here: 4420 us
  waiting for transfers between devices  3740 us (84%)
  matrix products  413 us (9%)
  local copies, waits for them, and re-layouts  133 us (3%)
  other arithmetic  108 us (2%)
    reduce_scatter x1, waiting for transfers between devices, on_device(): lax.psum_scatter(jnp.concatenate([contract_rows(take_cols(normed), d_mixe...  2310 us
    all_gather x1, waiting for transfers between devices, on_device(): full_weights = lax.all_gather(group_rows, 'grp', axis=0, tiled=True)  777 us
    all_gather x1, waiting for transfers between devices, on_device(): group_rows = lax.all_gather(weights, 'rep', axis=0, tiled=True)  654 us
    dot_general x5, matrix products, contract_rows(): lax.dot_general(left, right, (((0,), (0,)), ((), ())), preferred_element_...  106 us
  transfers between devices with their start and end apart: 3, of which 3 were waited for; matrix products, arithmetic and copies ran while one was open for 1% of the time, Pallas kernels for 0%

commit v1 on v0

v1 whole, which is shorter than its diff:
```python
import functools

import jax
import jax.numpy as jnp
from jax import lax
from jax.experimental import pallas as pl
from jax.experimental.pallas import tpu as pltpu
from jax.sharding import PartitionSpec as P

D = 2048
H = 16
DK = 128
DV = 256
FF = 5632
CONV = 4
EXTRA = 128
KD = 2048
VD = 4096
MIX_END = 2 * KD + 2 * VD
FFN_START = MIX_END + VD
DOWN_START = FFN_START + 2 * FF
EXTRA_START = DOWN_START + FF
COLS = EXTRA_START + EXTRA

EPS_NORM = 1e-06
EPS_GATED = 1e-05
EPS_ADAM = 1e-08
DECAY_WEIGHT = 0.1
HIGH = lax.Precision.HIGHEST
MESH = pl.DeviceIdType.MESH

RANKS = 8
HEADS = H // RANKS
QW = HEADS * DK
VW = HEADS * DV
MIXW = 2 * QW + 2 * VW + EXTRA
OW = VW
TILES = FF // 128
FULL_RANKS = TILES - (TILES // RANKS) * RANKS
FT = TILES // RANKS + 1
FW = FT * 128
ORDERS = ((4, 2, 1), (2, 1, 4), (1, 4, 2))
PLAIN = ((2, 4, 1), (2, 1, 4))
BF = jnp.bfloat16
F32 = jnp.float32


def rank_of(rep, grp):
    return (grp // 2) * 4 + rep % 4


class Place:
    def __init__(self, copies):
        self.rep = lax.axis_index("rep")
        self.grp = lax.axis_index("grp")
        self.copies = copies
        self.dp = self.rep // 4
        self.core = self.grp % 2
        self.rank = rank_of(self.rep, self.grp)
        self.bits = {4: self.rank // 4, 2: self.rank // 2 % 2, 1: self.rank % 2}

    def flip(self, mask):
        total = 0
        for weight, bit in self.bits.items():
            total = total + weight * ((1 - bit) if mask & weight else bit)
        return total

    def peer(self, mask):
        rank = self.flip(mask)
        return (self.dp * 4 + rank % 4, (rank // 4) * 2 + self.core)

    def sibling(self):
        return (self.rep, self.grp + 1 - 2 * self.core)

    def copy_at(self, shift):
        return (((self.dp + shift) % self.copies) * 4 + self.rep % 4, self.grp)


def meet(devices):
    barrier = pltpu.get_barrier_semaphore()
    for device in devices:
        pl.semaphore_signal(barrier, inc=1, device_id=device, device_id_type=MESH)
    pl.semaphore_wait(barrier, len(devices))


def remote(src, dst, send, recv, device):
    return pltpu.make_async_remote_copy(
        src_ref=src, dst_ref=dst, send_sem=send, recv_sem=recv, device_id=device, device_id_type=MESH
    )


def row_parts(tokens):
    if tokens == 128:
        return ((0, 48), (48, 48), (96, 32))
    third = tokens // 48 * 16
    return ((0, third), (third, third), (2 * third, tokens - 2 * third))


class Gather:
    def __init__(self, place, buf, parts, orders, send, recv):
        self.place, self.buf, self.parts, self.orders = place, buf, parts, orders
        self.send, self.recv = send, recv
        self.flights = {}

    def start(self, part, stage):
        order = self.orders[part]
        delta = order[stage]
        held = [0]
        for earlier in order[:stage]:
            held = held + [mask ^ earlier for mask in held]
        first, rows = self.parts[part]
        begin = 2**stage - 1
        here = []
        for at, mask in enumerate(held):
            block = self.buf.at[self.place.flip(mask), pl.ds(first, rows)]
            slot = begin + at
            copy = remote(
                block, block, self.send.at[part, slot], self.recv.at[part, slot], self.place.peer(delta)
            )
            copy.start()
            here.append(copy)
        self.flights[part, stage] = here

    def landed(self, part, stage):
        for copy in self.flights[part, stage]:
            copy.wait_recv()

    def finish(self):
        for here in self.flights.values():
            for copy in here:
                copy.wait_send()


class Scatter:
    def __init__(self, place, buf, land, parts, orders, send, recv):
        self.place, self.buf, self.land, self.parts, self.orders = place, buf, land, parts, orders
        self.send, self.recv = send, recv
        self.flights = {}
        self.sums = {}

    def held(self, part, stage, mask):
        first, rows = self.parts[part]
        if stage == 0:
            return self.buf.at[self.place.flip(mask), pl.ds(first, rows)]
        return self.land.at[self.sums[part, stage - 1][mask], pl.ds(first, rows)]

    def start(self, part, stage):
        order = self.orders[part]
        delta = order[stage]
        kept = [0]
        for later in order[stage + 1 :]:
            kept = kept + [mask ^ later for mask in kept]
        first, rows = self.parts[part]
        begin = (0, 4, 6)[stage]
        here = []
        for at, mask in enumerate(kept):
            slot = begin + at
            copy = remote(
                self.held(part, stage, mask ^ delta),
                self.land.at[slot, pl.ds(first, rows)],
                self.send.at[part, slot],
                self.recv.at[part, slot],
                self.place.peer(delta),
            )
            copy.start()
            here.append((copy, mask, slot))
        self.flights[part, stage] = here
        self.sums[part, stage] = {mask: slot for _, mask, slot in here}

    def add(self, part, stage):
        first, rows = self.parts[part]
        result = None
        for copy, mask, slot in self.flights[part, stage]:
            copy.wait_recv()
            total = self.held(part, stage, mask)[...].astype(F32) + self.land[
                slot, pl.ds(first, rows)
            ].astype(F32)
            if stage < 2:
                self.land[slot, pl.ds(first, rows)] = total.astype(BF)
            else:
                result = total
        return result

    def finish(self):
        for here in self.flights.values():
            for copy, _, _ in here:
                copy.wait_send()


def tile_start(rank):
    few = FT - 1
    return 128 * jnp.where(rank < FULL_RANKS, FT * rank, FULL_RANKS + few * rank)


def first_columns(rank):
    mixer = (
        (rank * QW, 0, QW),
        (KD + rank * QW, QW, QW),
        (2 * KD + rank * VW, 2 * QW, VW),
        (2 * KD + VD + rank * VW, 2 * QW + VW, VW),
        (EXTRA_START, 2 * QW + 2 * VW, EXTRA),
    )
    outward = ((MIX_END + rank * VW, 0, VW),)
    at = tile_start(rank)
    gates = ((FFN_START + at, 0, FW), (FFN_START + FF + at, FW, FW))
    down = ((DOWN_START + at, 0, FW),)
    return mixer, outward, gates, down


def columns(at, width):
    if not isinstance(at, int):
        at = pl.multiple_of(at, 128)
    return pl.ds(at, width)


def spread_kernel(copies, parts, w_ref, x_ref, s_ref, mix, outward, gates, down, xall, sall,
                  local, send, recv, seg_send, seg_recv, ag_send, ag_recv,
                  copy_send, copy_recv, core_send, core_recv):
    place = Place(copies)
    peers = [place.peer(mask) for mask in range(1, RANKS)]
    partners = [place.copy_at(shift) for shift in range(1, copies)]
    meet(peers + partners + [place.sibling()])
    me = place.rank
    targets = (mix.at[0, 0], outward, gates, down)
    own = []
    firsts = (0, 5, 6, 8)
    for group, pieces in enumerate(first_columns(me)):
        here = []
        for slot, (at, to, width) in enumerate(pieces):
            copy = pltpu.make_async_copy(
                w_ref.at[:, columns(at, width)], targets[group].at[me, :, pl.ds(to, width)],
                local.at[firsts[group] + slot],
            )
            copy.start()
            here.append(copy)
        own.append(here)
    own_x = pltpu.make_async_copy(x_ref, xall.at[me], local.at[9])
    own_x.start()
    own_s = pltpu.make_async_copy(s_ref, sall.at[me], local.at[10])
    own_s.start()

    def send_group(group):
        flights = []
        for mask in range(1, RANKS):
            there = place.flip(mask)
            for slot, (at, to, width) in enumerate(first_columns(there)[group]):
                copy = remote(
                    w_ref.at[:, columns(at, width)],
                    targets[group].at[me, :, pl.ds(to, width)],
                    send.at[firsts[group] + slot, mask - 1],
                    recv.at[group, mask - 1],
                    place.peer(mask),
                )
                copy.start()
                flights.append(copy)
        return flights

    def got(group, mask):
        block = targets[group].at[place.flip(mask)]
        remote(block, block, send.at[0, mask - 1], recv.at[group, mask - 1], place.peer(mask)).wait_recv()

    sent = send_group(0)
    onward = []

    def forward(mask):
        block = mix.at[0, 0, place.flip(mask)]
        for shift in range(1, copies):
            copy = remote(
                block, mix.at[0, copies - shift, place.flip(mask)],
                copy_send.at[shift - 1, mask], copy_recv.at[copies - shift - 1, mask],
                place.copy_at(shift),
            )
            copy.start()
            onward.append(copy)
        copy = remote(
            block, mix.at[1, 0, place.flip(mask)], core_send.at[0, mask], core_recv.at[0, mask],
            place.sibling(),
        )
        copy.start()
        onward.append(copy)

    for copy in own[0]:
        copy.wait()
    forward(0)
    own_s.wait()
    seg_flights = []
    for mask in range(1, RANKS):
        copy = remote(s_ref, sall.at[me], seg_send.at[mask - 1], seg_recv.at[mask - 1], place.peer(mask))
        copy.start()
        seg_flights.append(copy)
    for mask in range(1, RANKS):
        got(0, mask)
        forward(mask)
    own_x.wait()
    gather = Gather(place, xall, parts, PLAIN, ag_send, ag_recv)
    for part in range(len(parts)):
        gather.start(part, 0)
    for group in range(1, 4):
        sent = sent + send_group(group)
    for stage in range(3):
        for part in range(len(parts)):
            gather.landed(part, stage)
            if stage < 2:
                gather.start(part, stage + 1)
    for shift in range(1, copies):
        for mask in range(RANKS):
            block = mix.at[0, shift, place.flip(mask)]
            remote(
                block, block, copy_send.at[shift - 1, mask], copy_recv.at[shift - 1, mask], place.copy_at(shift)
            ).wait_recv()
            copy = remote(
                block, mix.at[1, shift, place.flip(mask)],
                core_send.at[shift, mask], core_recv.at[shift, mask], place.sibling(),
            )
            copy.start()
            onward.append(copy)
    for group in range(1, 4):
        for mask in range(1, RANKS):
            got(group, mask)
    for shift in range(copies):
        for mask in range(RANKS):
            block = mix.at[1, shift, place.flip(mask)]
            remote(
                block, block, core_send.at[shift, mask], core_recv.at[shift, mask], place.sibling()
            ).wait_recv()
    for copy in seg_flights:
        copy.wait()
    for here in own[1:]:
        for copy in here:
            copy.wait()
    for copy in sent + onward:
        copy.wait_send()
    gather.finish()


def any_spec():
    return pl.BlockSpec(memory_space=pl.ANY)


def vmem_spec():
    return pl.BlockSpec(memory_space=pltpu.VMEM)


def dma(*shape):
    return pltpu.SemaphoreType.DMA(shape)


def spread(copies, weights, x, seg):
    rows = weights.shape[0]
    tokens = x.shape[0]
    shape = jax.ShapeDtypeStruct
    return pl.pallas_call(
        functools.partial(spread_kernel, copies, ((0, tokens // 2), (tokens // 2, tokens // 2))),
        out_shape=(
            shape((2, copies, RANKS, rows, MIXW), BF),
            shape((RANKS, rows, OW), BF),
            shape((RANKS, rows, 2 * FW), BF),
            shape((RANKS, rows, FW), BF),
            shape((RANKS, tokens, D), BF),
            shape((RANKS,) + seg.shape, seg.dtype),
        ),
        in_specs=[any_spec()] * 3,
        out_specs=[any_spec()] * 6,
        scratch_shapes=[
            dma(11), dma(9, RANKS - 1), dma(4, RANKS - 1), dma(RANKS - 1), dma(RANKS - 1),
            dma(3, 7), dma(3, 7),
            dma(copies - 1, RANKS), dma(copies - 1, RANKS), dma(copies, RANKS), dma(copies, RANKS),
        ],
        compiler_params=pltpu.CompilerParams(collective_id=1, has_side_effects=True),
        name="spread",
    )(weights, x, seg)


def norm_scale(values, epsilon):
    return lax.rsqrt(jnp.mean(values * values, axis=-1, keepdims=True) + epsilon)


def branch_kernel(copies, parts, part_ref, x_ref, gain_ref, hidden_ref, nall, land,
                  send, recv, ag_send, ag_recv):
    place = Place(copies)
    meet([place.peer(mask) for mask in (4, 2, 1)])
    me = place.rank
    scatter = Scatter(place, part_ref, land, parts, ORDERS, send, recv)
    gather = Gather(place, nall, parts, ORDERS, ag_send, ag_recv)
    for part in range(3):
        scatter.start(part, 0)
    for stage in range(2):
        for part in range(3):
            scatter.add(part, stage)
            scatter.start(part, stage + 1)
    for part in range(3):
        first, rows = parts[part]
        hidden = x_ref[pl.ds(first, rows)].astype(F32) + scatter.add(part, 2)
        hidden_ref[pl.ds(first, rows)] = hidden
        unit = hidden * norm_scale(hidden, EPS_NORM)
        nall[me, pl.ds(first, rows)] = (unit * gain_ref[...]).astype(BF)
        gather.start(part, 0)
    for stage in range(3):
        for part in range(3):
            gather.landed(part, stage)
            if stage < 2:
                gather.start(part, stage + 1)
    scatter.finish()
    gather.finish()


def cube_scratch(tokens):
    return [pltpu.VMEM((7, tokens, D), BF), dma(3, 7), dma(3, 7)]


BIG = 56 * 2**20


def branch(copies, partial, x, gain):
    tokens = x.shape[0]
    shape = jax.ShapeDtypeStruct
    return pl.pallas_call(
        functools.partial(branch_kernel, copies, row_parts(tokens)),
        out_shape=(shape((tokens, D), F32), shape((RANKS, tokens, D), BF)),
        in_specs=[vmem_spec()] * 3,
        out_specs=[vmem_spec()] * 2,
        scratch_shapes=cube_scratch(tokens) + [dma(3, 7), dma(3, 7)],
        compiler_params=pltpu.CompilerParams(collective_id=2, has_side_effects=True, vmem_limit_bytes=BIG),
        name="branch",
    )(partial, x, gain)


def norm_back(grad, values, gain, epsilon):
    scale = norm_scale(values, epsilon)
    unit = values * scale
    scaled = grad * gain
    back = scale * (scaled - unit * jnp.mean(scaled * unit, axis=1, keepdims=True))
    return back, grad * unit


def hidden_back_kernel(copies, parts, part_ref, h_ref, dy_ref, gain_ref, dh_ref, gain_grad, dall, land,
                       send, recv, ag_send, ag_recv):
    place = Place(copies)
    meet([place.peer(mask) for mask in (4, 2, 1)])
    me = place.rank
    scatter = Scatter(place, part_ref, land, parts, ORDERS, send, recv)
    gather = Gather(place, dall, parts, ORDERS, ag_send, ag_recv)
    for part in range(3):
        scatter.start(part, 0)
    for stage in range(2):
        for part in range(3):
            scatter.add(part, stage)
            scatter.start(part, stage + 1)
    total = jnp.zeros((1, D), F32)
    for part in range(3):
        first, rows = parts[part]
        back, gain_part = norm_back(
            scatter.add(part, 2), h_ref[pl.ds(first, rows)], gain_ref[...], EPS_NORM
        )
        back = dy_ref[pl.ds(first, rows)].astype(F32) + back
        dh_ref[pl.ds(first, rows)] = back
        dall[me, pl.ds(first, rows)] = back.astype(BF)
        gather.start(part, 0)
        total = total + jnp.sum(gain_part, axis=0, keepdims=True)
    gain_grad[...] = total
    for stage in range(3):
        for part in range(3):
            gather.landed(part, stage)
            if stage < 2:
                gather.start(part, stage + 1)
    scatter.finish()
    gather.finish()


def hidden_back(copies, partial, hidden, dy, gain):
    tokens = dy.shape[0]
    shape = jax.ShapeDtypeStruct
    return pl.pallas_call(
        functools.partial(hidden_back_kernel, copies, row_parts(tokens)),
        out_shape=(shape((tokens, D), F32), shape((1, D), F32), shape((RANKS, tokens, D), BF)),
        in_specs=[vmem_spec()] * 4,
        out_specs=[vmem_spec()] * 3,
        scratch_shapes=cube_scratch(tokens) + [dma(3, 7), dma(3, 7)],
        compiler_params=pltpu.CompilerParams(collective_id=3, has_side_effects=True, vmem_limit_bytes=BIG),
        name="hidden_back",
    )(partial, hidden, dy, gain)


def ends_kernel(copies, parts, dn_ref, feed_ref, h_ref, dh_ref, x_ref, gain_ref, out_ref, in_grad, gain_grad,
                dn_land, dn_send, dn_recv, feed_land, feed_send, feed_recv):
    place = Place(copies)
    meet([place.peer(mask) for mask in (4, 2, 1)])
    back = Scatter(place, dn_ref, dn_land, parts, ORDERS, dn_send, dn_recv)
    feed = Scatter(place, feed_ref, feed_land, parts, ORDERS, feed_send, feed_recv)
    for part in range(3):
        back.start(part, 0)
    for part in range(3):
        feed.start(part, 0)
    for stage in range(2):
        for one in (back, feed):
            for part in range(3):
                one.add(part, stage)
                one.start(part, stage + 1)
    total = jnp.zeros((1, D), F32)
    for part in range(3):
        first, rows = parts[part]
        grad, gain_part = norm_back(
            back.add(part, 2), x_ref[pl.ds(first, rows)].astype(F32), gain_ref[...], EPS_NORM
        )
        in_grad[pl.ds(first, rows)] = (dh_ref[pl.ds(first, rows)] + grad).astype(BF)
        total = total + jnp.sum(gain_part, axis=0, keepdims=True)
    gain_grad[...] = total
    for part in range(3):
        first, rows = parts[part]
        out_ref[pl.ds(first, rows)] = (h_ref[pl.ds(first, rows)] + feed.add(part, 2)).astype(BF)
    back.finish()
    feed.finish()


def ends(copies, dn_part, feed_part, hidden, d_hidden, x, gain):
    tokens = x.shape[0]
    shape = jax.ShapeDtypeStruct
    return pl.pallas_call(
        functools.partial(ends_kernel, copies, row_parts(tokens)),
        out_shape=(shape((tokens, D), BF), shape((tokens, D), BF), shape((1, D), F32)),
        in_specs=[vmem_spec()] * 6,
        out_specs=[vmem_spec()] * 3,
        scratch_shapes=cube_scratch(tokens) + cube_scratch(tokens),
        compiler_params=pltpu.CompilerParams(collective_id=4, has_side_effects=True, vmem_limit_bytes=BIG),
        name="ends",
    )(dn_part, feed_part, hidden, d_hidden, x, gain)


def home_kernel(copies, groups, base, n_in, *refs):
    ins, out = refs[:n_in], refs[n_in]
    local, send, recv = refs[n_in + 1 :]
    place = Place(copies)
    meet([place.peer(mask) for mask in range(1, RANKS)])
    me = place.rank

    def pieces(rank):
        found = []
        for index, group in enumerate(groups):
            for at, to, width in first_columns(rank)[group]:
                if group == 0 and width == EXTRA and to == 2 * QW + 2 * VW:
                    continue
                if group >= 2:
                    found.append((index, to, at - base, width - 128, False))
                    found.append((index, to + width - 128, at - base + width - 128, 128, True))
                else:
                    found.append((index, to, at - base, width, False))
        return found

    def when(flag, rank, act):
        if flag:
            pl.when(rank < FULL_RANKS)(act)
        else:
            act()

    def run(method):
        for slot, (index, to, at, width, flag) in enumerate(pieces(me)):
            copy = pltpu.make_async_copy(
                ins[index].at[me, :, pl.ds(to, width)], out.at[:, columns(at, width)], local.at[slot]
            )
            when(flag, me, getattr(copy, method))
        for mask in range(1, RANKS):
            there = place.flip(mask)
            for slot, (index, to, at, width, flag) in enumerate(pieces(me)):
                copy = remote(
                    ins[index].at[there, :, pl.ds(to, width)], out.at[:, columns(at, width)],
                    send.at[mask - 1, slot], recv.at[mask - 1, slot], place.peer(mask),
                )
                when(flag, me, copy.start if method == "start" else copy.wait_send)
            if method == "wait":
                for slot, (index, to, at, width, flag) in enumerate(pieces(there)):
                    block = out.at[:, columns(at, width)]
                    copy = remote(
                        block, block, send.at[mask - 1, slot], recv.at[mask - 1, slot], place.peer(mask)
                    )
                    when(flag, there, copy.wait_recv)

    run("start")
    run("wait")


def home(copies, ident, groups, arrays):
    rows = arrays[0].shape[1]
    base = 0 if groups[0] == 0 else MIX_END
    width = MIX_END if groups[0] == 0 else EXTRA_START - MIX_END
    return pl.pallas_call(
        functools.partial(home_kernel, copies, groups, base, len(arrays)),
        out_shape=jax.ShapeDtypeStruct((rows, width), BF),
        in_specs=[any_spec()] * len(arrays),
        out_specs=any_spec(),
        scratch_shapes=[dma(7), dma(RANKS - 1, 7), dma(RANKS - 1, 7)],
        compiler_params=pltpu.CompilerParams(collective_id=ident, has_side_effects=True),
        name="home%d" % ident,
    )(*arrays)


def mul(left, right, axes, precision=HIGH):
    return lax.dot_general(left, right, (axes, ((), ())), precision=precision, preferred_element_type=F32)


NN = ((1,), (0,))
NT = ((1,), (1,))
TN = ((0,), (0,))


def unit_lower_inverse(lower, row, col):
    size = lower.shape[0]
    inverse = jnp.where(row == col, 1.0, jnp.where(row // 2 == col // 2, -lower, 0.0))
    block = 2
    while block < size:
        joined = (row // (2 * block) == col // (2 * block)) & (row // block != col // block)
        part = mul(jnp.where(joined, lower, 0.0), inverse, NN)
        inverse = inverse - mul(inverse, part, NN)
        block = block * 2
    return inverse


class Sequence:
    def __init__(self, seg_row):
        tokens = seg_row.shape[1]
        self.tokens = tokens
        shape = (tokens, tokens)
        self.row = lax.broadcasted_iota(jnp.int32, shape, 0)
        self.col = lax.broadcasted_iota(jnp.int32, shape, 1)
        ids = jnp.broadcast_to(seg_row.astype(F32), shape)
        turned = ids.T
        same = turned == ids
        self.inclusive = same & (self.row >= self.col)
        self.strict = same & (self.row > self.col)
        self.lower = (self.row >= self.col).astype(F32)
        column = turned[:, :1]
        at = self.row[:, :1]
        self.near = [None]
        for back in range(1, CONV):
            before = pltpu.roll(turned, back, 0)[:, :1]
            self.near.append(((before == column) & (at >= back)).astype(F32))

    def conv(self, taps, values):
        total = taps[CONV - 1 : CONV] * values
        for back in range(1, CONV):
            total = total + taps[CONV - 1 - back : CONV - back] * (
                self.near[back] * pltpu.roll(values, back, 0)
            )
        return total

    def conv_back(self, taps, values, grad):
        total = taps[CONV - 1 : CONV] * grad
        rows = [jnp.sum(values * grad, axis=0, keepdims=True)]
        for back in range(1, CONV):
            masked = self.near[back] * grad
            total = total + taps[CONV - 1 - back : CONV - back] * pltpu.roll(
                masked, self.tokens - back, 0
            )
            rows.append(jnp.sum(masked * pltpu.roll(values, back, 0), axis=0, keepdims=True))
        return total, jnp.concatenate(rows[::-1], axis=0)


def pick_lane(block, lane):
    at = lax.broadcasted_iota(jnp.int32, block.shape, 1)
    return jnp.sum(jnp.where(at == lane, block, 0.0), axis=1, keepdims=True)


def softplus(values):
    return jnp.maximum(values, 0.0) + jnp.log1p(jnp.exp(-jnp.abs(values)))


class Head:
    def __init__(self, seq, head, rank, scalars, p_ref, taps_ref):
        q_at, k_at = head * DK, QW + head * DK
        v_at, g_at = 2 * QW + head * DV, 2 * QW + VW + head * DV
        self.q_at, self.k_at, self.v_at, self.g_at = q_at, k_at, v_at, g_at
        self.raw = [p_ref[:, q_at : q_at + DK], p_ref[:, k_at : k_at + DK], p_ref[:, v_at : v_at + DV]]
        self.taps = [taps_ref[:, q_at : q_at + DK], taps_ref[:, k_at : k_at + DK], taps_ref[:, v_at : v_at + DV]]
        self.pre = [seq.conv(taps, raw) for taps, raw in zip(self.taps, self.raw)]
        self.sig = [jax.nn.sigmoid(pre) for pre in self.pre]
        conv_q, conv_k, self.v = [pre * sig for pre, sig in zip(self.pre, self.sig)]
        self.q_scale = lax.rsqrt(jnp.sum(conv_q * conv_q, axis=1, keepdims=True) + EPS_NORM)
        self.k_scale = lax.rsqrt(jnp.sum(conv_k * conv_k, axis=1, keepdims=True) + EPS_NORM)
        self.q_unit = conv_q * self.q_scale
        self.q = self.q_unit * DK**-0.5
        self.k = conv_k * self.k_scale
        pair = p_ref[:, 2 * QW + 2 * VW :]
        self.lane_a = rank * HEADS + head
        self.lane_b = H + rank * HEADS + head
        self.a = pick_lane(pair, self.lane_a) + scalars[HEADS + head]
        self.rate = scalars[head]
        self.beta = jax.nn.sigmoid(pick_lane(pair, self.lane_b))
        self.decay = -self.rate * softplus(self.a)
        spread_out = jnp.where(seq.row > seq.col, jnp.broadcast_to(self.decay, seq.row.shape), 0.0)
        gap = mul(seq.lower, spread_out, NN)
        self.pairs = jnp.where(seq.inclusive, jnp.exp(jnp.where(seq.inclusive, gap, 0.0)), 0.0)
        self.kk = mul(self.k, self.k, NT)
        self.qk = mul(self.q, self.k, NT)
        self.strict_pairs = jnp.where(seq.strict, self.pairs, 0.0)
        self.lower = self.beta * self.strict_pairs * self.kk
        self.attend = self.pairs * self.qk
        self.gate = p_ref[:, g_at : g_at + DV]


def mixer_kernel(rank_ref, scalars, seg_ref, p_ref, taps_ref, gain_ref, z_ref, inv_ref, upd_ref):
    seq = Sequence(seg_ref[0, :1])
    rank = rank_ref[0]
    for head in range(HEADS):
        one = Head(seq, head, rank, scalars, p_ref, taps_ref)
        inverse = unit_lower_inverse(one.lower, seq.row, seq.col)
        update = mul(inverse, one.beta * one.v, NN)
        out = mul(one.attend, update, NN)
        normed = out * norm_scale(out, EPS_GATED) * gain_ref[...]
        z_ref[:, head * DV : (head + 1) * DV] = (normed * (one.gate * jax.nn.sigmoid(one.gate))).astype(BF)
        inv_ref[0, head] = inverse
        upd_ref[0, head] = update


def mixer_back_kernel(rank_ref, scalars, seg_ref, p_ref, taps_ref, gain_ref, inv_ref, upd_ref, dz_ref,
                      dp_ref, dtaps_ref, dgain_ref, dscal_ref):
    @pl.when(pl.program_id(0) == 0)
    def _():
        dtaps_ref[...] = jnp.zeros_like(dtaps_ref)
        dgain_ref[...] = jnp.zeros_like(dgain_ref)
        dscal_ref[...] = jnp.zeros_like(dscal_ref)

    seq = Sequence(seg_ref[0, :1])
    rank = rank_ref[0]
    pair_grad = jnp.zeros((seq.tokens, EXTRA), F32)
    lane = lax.broadcasted_iota(jnp.int32, (seq.tokens, EXTRA), 1)
    scal_row = lax.broadcasted_iota(jnp.int32, (8, 128), 0)
    scal_col = lax.broadcasted_iota(jnp.int32, (8, 128), 1)
    scal = jnp.zeros((8, 128), F32)
    for head in range(HEADS):
        one = Head(seq, head, rank, scalars, p_ref, taps_ref)
        inverse = inv_ref[0, head]
        update = upd_ref[0, head]
        out = mul(one.attend, update, NN)
        dz = dz_ref[:, head * DV : (head + 1) * DV]
        scale = norm_scale(out, EPS_GATED)
        normed = out * scale
        sig = jax.nn.sigmoid(one.gate)
        gate = one.gate * sig
        d_gate = dz * normed * gain_ref[...] * (sig * (1 + one.gate * (1 - sig)))
        dp_ref[:, one.g_at : one.g_at + DV] = d_gate.astype(BF)
        dgain_ref[...] += jnp.sum(dz * normed * gate, axis=0, keepdims=True)
        d_normed = dz * gain_ref[...] * gate
        d_out = scale * (d_normed - normed * jnp.mean(d_normed * normed, axis=1, keepdims=True))
        d_attend = jnp.where(seq.inclusive, mul(d_out, update, NT), 0.0)
        d_update = mul(one.attend, d_out, TN)
        d_scaled = mul(inverse, d_update, TN)
        d_lower = jnp.where(seq.strict, -mul(d_scaled, update, NT), 0.0)
        d_v = one.beta * d_scaled
        d_beta = jnp.sum(d_scaled * one.v, axis=1, keepdims=True) + jnp.sum(
            d_lower * one.strict_pairs * one.kk, axis=1, keepdims=True
        )
        d_gap = d_attend * one.attend + d_lower * one.lower
        d_qk = d_attend * one.pairs
        d_kk = d_lower * (one.beta * one.strict_pairs)
        d_q = mul(d_qk, one.k, NN)
        d_k = mul(d_qk, one.q, TN) + mul(d_kk, one.k, NN) + mul(d_kk, one.k, TN)
        reach = mul(seq.lower, d_gap, TN)
        d_decay = jnp.sum(jnp.where(seq.row > seq.col, reach, 0.0), axis=1, keepdims=True)
        d_a = d_decay * (-one.rate) * jax.nn.sigmoid(one.a)
        d_b = d_beta * one.beta * (1 - one.beta)
        pair_grad = pair_grad + jnp.where(lane == one.lane_a, d_a, 0.0) + jnp.where(lane == one.lane_b, d_b, 0.0)
        sum_rate = jnp.sum(d_decay * one.decay, axis=0, keepdims=True)
        sum_a = jnp.sum(d_a, axis=0, keepdims=True)
        scal = scal + jnp.where((scal_row == 0) & (scal_col == head), sum_rate, 0.0)
        scal = scal + jnp.where((scal_row == 0) & (scal_col == HEADS + head), sum_a, 0.0)
        dq_unit = d_q * DK**-0.5
        dc_q = one.q_scale * (dq_unit - one.q_unit * jnp.sum(dq_unit * one.q_unit, axis=1, keepdims=True))
        dc_k = one.k_scale * (d_k - one.k * jnp.sum(d_k * one.k, axis=1, keepdims=True))
        for grad, pre, sig, raw, taps, at, width in (
            (dc_q, one.pre[0], one.sig[0], one.raw[0], one.taps[0], one.q_at, DK),
            (dc_k, one.pre[1], one.sig[1], one.raw[1], one.taps[1], one.k_at, DK),
            (d_v, one.pre[2], one.sig[2], one.raw[2], one.taps[2], one.v_at, DV),
        ):
            d_pre = grad * (sig * (1 + pre * (1 - sig)))
            d_raw, d_taps = seq.conv_back(taps, raw, d_pre)
            dp_ref[:, at : at + width] = d_raw.astype(BF)
            dtaps_ref[:, at : at + width] += d_taps
    dp_ref[:, 2 * QW + 2 * VW :] = pair_grad.astype(BF)
    dscal_ref[...] += scal


def smem_spec():
    return pl.BlockSpec(memory_space=pltpu.SMEM)


def by_sequence(*shape):
    rest = (0,) * (len(shape) - 1)
    return pl.BlockSpec(shape, lambda at: (at,) + rest)


def whole_block(*shape):
    return pl.BlockSpec(shape, lambda at: (0,) * len(shape))


CHANNELS = 2 * QW + VW


def mixer(rank, scalars, seg, p, taps, gain, tokens):
    count = p.shape[0] // tokens
    shape = jax.ShapeDtypeStruct
    return pl.pallas_call(
        mixer_kernel,
        grid=(count,),
        out_shape=(
            shape((p.shape[0], VW), BF),
            shape((count, HEADS, tokens, tokens), F32),
            shape((count, HEADS, tokens, DV), F32),
        ),
        in_specs=[
            smem_spec(), smem_spec(), by_sequence(1, 8, tokens), by_sequence(tokens, MIXW),
            whole_block(CONV, CHANNELS), whole_block(1, DV),
        ],
        out_specs=[
            by_sequence(tokens, VW), by_sequence(1, HEADS, tokens, tokens), by_sequence(1, HEADS, tokens, DV),
        ],
        compiler_params=pltpu.CompilerParams(vmem_limit_bytes=40 * 2**20),
        name="mixer",
    )(rank, scalars, seg, p, taps, gain)


def mixer_back(rank, scalars, seg, p, taps, gain, inverse, update, dz, tokens):
    count = p.shape[0] // tokens
    shape = jax.ShapeDtypeStruct
    return pl.pallas_call(
        mixer_back_kernel,
        grid=(count,),
        out_shape=(
            shape((p.shape[0], MIXW), BF),
            shape((CONV, CHANNELS), F32),
            shape((1, DV), F32),
            shape((8, 128), F32),
        ),
        in_specs=[
            smem_spec(), smem_spec(), by_sequence(1, 8, tokens), by_sequence(tokens, MIXW),
            whole_block(CONV, CHANNELS), whole_block(1, DV),
            by_sequence(1, HEADS, tokens, tokens), by_sequence(1, HEADS, tokens, DV), by_sequence(tokens, VW),
        ],
        out_specs=[
            by_sequence(tokens, MIXW), whole_block(CONV, CHANNELS), whole_block(1, DV), whole_block(8, 128),
        ],
        compiler_params=pltpu.CompilerParams(vmem_limit_bytes=40 * 2**20),
        name="mixer_back",
    )(rank, scalars, seg, p, taps, gain, inverse, update, dz)


def turn(blocks, shift, axis):
    size = blocks.shape[axis]
    twice = jnp.concatenate([blocks, blocks], axis=axis)
    return lax.dynamic_slice_in_dim(twice, shift % size, size, axis)


class Order:
    def __init__(self, copies, core, dp):
        self.copies, self.core, self.dp = copies, core, dp

    def relative(self, values, axis):
        lead, tail = values.shape[:axis], values.shape[axis + 1 :]
        whole = values.reshape(lead + (2, 2, self.copies, D // (4 * self.copies)) + tail)
        whole = turn(turn(whole, self.core, axis + 1), self.dp, axis + 2)
        whole = jnp.moveaxis(whole, axis, axis + 2)
        return whole.reshape(values.shape)

    def plain(self, values, axis):
        lead, tail = values.shape[:axis], values.shape[axis + 1 :]
        whole = values.reshape(lead + (2, self.copies, 2, D // (4 * self.copies)) + tail)
        whole = jnp.moveaxis(whole, axis + 2, axis)
        whole = turn(turn(whole, 2 - self.core, axis + 1), self.copies - self.dp, axis + 2)
        return whole.reshape(values.shape)


def dot(left, right, axes):
    return lax.dot_general(left, right, (axes, ((), ())), preferred_element_type=F32)


def on_device(inputs, cotangent, segment_ids, weights, master, moment_one, moment_two,
              step, learn_rate, beta_one, beta_two):
    tokens = inputs.shape[0]
    rows = weights.shape[0]
    replicas = lax.axis_size("rep")
    copies = replicas // 4
    members = replicas * 4
    rep = lax.axis_index("rep")
    grp = lax.axis_index("grp")
    core = grp % 2
    dp = rep // 4
    rank = rank_of(rep, grp)
    order = Order(copies, core, dp)
    axes = ("rep", "grp")
    group_tokens = RANKS * tokens
    block_rows = RANKS * rows

    def pairs_to(move):
        return [(at, move(at // 4, at % 4)) for at in range(members)]

    core_pairs = pairs_to(lambda r, g: r * 4 + (g ^ 1))
    copy_pairs = [
        pairs_to(lambda r, g, shift=shift: ((r + 4 * shift) % replicas) * 4 + g) for shift in range(1, copies)
    ]

    x = order.relative(inputs, 1)
    dy = order.relative(cotangent, 1)
    seg = jnp.broadcast_to(segment_ids[None, :], (8, tokens))
    mix_blocks, out_block, gate_block, down_block, x_all, seg_all = spread(copies, weights, x, seg)
    x_all = x_all.reshape(group_tokens, D)
    w_mix = mix_blocks.reshape(D, MIXW)

    def collect(block):
        block = block.reshape(block_rows, block.shape[2])
        mine = [block]
        for shift in range(1, copies):
            mine.append(lax.ppermute(block, axes, copy_pairs[copies - shift - 1]))
        theirs = [lax.ppermute(one, axes, core_pairs) for one in mine]
        return jnp.concatenate(mine + theirs, axis=0)

    w_out = collect(out_block)
    w_gates = collect(gate_block)
    w_down = collect(down_block)

    pieces = [dy]
    for mask in range(1, RANKS):
        def to_rank(r, g, mask=mask):
            there = ((g // 2) * 4 + r % 4) ^ mask
            return ((r // 4) * 4 + there % 4) * 4 + (there // 4) * 2 + g % 2
        pieces.append(lax.ppermute(dy, axes, pairs_to(to_rank)))
    dy_all = jnp.zeros((RANKS, tokens, D), BF)
    for mask in range(RANKS):
        there = ((rank // 4) ^ (mask // 4)) * 4 + ((rank // 2 % 2) ^ (mask // 2 % 2)) * 2 + ((rank % 2) ^ (mask % 2))
        dy_all = lax.dynamic_update_slice(dy_all, pieces[mask][None], (there, 0, 0))
    dy_all = dy_all.reshape(group_tokens, D)

    extra_rel = w_mix[:, MIXW - EXTRA :]
    gain_one = extra_rel[:, 2 * H].astype(F32)[None]
    gain_two = extra_rel[:, 2 * H + 1].astype(F32)[None]
    extra = order.plain(extra_rel, 0).astype(F32)
    conv_cols = CONV * (2 * KD + VD) // D
    kernel = extra[:, 2 * H + 2 : 2 * H + 2 + conv_cols].reshape(CONV, 2 * KD + VD)
    taps = jnp.concatenate(
        [
            lax.dynamic_slice_in_dim(kernel, rank * QW, QW, 1),
            lax.dynamic_slice_in_dim(kernel, KD + rank * QW, QW, 1),
            lax.dynamic_slice_in_dim(kernel, 2 * KD + rank * VW, VW, 1),
        ],
        axis=1,
    )
    column = extra[:, 2 * H + 2 + conv_cols]
    scalars = jnp.concatenate(
        [
            jnp.exp(lax.dynamic_slice_in_dim(column, rank * HEADS, HEADS, 0)),
            lax.dynamic_slice_in_dim(column, H + rank * HEADS, HEADS, 0),
        ]
    )
    out_gain = column[2 * H : 2 * H + DV][None]
    rank_arg = jnp.reshape(rank, (1,)).astype(jnp.int32)

    tokens_all = x_all.astype(F32)
    normed = (tokens_all * norm_scale(tokens_all, EPS_NORM) * gain_one).astype(BF)
    p = dot(normed, w_mix, NN)
    gated, inverse, update = mixer(rank_arg, scalars, seg_all, p, taps, out_gain, tokens)
    partial = dot(gated, w_out, NT).astype(BF)
    hidden, normed_two = branch(copies, partial.reshape(RANKS, tokens, D), x, gain_two)
    normed_two = normed_two.reshape(group_tokens, D)

    gate_up = dot(normed_two, w_gates, NN)
    gate_part, up_part = gate_up[:, :FW], gate_up[:, FW:]
    tile_count = jnp.where(rank < FULL_RANKS, FT, FT - 1)
    real = (jnp.arange(FW) < tile_count * 128)[None]
    sigmoid_gate = jax.nn.sigmoid(gate_part)
    activated = jnp.where(real, gate_part * sigmoid_gate * up_part, 0.0).astype(BF)
    feed = dot(activated, w_down, NT).astype(BF)
    d_act = dot(dy_all, w_down, NN)
    d_gate = d_act * up_part * sigmoid_gate * (1 + gate_part * (1 - sigmoid_gate))
    d_up = d_act * gate_part * sigmoid_gate
    real_two = jnp.concatenate([real, real], axis=1)
    d_gate_up = jnp.where(real_two, jnp.concatenate([d_gate, d_up], axis=1), 0.0).astype(BF)
    d_normed_two = dot(d_gate_up, w_gates, NT).astype(BF)
    d_hidden, gain_two_grad, d_hidden_all = hidden_back(
        copies, d_normed_two.reshape(RANKS, tokens, D), hidden, dy, gain_two
    )
    d_hidden_all = d_hidden_all.reshape(group_tokens, D)
    d_gated = dot(d_hidden_all, w_out, NN)
    d_mix, d_taps, d_out_gain, d_scalars = mixer_back(
        rank_arg, scalars, seg_all, p, taps, out_gain, inverse, update, d_gated, tokens
    )
    d_normed = dot(d_mix, w_mix, NT).astype(BF)
    out_rel, in_grad_rel, gain_one_grad = ends(
        copies, d_normed.reshape(RANKS, tokens, D), feed.reshape(RANKS, tokens, D), hidden, d_hidden, x, gain_one
    )
    output = order.plain(out_rel, 1)
    input_grad = order.plain(in_grad_rel, 1)

    def reduce_rows(left, right):
        half = copies * block_rows
        theirs = dot(left[:, half:], right, TN).astype(BF)
        got = lax.ppermute(theirs, axes, core_pairs)
        away = [
            (dot(left[:, at * block_rows : (at + 1) * block_rows], right, TN)
             + got[at * block_rows : (at + 1) * block_rows].astype(F32)).astype(BF)
            for at in range(1, copies)
        ]
        total = dot(left[:, :block_rows], right, TN) + got[:block_rows].astype(F32)
        for shift in range(1, copies):
            total = total + lax.ppermute(away[shift - 1], axes, copy_pairs[shift - 1]).astype(F32)
        return total.astype(BF).reshape(RANKS, rows, right.shape[1])

    down_rows = reduce_rows(dy_all, activated)
    gate_rows = reduce_rows(normed_two, d_gate_up)
    out_rows = reduce_rows(d_hidden_all, gated)
    mix_rows = reduce_rows(normed, d_mix)
    grads_rest = home(copies, 5, (1, 2, 3), (out_rows, gate_rows, down_rows))
    grads_mix = home(copies, 6, (0,), (mix_rows,))

    pair_grad = dot(normed, d_mix[:, MIXW - EXTRA :], TN)
    lanes = jnp.arange(EXTRA)[None]
    rel_grad = (
        pair_grad
        + jnp.where(lanes == 2 * H, gain_one_grad.reshape(D, 1), 0.0)
        + jnp.where(lanes == 2 * H + 1, gain_two_grad.reshape(D, 1), 0.0)
    )
    tap_grad = jnp.zeros((CONV, 2 * KD + VD), F32)
    tap_grad = lax.dynamic_update_slice(tap_grad, d_taps[:, :QW], (0, rank * QW))
    tap_grad = lax.dynamic_update_slice(tap_grad, d_taps[:, QW : 2 * QW], (0, KD + rank * QW))
    tap_grad = lax.dynamic_update_slice(tap_grad, d_taps[:, 2 * QW :], (0, 2 * KD + rank * VW))
    small = jnp.zeros((D,), F32)
    small = lax.dynamic_update_slice(small, d_scalars[0, :HEADS], (rank * HEADS,))
    small = lax.dynamic_update_slice(small, d_scalars[0, HEADS : 2 * HEADS], (H + rank * HEADS,))
    small = lax.dynamic_update_slice(small, d_out_gain[0], (2 * H,))
    core_grad = jnp.concatenate(
        [
            jnp.zeros((D, 2 * H + 2), F32),
            tap_grad.reshape(D, conv_cols),
            small[:, None],
            jnp.zeros((D, EXTRA - 2 * H - 3 - conv_cols), F32),
        ],
        axis=1,
    )
    extra_grad = order.plain(rel_grad, 0) + core_grad
    extra_grad = jnp.swapaxes(extra_grad.reshape(4, replicas, rows, EXTRA), 0, 1).reshape(D, EXTRA)
    extra_rows = lax.psum_scatter(extra_grad, axes, scatter_dimension=0, tiled=True)

    grads = jnp.concatenate([grads_mix.astype(F32), grads_rest.astype(F32), extra_rows], axis=1)
    gain_grads = extra_rows[:, 2 * H : 2 * H + 2]
    step_size = learn_rate[0]
    first_beta = beta_one[0]
    second_beta = beta_two[0]
    step_float = step[0].astype(F32)
    moment_one_new = first_beta * moment_one + (1 - first_beta) * grads
    moment_two_new = second_beta * moment_two + (1 - second_beta) * grads * grads
    first_hat = moment_one_new / (1 - first_beta**step_float)
    second_hat = moment_two_new / (1 - second_beta**step_float)
    master_new = master - step_size * (first_hat / (jnp.sqrt(second_hat) + EPS_ADAM) + DECAY_WEIGHT * master)
    return (output, input_grad, grads, moment_one_new, moment_two_new, master_new,
            master_new.astype(BF), gain_grads)


def solution(mesh):
    by_token = P(("rep", "grp"), None)
    by_row = P(("grp", "rep"), None)
    return jax.shard_map(
        on_device,
        mesh=mesh,
        in_specs=(by_token, by_token, P(("rep", "grp")), by_row, by_row, by_row, by_row, P(), P(), P(), P()),
        out_specs=(by_token, by_token) + (by_row,) * 6,
        check_vma=False,
    )
```

time: 4430 us -> 1100 us (0.25)
  waiting for transfers between devices: 3740 us -> 244 us
  Pallas kernels: 0 us -> 558 us
  matrix products: 413 us -> 118 us
  local copies, waits for them, and re-layouts: 133 us -> 47.1 us
    reduce_scatter x1, waiting for transfers between devices: 2310 us -> 48.3 us  [on_device(): lax.psum_scatter(extra_grad, axes, scatter_dimension=0, tiled=True)]
    all_gather x2 -> x0, waiting for transfers between devices: 1430 us -> none  [the longest x1 777 us: on_device(): full_weights = lax.all_gather(group_rows, 'grp', axis=0, tiled=True)]
    pallas_call x0 -> x8, Pallas kernels: none -> 558 us  [the longest x1 155 us: spread(): pl.pallas_call(functools.partial(spread_kernel, copies, ((0, tokens // 2)...]
    dot_general x81 -> x21, matrix products: 413 us -> 118 us  [dot(): lax.dot_general(left, right, (axes, ((), ())), preferred_element_type=F32)]
    ppermute x0 -> x24, waiting for transfers between devices: none -> 196 us  [the longest x3 90 us: collect(): mine.append(lax.ppermute(block, axes, copy_pairs[copies - shift - 1]))]
  transfers between devices with their start and end apart: 3 -> 25, of which waited for: 3 -> 7; matrix products, arithmetic and copies ran while one was open for 1% -> 14% of each run, Pallas kernels for 0% -> 38%
where the time goes in v1:
time: 1100 us; the launch traced here: 1090 us
  Pallas kernels  558 us (51%)
  waiting for transfers between devices  244 us (22%)
  matrix products  118 us (11%)
  other arithmetic  74.7 us (7%)
  local copies, waits for them, and re-layouts  47.1 us (4%)
  starting transfers between devices  30 us (3%)
  between operations  18.1 us (2%)
    pallas_call x1, Pallas kernels, spread(): pl.pallas_call(functools.partial(spread_kernel, copies, ((0, tokens // 2)...  155 us
    dot_general x21, matrix products, dot(): lax.dot_general(left, right, (axes, ((), ())), preferred_element_type=F32)  118 us
    ppermute x3, waiting for transfers between devices, collect(): mine.append(lax.ppermute(block, axes, copy_pairs[copies - shift - 1]))  90 us
    ppermute x4, waiting for transfers between devices, reduce_rows(): lax.ppermute(away[shift - 1], axes, copy_pairs[shift - 1]).astype(F32)  87.2 us
    pallas_call x2, Pallas kernels, home(): pl.pallas_call(functools.partial(home_kernel, copies, groups, base, len(a...  87.1 us
    pallas_call x1, Pallas kernels, branch(): pl.pallas_call(functools.partial(branch_kernel, copies, row_parts(tokens)...  72.7 us
    pallas_call x1, Pallas kernels, hidden_back(): pl.pallas_call(functools.partial(hidden_back_kernel, copies, row_parts(to...  71.1 us
    pallas_call x1, Pallas kernels, ends(): pl.pallas_call(functools.partial(ends_kernel, copies, row_parts(tokens)),...  65.7 us
  transfers between devices with their start and end apart: 25, of which 7 were waited for; matrix products, arithmetic and copies ran while one was open for 14% of the time, Pallas kernels for 38%

profile of v1, /device:TPU:0, one launch (start us, length us, event | category | flops | bytes accessed | tf_op | source)
XLA Modules:
  0.0 1089.9 jit_solution(1803590685755639483)
XLA Ops:
  13.1 4.9 collective-permute-start.6
  27.7 154.5 %spread.1 = (bf16[2,2,8,64,1664]{4,3,2,1,0:T(8,128)(2,1)}, bf16[8,64,512]{2,1,0:T(8,128)(2,1)}, bf16[8,64,1536]{2,1,0:T(8,128)(2,1)}, bf16[8,64,768]{2,1,0:T(8,1...) custom-call(bf16[64,33408]{1,0:T(8,128)(2,1)} %w_ref.1, bf16[128,2048]{1,0:T(8,128)(2,1)} %reshape.212.x_ref, ...), custom_call_target="tpu_custom_call" | custom-call | tf_op jit(solution)/shard_map/spread/pallas_call | solution.py:352
  189.7 3.1 multiply_reduce_fusion
  194.3 5.4 fusion.2
  201.5 9.7 fusion.69.p_ref
  218.1 2.9 copy-done
  221.1 62.2 %mixer.1 = (bf16[1024,512]{1,0:T(8,128)(2,1)S(1)}, f32[8,2,128,128]{3,2,1,0:T(8,128)S(1)}, f32[8,2,128,256]{3,2,1,0:T(8,128)S(1)}) custom-call(s32[1]{0:T(128)} %bitcast.rank_ref, f32[4]{0:T(128)S(1)} %pad_maximum_fusion.11.scalars, s32[8,8,128]{2,1,0:T(8,128)S(1)} %copy-done.1, f32[1024,1664]{1,0:T(8,128)S(1)} %copy-done, ...), custom_call_target="tpu_custom_call" | custom-call | tf_op jit(solution)/shard_map/mixer/pallas_call | solution.py:800
  283.3 9.0 collective-permute-start.13
  297.2 3.0 collective-permute-start.4
  302.0 7.1 collective-permute-done.3
  310.2 11.5 %collective-permute-done.4 = bf16[128,2048]{1,0:T(8,128)(2,1)S(1)} collective-permute-done((bf16[128,2048]{1,0:T(8,128)(2,1)}, bf16[128,2048]{1,0:T(8,128)(2,1)S(1)}, u32[]{:S(2)}, u32[]{:S(2)}) %collective-permute-start.4) | collective-permute-done | bytes 524320 | tf_op jit(solution)/shard_map/ppermute | solution.py:923
  321.8 50.7 %collective-permute-done.13 = bf16[512,1536]{1,0:T(8,128)(2,1)S(1)} collective-permute-done((bf16[512,1536]{1,0:T(8,128)(2,1)S(1)}, bf16[512,1536]{1,0:T(8,128)(2,1)S(1)}, u32[]{:S(2)}, u32[]{:S(2)}) %collective-permute-start.13) | collective-permute-done | bytes 1572896 | tf_op jit(solution)/shard_map/ppermute | solution.py:910
  373.9 26.7 %collective-permute-done.10 = bf16[512,512]{1,0:T(8,128)(2,1)S(1)} collective-permute-done((bf16[512,512]{1,0:T(8,128)(2,1)S(1)}, bf16[512,512]{1,0:T(8,128)(2,1)S(1)}, u32[]{:S(2)}, u32[]{:S(2)}) %collective-permute-start.10) | collective-permute-done | bytes 524320 | tf_op jit(solution)/shard_map/ppermute | solution.py:910
  404.9 12.5 %collective-permute-done.7 = bf16[512,768]{1,0:T(8,128)(2,1)} collective-permute-done((bf16[512,768]{1,0:T(8,128)(2,1)}, bf16[512,768]{1,0:T(8,128)(2,1)}, u32[]{:S(2)}, u32[]{:S(2)}) %collective-permute-start.7) | collective-permute-done | bytes 786464 | tf_op jit(solution)/shard_map/ppermute | solution.py:910
  417.4 4.4 convolution_convert_fusion.3
  421.8 72.7 %branch.1 = (f32[128,2048]{1,0:T(8,128)}, bf16[8,128,2048]{2,1,0:T(8,128)(2,1)}) custom-call(bf16[8,128,2048]{2,1,0:T(8,128)(2,1)} %bitcast.114, bf16[128,2048]{1,0:T(8,128)(2,1)} %reshape.212.x_ref, f32[1,2048]{1,0:T(1,128)} %bitcast_convert_fusion.gain_ref), custom_call_target="tpu_custom_call" | custom-call | tf_op jit(solution)/shard_map/branch/pallas_call | solution.py:417
  494.6 10.2 fusion.17
  507.0 7.4 add_multiply_fusion
  516.6 5.0 convolution_convert_fusion.4
  521.7 10.3 convolution_convert_fusion.1
  532.0 71.1 %hidden_back.1 = (f32[128,2048]{1,0:T(8,128)}, f32[1,2048]{1,0:T(1,128)}, bf16[8,128,2048]{2,1,0:T(8,128)(2,1)}) custom-call(bf16[8,128,2048]{2,1,0:T(8,128)(2,1)} %bitcast.118, f32[128,2048]{1,0:T(8,128)} %get-tuple-element.39.h_ref, bf16[128,2048]{1,0:T(8,128)(2,1)} %reshape.217.dy_ref, f32[1,2048]{1,0:T(1,128)} %bitcast_convert_fusion.gain_ref), custom_call_target="tpu_custom_call" | custom-call | tf_op jit(solution)/shard_map/hidden_back/pallas_call | solution.py:473
  603.2 4.0 fusion.14
  609.5 44.5 %mixer_back.1 = (bf16[1024,1664]{1,0:T(8,128)(2,1)S(1)}, f32[4,1024]{1,0:T(4,128)S(1)}, f32[1,256]{1,0:T(1,128)S(1)}, f32[8,128]{1,0:T(8,128)S(1)}) custom-call(s32[1]{0:T(128)} %bitcast.rank_ref, f32[4]{0:T(128)S(1)} %pad_maximum_fusion.11.scalars, s32[8,8,128]{2,1,0:T(8,128)S(1)} %copy-done.1, f32[1024,1664]{1,0:T(8,128)} %fusion.69.p_ref, ...), custom_call_target="tpu_custom_call" | custom-call | tf_op jit(solution)/shard_map/mixer_back/pallas_call | solution.py:823
  654.1 9.3 convolution_convert_fusion
  663.5 4.8 fusion.11
  668.3 5.7 convolution_convert_fusion.2
  674.5 7.3 convolution_convert_fusion.5
  681.9 65.7 %ends.1 = (bf16[128,2048]{1,0:T(8,128)(2,1)}, bf16[128,2048]{1,0:T(8,128)(2,1)}, f32[1,2048]{1,0:T(1,128)}) custom-call(bf16[8,128,2048]{2,1,0:T(8,128)(2,1)} %bitcast.116, bf16[8,128,2048]{2,1,0:T(8,128)(2,1)} %bitcast.117, f32[128,2048]{1,0:T(8,128)} %get-tuple-element.39.h_ref, f32[128,2048]{1,0:T(8,128)} %get-tuple-element.42.dh_ref, ...), custom_call_target="tpu_custom_call" | custom-call | tf_op jit(solution)/shard_map/ends/pallas_call | solution.py:518
  747.6 4.9 fusion.4
  767.0 3.0 fusion.31
  775.3 5.9 fusion.27
  781.2 3.9 fusion.37
  785.1 3.1 add_convert_fusion.7
  788.5 3.4 add_convert_fusion.5
  794.5 5.0 add_convert_fusion.3
  799.9 4.8 add_convert_fusion.1
  804.7 2.6 collective-permute-start.17
  807.3 2.6 fusion.41
  813.1 3.5 fusion.21
  816.6 87.2 %collective-permute-done.19 = bf16[512,512]{1,0:T(8,128)(2,1)} collective-permute-done((bf16[512,512]{1,0:T(8,128)(2,1)}, bf16[512,512]{1,0:T(8,128)(2,1)}, u32[]{:S(2)}, u32[]{:S(2)}) %collective-permute-start.19) | collective-permute-done | bytes 524320 | tf_op jit(solution)/shard_map/ppermute | solution.py:1001
  906.1 48.3 %reduce-scatter.2.cloned.1.call-done = f32[64,128]{1,0:T(8,128)} async-done(((f32[2048,128]{1,0:T(8,128)}), f32[64,128]{1,0:T(8,128)}) %reduce-scatter.2.cloned.1.call-update) | async-done | bytes 32784 | tf_op jit(solution)/shard_map/reduce_scatter | solution.py:1037
  955.8 3.0 add_convert_fusion.4
  958.8 3.6 add_convert_fusion.2
  962.4 59.8 %home5.1 = bf16[64,20992]{1,0:T(8,128)(2,1)} custom-call(bf16[8,64,512]{2,1,0:T(8,128)(2,1)} %bitcast.126, bf16[8,64,1536]{2,1,0:T(8,128)(2,1)} %bitcast.112, bf16[8,64,768]{2,1,0:T(8,128)(2,1)} %bitcast.121), custom_call_target="tpu_custom_call" | custom-call | tf_op jit(solution)/shard_map/home5/pallas_call | solution.py:585
  1022.3 4.6 convert_element_type.206
  1026.9 3.8 add_convert_fusion
  1030.7 27.3 %home6.1 = bf16[64,12288]{1,0:T(8,128)(2,1)} custom-call(bf16[8,64,1664]{2,1,0:T(8,128)(2,1)} %bitcast.111), custom_call_target="tpu_custom_call" | custom-call | tf_op jit(solution)/shard_map/home6/pallas_call | solution.py:585
  1059.6 22.9 %fusion.66 = (bf16[64,33408]{1,0:T(8,128)(2,1)}, f32[64,33408]{1,0:T(8,128)}, f32[64,33408]{1,0:T(8,128)}, f32[64,33408]{1,0:T(8,128)}, f32[64,33408]{1,0:T(8,128)}) fusion(f32[64,33408]{1,0:T(8,128)} %param.15, f32[]{:T(128)S(6)} %sub.67, f32[]{:T(128)S(6)} %sub.66, f32[]{:T(128)} %bitcast.103, f32[]{:T(128)S(6)} %sub.65, f32[64,33408]{1,0:T(8,128)} %param.17, ...), kind=kLoop, calls=%fused_computation.143 | loop fusion | flops 38486016 | bytes 72695840 | tf_op jit(solution)/shard_map/convert_element_type | solution.py:1051
  (210 shorter events, 82.8 us)
Async XLA Ops:
  7.2 15.2 %copy-start.23 = (bf16[128,2048]{1,0:T(8,128)(2,1)S(1)}, bf16[128,2048]{1,0:T(8,128)(2,1)}, u32[]{:S(2)}) copy-start(bf16[128,2048]{1,0:T(8,128)(2,1)} %param.11) | copy-start | bytes 1572868
  7.2 947.2 %reduce-scatter.2.cloned.1.call-start = ((), (), s32[]{:S(2)}) async-start(), calls=%async_computation.1 | async-start | bytes 1081344 | tf_op jit(solution)/shard_map/reduce_scatter | solution.py:1037
  10.6 16.5 %copy-start.26 = (s32[128]{0:T(128)S(1)}, s32[128]{0:T(128)}, u32[]{:S(2)}) copy-start(s32[128]{0:T(128)} %param.13) | copy-start | bytes 1540
  13.1 360.3 %collective-permute-start.6 = (bf16[128,2048]{1,0:T(8,128)(2,1)}, bf16[128,2048]{1,0:T(8,128)(2,1)}, u32[]{:S(2)}, u32[]{:S(2)}) collective-permute-start(bf16[128,2048]{1,0:T(8,128)(2,1)} %reshape.217.dy_ref), channel_id=1, source_target_pairs={{0,14},{1,15},{2,12},{3,13},{4,10},{5,11},{6,8},{7,9},{8,6},{9,7},... | collective-permute-start | bytes 1572872 | tf_op jit(solution)/shard_map/ppermute | solution.py:923
  18.0 355.9 %collective-permute-start.5 = (bf16[128,2048]{1,0:T(8,128)(2,1)}, bf16[128,2048]{1,0:T(8,128)(2,1)}, u32[]{:S(2)}, u32[]{:S(2)}) collective-permute-start(bf16[128,2048]{1,0:T(8,128)(2,1)} %reshape.217.dy_ref), channel_id=1, source_target_pairs={{0,10},{1,11},{2,8},{3,9},{4,14},{5,15},{6,12},{7,13},{8,2},{9,3},... | collective-permute-start | bytes 1572872 | tf_op jit(solution)/shard_map/ppermute | solution.py:923
  18.4 278.8 %collective-permute-start.2 = (bf16[128,2048]{1,0:T(8,128)(2,1)}, bf16[128,2048]{1,0:T(8,128)(2,1)}, u32[]{:S(2)}, u32[]{:S(2)}) collective-permute-start(bf16[128,2048]{1,0:T(8,128)(2,1)} %reshape.217.dy_ref), channel_id=1, source_target_pairs={{0,12},{1,13},{2,14},{3,15},{4,8},{5,9},{6,10},{7,11},{8,4},{9,5},... | collective-permute-start | bytes 1572872 | tf_op jit(solution)/shard_map/ppermute | solution.py:923
  20.0 274.3 %collective-permute-start.1 = (bf16[128,2048]{1,0:T(8,128)(2,1)}, bf16[128,2048]{1,0:T(8,128)(2,1)}, u32[]{:S(2)}, u32[]{:S(2)}) collective-permute-start(bf16[128,2048]{1,0:T(8,128)(2,1)} %reshape.217.dy_ref), channel_id=1, source_target_pairs={{0,8},{1,9},{2,10},{3,11},{4,12},{5,13},{6,14},{7,15},{8,0},{9,1},... | collective-permute-start | bytes 1572872 | tf_op jit(solution)/shard_map/ppermute | solution.py:923
  20.1 263.2 %collective-permute-start = (bf16[128,2048]{1,0:T(8,128)(2,1)}, bf16[128,2048]{1,0:T(8,128)(2,1)}, u32[]{:S(2)}, u32[]{:S(2)}) collective-permute-start(bf16[128,2048]{1,0:T(8,128)(2,1)} %reshape.217.dy_ref), channel_id=1, source_target_pairs={{0,4},{1,5},{2,6},{3,7},{4,0},{5,1},{6,2},{7,3},{8,12},{9,13},{10,... | collective-permute-start | bytes 1572872 | tf_op jit(solution)/shard_map/ppermute | solution.py:923
  194.3 6.4 slice-start
  211.2 6.9 copy-start.1
  211.2 72.1 %copy-start.29 = (bf16[8,64,1536]{2,1,0:T(8,128)(2,1)S(1)}, bf16[8,64,1536]{2,1,0:T(8,128)(2,1)}, u32[]{:S(2)}) copy-start(bf16[8,64,1536]{2,1,0:T(8,128)(2,1)} %get-tuple-element.38) | copy-start | bytes 4718596
  221.1 88.1 %copy-start.30 = (bf16[8,64,512]{2,1,0:T(8,128)(2,1)S(1)}, bf16[8,64,512]{2,1,0:T(8,128)(2,1)}, u32[]{:S(2)}) copy-start(bf16[8,64,512]{2,1,0:T(8,128)(2,1)} %get-tuple-element.36) | copy-start | bytes 1572868
  283.3 319.9 %copy-start.2 = (bf16[1024,512]{1,0:T(8,128)(2,1)}, bf16[1024,512]{1,0:T(8,128)(2,1)S(1)}, u32[]{:S(2)}) copy-start(bf16[1024,512]{1,0:T(8,128)(2,1)S(1)} %get-tuple-element.35) | copy-start | bytes 3145732
  283.3 89.2 %collective-permute-start.13 = (bf16[512,1536]{1,0:T(8,128)(2,1)S(1)}, bf16[512,1536]{1,0:T(8,128)(2,1)S(1)}, u32[]{:S(2)}, u32[]{:S(2)}) collective-permute-start(bf16[512,1536]{1,0:T(8,128)(2,1)S(1)} %bitcast.147), channel_id=1, source_target_pairs={{0,16},{1,17},{2,18},{3,19},{4,20},{5,21},{6,22},{7,23},{8,24},{9,... | collective-permute-start | bytes 4718600 | tf_op jit(solution)/shard_map/ppermute | solution.py:910
  294.2 15.0 %collective-permute-start.3 = (bf16[128,2048]{1,0:T(8,128)(2,1)}, bf16[128,2048]{1,0:T(8,128)(2,1)S(1)}, u32[]{:S(2)}, u32[]{:S(2)}) collective-permute-start(bf16[128,2048]{1,0:T(8,128)(2,1)} %reshape.217.dy_ref), channel_id=1, source_target_pairs={{0,2},{1,3},{2,0},{3,1},{4,6},{5,7},{6,4},{7,5},{8,10},{9,11},{10,... | collective-permute-start | bytes 1572872 | tf_op jit(solution)/shard_map/ppermute | solution.py:923
  297.2 24.6 %collective-permute-start.4 = (bf16[128,2048]{1,0:T(8,128)(2,1)}, bf16[128,2048]{1,0:T(8,128)(2,1)S(1)}, u32[]{:S(2)}, u32[]{:S(2)}) collective-permute-start(bf16[128,2048]{1,0:T(8,128)(2,1)} %reshape.217.dy_ref), channel_id=1, source_target_pairs={{0,6},{1,7},{2,4},{3,5},{4,2},{5,3},{6,0},{7,1},{8,14},{9,15},{10,... | collective-permute-start | bytes 1572872 | tf_op jit(solution)/shard_map/ppermute | solution.py:923
  309.2 91.4 %collective-permute-start.10 = (bf16[512,512]{1,0:T(8,128)(2,1)S(1)}, bf16[512,512]{1,0:T(8,128)(2,1)S(1)}, u32[]{:S(2)}, u32[]{:S(2)}) collective-permute-start(bf16[512,512]{1,0:T(8,128)(2,1)S(1)} %bitcast.151), channel_id=1, source_target_pairs={{0,16},{1,17},{2,18},{3,19},{4,20},{5,21},{6,22},{7,23},{8,24},{9,... | collective-permute-start | bytes 1572872 | tf_op jit(solution)/shard_map/ppermute | solution.py:910
  321.8 172.8 %collective-permute-start.14 = (bf16[512,1536]{1,0:T(8,128)(2,1)S(1)}, bf16[512,1536]{1,0:T(8,128)(2,1)}, u32[]{:S(2)}, u32[]{:S(2)}) collective-permute-start(bf16[512,1536]{1,0:T(8,128)(2,1)S(1)} %bitcast.148), channel_id=1, source_target_pairs={{0,1},{1,0},{2,3},{3,2},{4,5},{5,4},{6,7},{7,6},{8,9},{9,8},{10,11... | collective-permute-start | bytes 4718600 | tf_op jit(solution)/shard_map/ppermute | solution.py:911
  372.5 122.1 %collective-permute-start.15 = (bf16[512,1536]{1,0:T(8,128)(2,1)S(1)}, bf16[512,1536]{1,0:T(8,128)(2,1)}, u32[]{:S(2)}, u32[]{:S(2)}) collective-permute-start(bf16[512,1536]{1,0:T(8,128)(2,1)S(1)} %collective-permute-done.13), channel_id=1, source_target_pairs={{0,1},{1,0},{2,3},{3,2},{4,5},{5,4},{6,7},{7,6},{8,9},{9,8},{10,11... | collective-permute-start | bytes 4718600 | tf_op jit(solution)/shard_map/ppermute | solution.py:911
  373.4 31.2 %collective-permute-start.11 = (bf16[512,512]{1,0:T(8,128)(2,1)S(1)}, bf16[512,512]{1,0:T(8,128)(2,1)S(1)}, u32[]{:S(2)}, u32[]{:S(2)}) collective-permute-start(bf16[512,512]{1,0:T(8,128)(2,1)S(1)} %bitcast.152), channel_id=1, source_target_pairs={{0,1},{1,0},{2,3},{3,2},{4,5},{5,4},{6,7},{7,6},{8,9},{9,8},{10,11... | collective-permute-start | bytes 1572872 | tf_op jit(solution)/shard_map/ppermute | solution.py:911
  373.9 43.5 %collective-permute-start.7 = (bf16[512,768]{1,0:T(8,128)(2,1)}, bf16[512,768]{1,0:T(8,128)(2,1)}, u32[]{:S(2)}, u32[]{:S(2)}) collective-permute-start(bf16[512,768]{1,0:T(8,128)(2,1)} %bitcast.19), channel_id=1, source_target_pairs={{0,16},{1,17},{2,18},{3,19},{4,20},{5,21},{6,22},{7,23},{8,24},{9,... | collective-permute-start | bytes 2359304 | tf_op jit(solution)/shard_map/ppermute | solution.py:910
  400.6 21.2 %copy-start.32 = (bf16[512,512]{1,0:T(8,128)(2,1)}, bf16[512,512]{1,0:T(8,128)(2,1)S(1)}, u32[]{:S(2)}) copy-start(bf16[512,512]{1,0:T(8,128)(2,1)S(1)} %collective-permute-done.10) | copy-start | bytes 1572868
  400.6 16.8 %collective-permute-start.12 = (bf16[512,512]{1,0:T(8,128)(2,1)S(1)}, bf16[512,512]{1,0:T(8,128)(2,1)S(1)}, u32[]{:S(2)}, u32[]{:S(2)}) collective-permute-start(bf16[512,512]{1,0:T(8,128)(2,1)S(1)} %collective-permute-done.10), channel_id=1, source_target_pairs={{0,1},{1,0},{2,3},{3,2},{4,5},{5,4},{6,7},{7,6},{8,9},{9,8},{10,11... | collective-permute-start | bytes 1572872 | tf_op jit(solution)/shard_map/ppermute | solution.py:911
  404.6 17.2 %copy-start.34 = (bf16[512,512]{1,0:T(8,128)(2,1)}, bf16[512,512]{1,0:T(8,128)(2,1)S(1)}, u32[]{:S(2)}) copy-start(bf16[512,512]{1,0:T(8,128)(2,1)S(1)} %collective-permute-done.11) | copy-start | bytes 1572868
  404.6 102.4 %collective-permute-start.8 = (bf16[512,768]{1,0:T(8,128)(2,1)}, bf16[512,768]{1,0:T(8,128)(2,1)}, u32[]{:S(2)}, u32[]{:S(2)}) collective-permute-start(bf16[512,768]{1,0:T(8,128)(2,1)} %bitcast.19), channel_id=1, source_target_pairs={{0,1},{1,0},{2,3},{3,2},{4,5},{5,4},{6,7},{7,6},{8,9},{9,8},{10,11... | collective-permute-start | bytes 2359304 | tf_op jit(solution)/shard_map/ppermute | solution.py:911
  417.4 89.6 %collective-permute-start.9 = (bf16[512,768]{1,0:T(8,128)(2,1)}, bf16[512,768]{1,0:T(8,128)(2,1)}, u32[]{:S(2)}, u32[]{:S(2)}) collective-permute-start(bf16[512,768]{1,0:T(8,128)(2,1)} %collective-permute-done.7), channel_id=1, source_target_pairs={{0,1},{1,0},{2,3},{3,2},{4,5},{5,4},{6,7},{7,6},{8,9},{9,8},{10,11... | collective-permute-start | bytes 2359304 | tf_op jit(solution)/shard_map/ppermute | solution.py:911
  532.0 75.2 %copy-start.35 = (bf16[512,512]{1,0:T(8,128)(2,1)S(1)}, bf16[512,512]{1,0:T(8,128)(2,1)}, u32[]{:S(2)}) copy-start(bf16[512,512]{1,0:T(8,128)(2,1)} %copy-done.34) | copy-start | bytes 1572868
  532.0 75.2 %copy-start.37 = (bf16[512,512]{1,0:T(8,128)(2,1)S(1)}, bf16[512,512]{1,0:T(8,128)(2,1)}, u32[]{:S(2)}) copy-start(bf16[512,512]{1,0:T(8,128)(2,1)} %copy-done.36) | copy-start | bytes 1572868
  603.1 50.9 %slice-start.2 = ((s8[6815744]{0:T(1024)(128)(4,1)}), s8[4194304]{0:T(1024)(128)(4,1)S(1)}, s32[]{:S(2)}) async-start(s8[6815744]{0:T(1024)(128)(4,1)} %bitcast.133), calls=%async_computation.4 | async-start | bytes 8388608
  607.2 46.8 %slice-start.3 = ((s8[6815744]{0:T(1024)(128)(4,1)}), s8[2621440]{0:T(1024)(128)(4,1)S(1)}, s32[]{:S(2)}) async-start(s8[6815744]{0:T(1024)(128)(4,1)} %bitcast.133), calls=%async_computation.5 | async-start | bytes 5242880
  654.1 9.4 copy-start.18
  668.3 126.2 %collective-permute-start.20 = (bf16[1024,1536]{1,0:T(8,128)(2,1)}, bf16[1024,1536]{1,0:T(8,128)(2,1)}, u32[]{:S(2)}, u32[]{:S(2)}) collective-permute-start(bf16[1024,1536]{1,0:T(8,128)(2,1)} %convolution_convert_fusion.4), channel_id=1, source_target_pairs={{0,1},{1,0},{2,3},{3,2},{4,5},{5,4},{6,7},{7,6},{8,9},{9,8},{10,11... | collective-permute-start | bytes 9437192 | tf_op jit(solution)/shard_map/ppermute | solution.py:993
  674.0 126.0 %collective-permute-start.16 = (bf16[1024,1664]{1,0:T(8,128)(2,1)}, bf16[1024,1664]{1,0:T(8,128)(2,1)}, u32[]{:S(2)}, u32[]{:S(2)}) collective-permute-start(bf16[1024,1664]{1,0:T(8,128)(2,1)} %convolution_convert_fusion.2), channel_id=1, source_target_pairs={{0,1},{1,0},{2,3},{3,2},{4,5},{5,4},{6,7},{7,6},{8,9},{9,8},{10,11... | collective-permute-start | bytes 10223624 | tf_op jit(solution)/shard_map/ppermute | solution.py:993
  681.9 65.7 %copy-start.38 = (f32[1,2048]{1,0:T(1,128)S(1)}, f32[1,2048]{1,0:T(1,128)}, u32[]{:S(2)}) copy-start(f32[1,2048]{1,0:T(1,128)} %get-tuple-element.46) | copy-start | bytes 24580
  765.2 19.9 %collective-permute-start.18 = (bf16[1024,512]{1,0:T(8,128)(2,1)}, bf16[1024,512]{1,0:T(8,128)(2,1)}, u32[]{:S(2)}, u32[]{:S(2)}) collective-permute-start(bf16[1024,512]{1,0:T(8,128)(2,1)} %fusion.14), channel_id=1, source_target_pairs={{0,1},{1,0},{2,3},{3,2},{4,5},{5,4},{6,7},{7,6},{8,9},{9,8},{10,11... | collective-permute-start | bytes 3145736 | tf_op jit(solution)/shard_map/ppermute | solution.py:993
  765.3 23.2 %collective-permute-start.22 = (bf16[1024,768]{1,0:T(8,128)(2,1)}, bf16[1024,768]{1,0:T(8,128)(2,1)}, u32[]{:S(2)}, u32[]{:S(2)}) collective-permute-start(bf16[1024,768]{1,0:T(8,128)(2,1)} %fusion.11), channel_id=1, source_target_pairs={{0,1},{1,0},{2,3},{3,2},{4,5},{5,4},{6,7},{7,6},{8,9},{9,8},{10,11... | collective-permute-start | bytes 4718600 | tf_op jit(solution)/shard_map/ppermute | solution.py:993
  775.3 5.9 copy-start.9
  785.1 9.4 copy-start.12
  788.2 115.6 %collective-permute-start.19 = (bf16[512,512]{1,0:T(8,128)(2,1)}, bf16[512,512]{1,0:T(8,128)(2,1)}, u32[]{:S(2)}, u32[]{:S(2)}) collective-permute-start(bf16[512,512]{1,0:T(8,128)(2,1)} %add_convert_fusion.7), channel_id=1, source_target_pairs={{0,16},{1,17},{2,18},{3,19},{4,20},{5,21},{6,22},{7,23},{8,24},{9,... | collective-permute-start | bytes 1572872 | tf_op jit(solution)/shard_map/ppermute | solution.py:1001
  791.9 163.9 %collective-permute-start.23 = (bf16[512,768]{1,0:T(8,128)(2,1)}, bf16[512,768]{1,0:T(8,128)(2,1)}, u32[]{:S(2)}, u32[]{:S(2)}) collective-permute-start(bf16[512,768]{1,0:T(8,128)(2,1)} %add_convert_fusion.5), channel_id=1, source_target_pairs={{0,16},{1,17},{2,18},{3,19},{4,20},{5,21},{6,22},{7,23},{8,24},{9,... | collective-permute-start | bytes 2359304 | tf_op jit(solution)/shard_map/ppermute | solution.py:1001
  799.6 7.7 copy-start.14
  799.6 7.7 copy-start.15
  799.6 159.2 %collective-permute-start.21 = (bf16[512,1536]{1,0:T(8,128)(2,1)}, bf16[512,1536]{1,0:T(8,128)(2,1)}, u32[]{:S(2)}, u32[]{:S(2)}) collective-permute-start(bf16[512,1536]{1,0:T(8,128)(2,1)} %add_convert_fusion.3), channel_id=1, source_target_pairs={{0,16},{1,17},{2,18},{3,19},{4,20},{5,21},{6,22},{7,23},{8,24},{9,... | collective-permute-start | bytes 4718600 | tf_op jit(solution)/shard_map/ppermute | solution.py:1001
  804.7 8.4 copy-start.20
  804.7 222.2 %collective-permute-start.17 = (bf16[512,1664]{1,0:T(8,128)(2,1)}, bf16[512,1664]{1,0:T(8,128)(2,1)}, u32[]{:S(2)}, u32[]{:S(2)}) collective-permute-start(bf16[512,1664]{1,0:T(8,128)(2,1)} %add_convert_fusion.1), channel_id=1, source_target_pairs={{0,16},{1,17},{2,18},{3,19},{4,20},{5,21},{6,22},{7,23},{8,24},{9,... | collective-permute-start | bytes 5111816 | tf_op jit(solution)/shard_map/ppermute | solution.py:1001
  813.1 90.7 %copy-start.21 = (f32[512,512]{1,0:T(8,128)S(1)}, f32[512,512]{1,0:T(8,128)}, u32[]{:S(2)}) copy-start(f32[512,512]{1,0:T(8,128)} %fusion.31) | copy-start | bytes 3145732
  816.6 142.2 %copy-start.13 = (f32[512,1536]{1,0:T(8,128)S(1)}, f32[512,1536]{1,0:T(8,128)}, u32[]{:S(2)}) copy-start(f32[512,1536]{1,0:T(8,128)} %fusion.27) | copy-start | bytes 9437188
  1030.7 28.9 %copy-start.24 = (f32[64,128]{1,0:T(8,128)S(1)}, f32[64,128]{1,0:T(8,128)}, u32[]{:S(2)}) copy-start(f32[64,128]{1,0:T(8,128)} %reduce-scatter.2.cloned.1.call-done) | copy-start | bytes 98308
  (20 other events, 72.0 us)
Sparse Core Ops, SparseCore 0:
  775.4 178.8 reduce-scatter.1

commit v2 on v1

--- a/solution.py
+++ b/solution.py
@@ -26,7 +26,6 @@
 EPS_GATED = 1e-05
 EPS_ADAM = 1e-08
 DECAY_WEIGHT = 0.1
-HIGH = lax.Precision.HIGHEST
 MESH = pl.DeviceIdType.MESH
 
 RANKS = 8
@@ -39,8 +38,9 @@
 FULL_RANKS = TILES - (TILES // RANKS) * RANKS
 FT = TILES // RANKS + 1
 FW = FT * 128
-ORDERS = ((4, 2, 1), (2, 1, 4), (1, 4, 2))
-PLAIN = ((2, 4, 1), (2, 1, 4))
+SPLIT = ((4, 1, 2), (1, 2, 4), (2, 4, 1))
+MEET = ((2, 1, 4), (4, 2, 1), (1, 4, 2))
+MEET_EARLY = ((2, 4, 1), (2, 1, 4))
 BF = jnp.bfloat16
 F32 = jnp.float32
 
@@ -89,11 +89,11 @@
     )
 
 
-def row_parts(tokens):
-    if tokens == 128:
-        return ((0, 48), (48, 48), (96, 32))
-    third = tokens // 48 * 16
-    return ((0, third), (third, third), (2 * third, tokens - 2 * third))
+def row_parts(tokens, count):
+    tiles = tokens // 16
+    sizes = [16 * (tiles * (at + 1) // count - tiles * at // count) for at in range(count)]
+    sizes.sort(reverse=True)
+    return tuple((sum(sizes[:at]), sizes[at]) for at in range(count))
 
 
 class Gather:
@@ -207,38 +207,50 @@
     return mixer, outward, gates, down
 
 
+def feature_blocks(place):
+    copies = place.copies
+    width = D // (4 * copies)
+    if width % 128:
+        return [(0, 0, D)]
+    found = []
+    for core in range(2):
+        for copy in range(copies):
+            for x in range(2):
+                block = (x * 2 + (place.core + core) % 2) * copies + (place.dp + copy) % copies
+                found.append((block * width, ((core * copies + copy) * 2 + x) * width, width))
+    return found
+
+
 def columns(at, width):
     if not isinstance(at, int):
         at = pl.multiple_of(at, 128)
     return pl.ds(at, width)
 
 
-def spread_kernel(copies, parts, w_ref, x_ref, s_ref, mix, outward, gates, down, xall, sall,
-                  local, send, recv, seg_send, seg_recv, ag_send, ag_recv,
-                  copy_send, copy_recv, core_send, core_recv):
+def spread_kernel(copies, parts, w_ref, x_ref, dy_ref, s_ref, mix, outward, gates, down, xall, sall, x_own, dy_own,
+                  pack, pack_sem, local, send, recv, seg_send, seg_recv,
+                  ag_send, ag_recv, copy_send, copy_recv, core_send, core_recv, side_send, side_recv, turned):
     place = Place(copies)
     peers = [place.peer(mask) for mask in range(1, RANKS)]
     partners = [place.copy_at(shift) for shift in range(1, copies)]
     meet(peers + partners + [place.sibling()])
     me = place.rank
-    targets = (mix.at[0, 0], outward, gates, down)
+    targets = (mix.at[0, 0], outward.at[0], gates.at[0], down.at[0])
+    others = (None, outward.at[1], gates.at[1], down.at[1])
     own = []
     firsts = (0, 5, 6, 8)
-    for group, pieces in enumerate(first_columns(me)):
+    packed = []
+    for mask in range(RANKS):
+        there = place.flip(mask)
         here = []
-        for slot, (at, to, width) in enumerate(pieces):
+        for slot, (at, to, width) in enumerate(first_columns(there)[0]):
             copy = pltpu.make_async_copy(
-                w_ref.at[:, columns(at, width)], targets[group].at[me, :, pl.ds(to, width)],
-                local.at[firsts[group] + slot],
+                w_ref.at[:, columns(at, width)], pack.at[mask, :, pl.ds(to, width)], pack_sem.at[mask, slot]
             )
             copy.start()
             here.append(copy)
-        own.append(here)
-    own_x = pltpu.make_async_copy(x_ref, xall.at[me], local.at[9])
-    own_x.start()
-    own_s = pltpu.make_async_copy(s_ref, sall.at[me], local.at[10])
-    own_s.start()
-
+        packed.append(here)
+    own_mix = pltpu.make_async_copy(pack.at[0], mix.at[0, 0, me], local.at[0])
     def send_group(group):
         flights = []
         for mask in range(1, RANKS):
@@ -259,11 +271,11 @@
         block = targets[group].at[place.flip(mask)]
         remote(block, block, send.at[0, mask - 1], recv.at[group, mask - 1], place.peer(mask)).wait_recv()
 
-    sent = send_group(0)
+    sent = []
     onward = []
 
     def forward(mask):
-        block = mix.at[0, 0, place.flip(mask)]
+        block = mix.at[0, 0, place.flip(mask)] if mask else pack.at[0]
         for shift in range(1, copies):
             copy = remote(
                 block, mix.at[0, copies - shift, place.flip(mask)],
@@ -279,9 +291,41 @@
         copy.start()
         onward.append(copy)
 
-    for copy in own[0]:
+    for mask in range(1, RANKS):
+        for copy in packed[mask]:
+            copy.wait()
+        copy = remote(
+            pack.at[mask], mix.at[0, 0, me], send.at[0, mask - 1], recv.at[0, mask - 1], place.peer(mask)
+        )
+        copy.start()
+        sent.append(copy)
+    for copy in packed[0]:
         copy.wait()
+    own_mix.start()
     forward(0)
+    turns = []
+    for row, (source, target) in enumerate(((x_ref, xall.at[me]), (x_ref, x_own), (dy_ref, dy_own))):
+        here = []
+        for slot, (at, to, width) in enumerate(feature_blocks(place)):
+            copy = pltpu.make_async_copy(
+                source.at[:, columns(at, width)], target.at[:, pl.ds(to, width)], turned.at[row, slot]
+            )
+            copy.start()
+            here.append(copy)
+        turns.append(here)
+    own_s = pltpu.make_async_copy(s_ref, sall.at[me], local.at[10])
+    own_s.start()
+
+    for group in range(1, 4):
+        here = []
+        for slot, (at, to, width) in enumerate(first_columns(me)[group]):
+            copy = pltpu.make_async_copy(
+                w_ref.at[:, columns(at, width)], targets[group].at[me, :, pl.ds(to, width)],
+                local.at[firsts[group] + slot],
+            )
+            copy.start()
+            here.append(copy)
+        own.append(here)
     own_s.wait()
     seg_flights = []
     for mask in range(1, RANKS):
@@ -291,8 +335,9 @@
     for mask in range(1, RANKS):
         got(0, mask)
         forward(mask)
-    own_x.wait()
-    gather = Gather(place, xall, parts, PLAIN, ag_send, ag_recv)
+    for copy in turns[0]:
+        copy.wait()
+    gather = Gather(place, xall, parts, MEET_EARLY, ag_send, ag_recv)
     for part in range(len(parts)):
         gather.start(part, 0)
     for group in range(1, 4):
@@ -315,8 +360,23 @@
             copy.start()
             onward.append(copy)
     for group in range(1, 4):
-        for mask in range(1, RANKS):
-            got(group, mask)
+        for copy in own[group - 1]:
+            copy.wait()
+        for mask in range(RANKS):
+            if mask:
+                got(group, mask)
+            copy = remote(
+                targets[group].at[place.flip(mask)], others[group].at[place.flip(mask)],
+                side_send.at[group - 1, mask], side_recv.at[group - 1, mask], place.sibling(),
+            )
+            copy.start()
+            onward.append(copy)
+    for group in range(1, 4):
+        for mask in range(RANKS):
+            block = others[group].at[place.flip(mask)]
+            remote(
+                block, block, side_send.at[group - 1, mask], side_recv.at[group - 1, mask], place.sibling()
+            ).wait_recv()
     for shift in range(copies):
         for mask in range(RANKS):
             block = mix.at[1, shift, place.flip(mask)]
@@ -325,7 +385,8 @@
             ).wait_recv()
     for copy in seg_flights:
         copy.wait()
-    for here in own[1:]:
+    own_mix.wait()
+    for here in turns[1:]:
         for copy in here:
             copy.wait()
     for copy in sent + onward:
@@ -341,11 +402,15 @@
     return pl.BlockSpec(memory_space=pltpu.VMEM)
 
 
+def takes(micros):
+    return pl.CostEstimate(flops=0, bytes_accessed=int(micros * 1e3), transcendentals=0)
+
+
 def dma(*shape):
     return pltpu.SemaphoreType.DMA(shape)
 
 
-def spread(copies, weights, x, seg):
+def spread(copies, weights, x, dy, seg):
     rows = weights.shape[0]
     tokens = x.shape[0]
     shape = jax.ShapeDtypeStruct
@@ -353,26 +418,50 @@
         functools.partial(spread_kernel, copies, ((0, tokens // 2), (tokens // 2, tokens // 2))),
         out_shape=(
             shape((2, copies, RANKS, rows, MIXW), BF),
-            shape((RANKS, rows, OW), BF),
-            shape((RANKS, rows, 2 * FW), BF),
-            shape((RANKS, rows, FW), BF),
+            shape((2, RANKS, rows, OW), BF),
+            shape((2, RANKS, rows, 2 * FW), BF),
+            shape((2, RANKS, rows, FW), BF),
             shape((RANKS, tokens, D), BF),
             shape((RANKS,) + seg.shape, seg.dtype),
+            shape((tokens, D), BF),
+            shape((tokens, D), BF),
         ),
-        in_specs=[any_spec()] * 3,
-        out_specs=[any_spec()] * 6,
+        in_specs=[any_spec(), vmem_spec(), vmem_spec(), any_spec()],
+        out_specs=[any_spec()] * 8,
         scratch_shapes=[
-            dma(11), dma(9, RANKS - 1), dma(4, RANKS - 1), dma(RANKS - 1), dma(RANKS - 1),
-            dma(3, 7), dma(3, 7),
+            pltpu.VMEM((RANKS, rows, MIXW), BF), dma(RANKS, 5), dma(11), dma(9, RANKS - 1), dma(4, RANKS - 1),
+            dma(RANKS - 1), dma(RANKS - 1), dma(3, 7), dma(3, 7),
             dma(copies - 1, RANKS), dma(copies - 1, RANKS), dma(copies, RANKS), dma(copies, RANKS),
+            dma(3, RANKS), dma(3, RANKS), dma(3, 4 * copies),
         ],
         compiler_params=pltpu.CompilerParams(collective_id=1, has_side_effects=True),
+        cost_estimate=takes(5),
         name="spread",
-    )(weights, x, seg)
+    )(weights, x, dy, seg)
 
 
 def norm_scale(values, epsilon):
     return lax.rsqrt(jnp.mean(values * values, axis=-1, keepdims=True) + epsilon)
+
+
+def sum_then_gather(scatter, gather, finish_rows):
+    parts = range(len(scatter.parts))
+    for part in parts:
+        scatter.start(part, 0)
+    for stage in range(2):
+        for part in parts:
+            scatter.add(part, stage)
+            scatter.start(part, stage + 1)
+    for part in parts:
+        finish_rows(part, scatter.add(part, 2))
+        gather.start(part, 0)
+    for stage in range(3):
+        for part in parts:
+            gather.landed(part, stage)
+            if stage < 2:
+                gather.start(part, stage + 1)
+    scatter.finish()
+    gather.finish()
 
 
 def branch_kernel(copies, parts, part_ref, x_ref, gain_ref, hidden_ref, nall, land,
@@ -380,28 +469,17 @@
     place = Place(copies)
     meet([place.peer(mask) for mask in (4, 2, 1)])
     me = place.rank
-    scatter = Scatter(place, part_ref, land, parts, ORDERS, send, recv)
-    gather = Gather(place, nall, parts, ORDERS, ag_send, ag_recv)
-    for part in range(3):
-        scatter.start(part, 0)
-    for stage in range(2):
-        for part in range(3):
-            scatter.add(part, stage)
-            scatter.start(part, stage + 1)
-    for part in range(3):
+    scatter = Scatter(place, part_ref, land, parts, SPLIT, send, recv)
+    gather = Gather(place, nall, parts, MEET, ag_send, ag_recv)
+
+    def finish_rows(part, total):
         first, rows = parts[part]
-        hidden = x_ref[pl.ds(first, rows)].astype(F32) + scatter.add(part, 2)
+        hidden = x_ref[pl.ds(first, rows)].astype(F32) + total
         hidden_ref[pl.ds(first, rows)] = hidden
         unit = hidden * norm_scale(hidden, EPS_NORM)
         nall[me, pl.ds(first, rows)] = (unit * gain_ref[...]).astype(BF)
-        gather.start(part, 0)
-    for stage in range(3):
-        for part in range(3):
-            gather.landed(part, stage)
-            if stage < 2:
-                gather.start(part, stage + 1)
-    scatter.finish()
-    gather.finish()
+
+    sum_then_gather(scatter, gather, finish_rows)
 
 
 def cube_scratch(tokens):
@@ -415,12 +493,13 @@
     tokens = x.shape[0]
     shape = jax.ShapeDtypeStruct
     return pl.pallas_call(
-        functools.partial(branch_kernel, copies, row_parts(tokens)),
+        functools.partial(branch_kernel, copies, row_parts(tokens, 3)),
         out_shape=(shape((tokens, D), F32), shape((RANKS, tokens, D), BF)),
         in_specs=[vmem_spec()] * 3,
         out_specs=[vmem_spec()] * 2,
         scratch_shapes=cube_scratch(tokens) + [dma(3, 7), dma(3, 7)],
         compiler_params=pltpu.CompilerParams(collective_id=2, has_side_effects=True, vmem_limit_bytes=BIG),
+        cost_estimate=takes(5),
         name="branch",
     )(partial, x, gain)
 
@@ -438,163 +517,178 @@
     place = Place(copies)
     meet([place.peer(mask) for mask in (4, 2, 1)])
     me = place.rank
-    scatter = Scatter(place, part_ref, land, parts, ORDERS, send, recv)
-    gather = Gather(place, dall, parts, ORDERS, ag_send, ag_recv)
-    for part in range(3):
-        scatter.start(part, 0)
-    for stage in range(2):
-        for part in range(3):
-            scatter.add(part, stage)
-            scatter.start(part, stage + 1)
-    total = jnp.zeros((1, D), F32)
-    for part in range(3):
+    scatter = Scatter(place, part_ref, land, parts, SPLIT, send, recv)
+    gather = Gather(place, dall, parts, MEET, ag_send, ag_recv)
+    gain_grad[...] = jnp.zeros_like(gain_grad)
+
+    def finish_rows(part, total):
         first, rows = parts[part]
-        back, gain_part = norm_back(
-            scatter.add(part, 2), h_ref[pl.ds(first, rows)], gain_ref[...], EPS_NORM
-        )
+        back, gain_part = norm_back(total, h_ref[pl.ds(first, rows)], gain_ref[...], EPS_NORM)
         back = dy_ref[pl.ds(first, rows)].astype(F32) + back
         dh_ref[pl.ds(first, rows)] = back
         dall[me, pl.ds(first, rows)] = back.astype(BF)
-        gather.start(part, 0)
-        total = total + jnp.sum(gain_part, axis=0, keepdims=True)
-    gain_grad[...] = total
-    for stage in range(3):
-        for part in range(3):
-            gather.landed(part, stage)
-            if stage < 2:
-                gather.start(part, stage + 1)
-    scatter.finish()
-    gather.finish()
+        gain_grad[...] += jnp.sum(gain_part, axis=0, keepdims=True)
+
+    sum_then_gather(scatter, gather, finish_rows)
 
 
 def hidden_back(copies, partial, hidden, dy, gain):
     tokens = dy.shape[0]
     shape = jax.ShapeDtypeStruct
     return pl.pallas_call(
-        functools.partial(hidden_back_kernel, copies, row_parts(tokens)),
+        functools.partial(hidden_back_kernel, copies, row_parts(tokens, 3)),
         out_shape=(shape((tokens, D), F32), shape((1, D), F32), shape((RANKS, tokens, D), BF)),
         in_specs=[vmem_spec()] * 4,
         out_specs=[vmem_spec()] * 3,
         scratch_shapes=cube_scratch(tokens) + [dma(3, 7), dma(3, 7)],
         compiler_params=pltpu.CompilerParams(collective_id=3, has_side_effects=True, vmem_limit_bytes=BIG),
+        cost_estimate=takes(5),
         name="hidden_back",
     )(partial, hidden, dy, gain)
 
 
-def ends_kernel(copies, parts, dn_ref, feed_ref, h_ref, dh_ref, x_ref, gain_ref, out_ref, in_grad, gain_grad,
-                dn_land, dn_send, dn_recv, feed_land, feed_send, feed_recv):
-    place = Place(copies)
-    meet([place.peer(mask) for mask in (4, 2, 1)])
-    back = Scatter(place, dn_ref, dn_land, parts, ORDERS, dn_send, dn_recv)
-    feed = Scatter(place, feed_ref, feed_land, parts, ORDERS, feed_send, feed_recv)
-    for part in range(3):
-        back.start(part, 0)
-    for part in range(3):
-        feed.start(part, 0)
-    for stage in range(2):
-        for one in (back, feed):
-            for part in range(3):
-                one.add(part, stage)
-                one.start(part, stage + 1)
-    total = jnp.zeros((1, D), F32)
-    for part in range(3):
-        first, rows = parts[part]
-        grad, gain_part = norm_back(
-            back.add(part, 2), x_ref[pl.ds(first, rows)].astype(F32), gain_ref[...], EPS_NORM
-        )
-        in_grad[pl.ds(first, rows)] = (dh_ref[pl.ds(first, rows)] + grad).astype(BF)
-        total = total + jnp.sum(gain_part, axis=0, keepdims=True)
-    gain_grad[...] = total
-    for part in range(3):
-        first, rows = parts[part]
-        out_ref[pl.ds(first, rows)] = (h_ref[pl.ds(first, rows)] + feed.add(part, 2)).astype(BF)
-    back.finish()
-    feed.finish()
-
-
-def ends(copies, dn_part, feed_part, hidden, d_hidden, x, gain):
-    tokens = x.shape[0]
-    shape = jax.ShapeDtypeStruct
-    return pl.pallas_call(
-        functools.partial(ends_kernel, copies, row_parts(tokens)),
-        out_shape=(shape((tokens, D), BF), shape((tokens, D), BF), shape((1, D), F32)),
-        in_specs=[vmem_spec()] * 6,
-        out_specs=[vmem_spec()] * 3,
-        scratch_shapes=cube_scratch(tokens) + cube_scratch(tokens),
-        compiler_params=pltpu.CompilerParams(collective_id=4, has_side_effects=True, vmem_limit_bytes=BIG),
-        name="ends",
-    )(dn_part, feed_part, hidden, d_hidden, x, gain)
-
-
-def home_kernel(copies, groups, base, n_in, *refs):
-    ins, out = refs[:n_in], refs[n_in]
-    local, send, recv = refs[n_in + 1 :]
-    place = Place(copies)
-    meet([place.peer(mask) for mask in range(1, RANKS)])
-    me = place.rank
-
-    def pieces(rank):
+class Home:
+    def __init__(self, place, groups, ins, out, local, send, recv):
+        self.place, self.groups, self.ins, self.out = place, groups, ins, out
+        self.local, self.send, self.recv = local, send, recv
+
+    def pieces(self, rank):
         found = []
-        for index, group in enumerate(groups):
+        for group, source in zip(self.groups, self.ins):
             for at, to, width in first_columns(rank)[group]:
-                if group == 0 and width == EXTRA and to == 2 * QW + 2 * VW:
+                if group == 0 and to == 2 * QW + 2 * VW:
                     continue
-                if group >= 2:
-                    found.append((index, to, at - base, width - 128, False))
-                    found.append((index, to + width - 128, at - base + width - 128, 128, True))
+                if group == 2:
+                    found.append((source[to // FW], 0, at, width - 128, False))
+                    found.append((source[to // FW], width - 128, at + width - 128, 128, True))
+                elif group == 3:
+                    found.append((source, 0, at, width - 128, False))
+                    found.append((source, width - 128, at + width - 128, 128, True))
                 else:
-                    found.append((index, to, at - base, width, False))
+                    found.append((source, to, at, width, False))
         return found
 
-    def when(flag, rank, act):
+    def when(self, flag, rank, act):
         if flag:
             pl.when(rank < FULL_RANKS)(act)
         else:
             act()
 
-    def run(method):
-        for slot, (index, to, at, width, flag) in enumerate(pieces(me)):
+    def run(self, method):
+        place = self.place
+        me = place.rank
+        for slot, (source, to, at, width, flag) in enumerate(self.pieces(me)):
             copy = pltpu.make_async_copy(
-                ins[index].at[me, :, pl.ds(to, width)], out.at[:, columns(at, width)], local.at[slot]
+                source.at[me, :, pl.ds(to, width)],
+                self.out.at[:, columns(at, width)],
+                self.local.at[slot],
             )
-            when(flag, me, getattr(copy, method))
+            self.when(flag, me, getattr(copy, method))
         for mask in range(1, RANKS):
             there = place.flip(mask)
-            for slot, (index, to, at, width, flag) in enumerate(pieces(me)):
+            for slot, (source, to, at, width, flag) in enumerate(self.pieces(me)):
                 copy = remote(
-                    ins[index].at[there, :, pl.ds(to, width)], out.at[:, columns(at, width)],
-                    send.at[mask - 1, slot], recv.at[mask - 1, slot], place.peer(mask),
+                    source.at[there, :, pl.ds(to, width)],
+                    self.out.at[:, columns(at, width)],
+                    self.send.at[mask - 1, slot],
+                    self.recv.at[mask - 1, slot],
+                    place.peer(mask),
                 )
-                when(flag, me, copy.start if method == "start" else copy.wait_send)
+                self.when(flag, me, copy.start if method == "start" else copy.wait_send)
             if method == "wait":
-                for slot, (index, to, at, width, flag) in enumerate(pieces(there)):
-                    block = out.at[:, columns(at, width)]
+                for slot, (source, to, at, width, flag) in enumerate(self.pieces(there)):
+                    block = self.out.at[:, columns(at, width)]
                     copy = remote(
-                        block, block, send.at[mask - 1, slot], recv.at[mask - 1, slot], place.peer(mask)
+                        block, block, self.send.at[mask - 1, slot], self.recv.at[mask - 1, slot], place.peer(mask)
                     )
-                    when(flag, there, copy.wait_recv)
-
-    run("start")
-    run("wait")
-
-
-def home(copies, ident, groups, arrays):
-    rows = arrays[0].shape[1]
-    base = 0 if groups[0] == 0 else MIX_END
-    width = MIX_END if groups[0] == 0 else EXTRA_START - MIX_END
+                    self.when(flag, there, copy.wait_recv)
+
+
+def home_scratch():
+    return [dma(7), dma(RANKS - 1, 7), dma(RANKS - 1, 7)]
+
+
+def home_kernel(copies, mix_ref, extra_ref, out, extra_out, local, send, recv, land, own, far, near):
+    place = Place(copies)
+    meet([place.peer(mask) for mask in range(1, RANKS)])
+    way = Home(place, (0,), (mix_ref,), out, local, send, recv)
+    flights = []
+    for mask in range(1, RANKS):
+        copy = remote(
+            extra_ref.at[place.flip(mask)], land.at[mask - 1], far.at[mask - 1], near.at[mask - 1], place.peer(mask)
+        )
+        copy.start()
+        flights.append(copy)
+    way.run("start")
+    mine = pltpu.make_async_copy(extra_ref.at[place.rank], own, local.at[6])
+    mine.start()
+    mine.wait()
+    total = own[...]
+    for mask in range(1, RANKS):
+        flights[mask - 1].wait_recv()
+        total = total + land[mask - 1]
+    extra_out[...] = total
+    for copy in flights:
+        copy.wait_send()
+    way.run("wait")
+
+
+def home(copies, array, extra):
+    rows = array.shape[1]
+    shape = jax.ShapeDtypeStruct
     return pl.pallas_call(
-        functools.partial(home_kernel, copies, groups, base, len(arrays)),
-        out_shape=jax.ShapeDtypeStruct((rows, width), BF),
-        in_specs=[any_spec()] * len(arrays),
+        functools.partial(home_kernel, copies),
+        out_shape=(shape((rows, MIX_END), BF), shape((rows, EXTRA), F32)),
+        in_specs=[any_spec()] * 2,
+        out_specs=(any_spec(), vmem_spec()),
+        scratch_shapes=home_scratch()
+        + [pltpu.VMEM((RANKS - 1, rows, EXTRA), F32), pltpu.VMEM((rows, EXTRA), F32), dma(RANKS - 1), dma(RANKS - 1)],
+        compiler_params=pltpu.CompilerParams(collective_id=6, has_side_effects=True),
+        cost_estimate=takes(5),
+        name="home",
+    )(array, extra)
+
+
+def home_rest_kernel(copies, out_rows, gate_rows, up_rows, down_rows, rest, local, send, recv):
+    place = Place(copies)
+    meet([place.peer(mask) for mask in range(1, RANKS)])
+    way = Home(place, (1, 2, 3), (out_rows, (gate_rows, up_rows), down_rows), rest, local, send, recv)
+    way.run("start")
+    way.run("wait")
+
+
+def home_rest(copies, grad_rows):
+    rows = grad_rows[0].shape[1]
+    return pl.pallas_call(
+        functools.partial(home_rest_kernel, copies),
+        out_shape=jax.ShapeDtypeStruct((rows, EXTRA_START), BF),
+        in_specs=[any_spec()] * 4,
         out_specs=any_spec(),
-        scratch_shapes=[dma(7), dma(RANKS - 1, 7), dma(RANKS - 1, 7)],
-        compiler_params=pltpu.CompilerParams(collective_id=ident, has_side_effects=True),
-        name="home%d" % ident,
-    )(*arrays)
-
-
-def mul(left, right, axes, precision=HIGH):
-    return lax.dot_general(left, right, (axes, ((), ())), precision=precision, preferred_element_type=F32)
+        scratch_shapes=home_scratch(),
+        compiler_params=pltpu.CompilerParams(collective_id=4, has_side_effects=True),
+        cost_estimate=takes(5),
+        name="home_rest",
+    )(*grad_rows)
+
+
+def dot(left, right, axes):
+    return lax.dot_general(left, right, (axes, ((), ())), preferred_element_type=F32)
+
+
+def halves(values):
+    high = values.astype(BF)
+    return high, (values - high.astype(F32)).astype(BF)
+
+
+def mul(left, right, axes):
+    left_high, left_low = halves(left)
+    right_high, right_low = halves(right)
+    return dot(left_high, right_high, axes) + (dot(left_high, right_low, axes) + dot(left_low, right_high, axes))
+
+
+def mul_mask(mask, right, axes):
+    right_high, right_low = halves(right)
+    return dot(mask, right_high, axes) + dot(mask, right_low, axes)
 
 
 NN = ((1,), (0,))
@@ -602,16 +696,17 @@
 TN = ((0,), (0,))
 
 
-def unit_lower_inverse(lower, row, col):
-    size = lower.shape[0]
-    inverse = jnp.where(row == col, 1.0, jnp.where(row // 2 == col // 2, -lower, 0.0))
-    block = 2
-    while block < size:
-        joined = (row // (2 * block) == col // (2 * block)) & (row // block != col // block)
-        part = mul(jnp.where(joined, lower, 0.0), inverse, NN)
-        inverse = inverse - mul(inverse, part, NN)
-        block = block * 2
-    return inverse
+def unit_lower_inverses(lowers, row, col):
+    size = lowers[0].shape[0]
+    pair = (row >> 1) == (col >> 1)
+    inverses = [jnp.where(row == col, 1.0, jnp.where(pair, -lower, 0.0)) for lower in lowers]
+    level = 1
+    while 2**level < size:
+        joined = ((row >> (level + 1)) == (col >> (level + 1))) & ((row >> level) != (col >> level))
+        parts = [mul(jnp.where(joined, lower, 0.0), inverse, NN) for lower, inverse in zip(lowers, inverses)]
+        inverses = [inverse - mul(inverse, part, NN) for inverse, part in zip(inverses, parts)]
+        level = level + 1
+    return inverses
 
 
 class Sequence:
@@ -626,7 +721,7 @@
         same = turned == ids
         self.inclusive = same & (self.row >= self.col)
         self.strict = same & (self.row > self.col)
-        self.lower = (self.row >= self.col).astype(F32)
+        self.lower = (self.row >= self.col).astype(BF)
         column = turned[:, :1]
         at = self.row[:, :1]
         self.near = [None]
@@ -686,7 +781,7 @@
         self.beta = jax.nn.sigmoid(pick_lane(pair, self.lane_b))
         self.decay = -self.rate * softplus(self.a)
         spread_out = jnp.where(seq.row > seq.col, jnp.broadcast_to(self.decay, seq.row.shape), 0.0)
-        gap = mul(seq.lower, spread_out, NN)
+        gap = mul_mask(seq.lower, spread_out, NN)
         self.pairs = jnp.where(seq.inclusive, jnp.exp(jnp.where(seq.inclusive, gap, 0.0)), 0.0)
         self.kk = mul(self.k, self.k, NT)
         self.qk = mul(self.q, self.k, NT)
@@ -699,11 +794,11 @@
 def mixer_kernel(rank_ref, scalars, seg_ref, p_ref, taps_ref, gain_ref, z_ref, inv_ref, upd_ref):
     seq = Sequence(seg_ref[0, :1])
     rank = rank_ref[0]
-    for head in range(HEADS):
-        one = Head(seq, head, rank, scalars, p_ref, taps_ref)
-        inverse = unit_lower_inverse(one.lower, seq.row, seq.col)
-        update = mul(inverse, one.beta * one.v, NN)
-        out = mul(one.attend, update, NN)
+    ones = [Head(seq, head, rank, scalars, p_ref, taps_ref) for head in range(HEADS)]
+    inverses = unit_lower_inverses([one.lower for one in ones], seq.row, seq.col)
+    updates = [mul(inverse, one.beta * one.v, NN) for inverse, one in zip(inverses, ones)]
+    outs = [mul(one.attend, update, NN) for one, update in zip(ones, updates)]
+    for head, (one, inverse, update, out) in enumerate(zip(ones, inverses, updates, outs)):
         normed = out * norm_scale(out, EPS_GATED) * gain_ref[...]
         z_ref[:, head * DV : (head + 1) * DV] = (normed * (one.gate * jax.nn.sigmoid(one.gate))).astype(BF)
         inv_ref[0, head] = inverse
@@ -753,7 +848,7 @@
         d_kk = d_lower * (one.beta * one.strict_pairs)
         d_q = mul(d_qk, one.k, NN)
         d_k = mul(d_qk, one.q, TN) + mul(d_kk, one.k, NN) + mul(d_kk, one.k, TN)
-        reach = mul(seq.lower, d_gap, TN)
+        reach = mul_mask(seq.lower, d_gap, TN)
         d_decay = jnp.sum(jnp.where(seq.row > seq.col, reach, 0.0), axis=1, keepdims=True)
         d_a = d_decay * (-one.rate) * jax.nn.sigmoid(one.a)
         d_b = d_beta * one.beta * (1 - one.beta)
@@ -813,6 +908,7 @@
             by_sequence(tokens, VW), by_sequence(1, HEADS, tokens, tokens), by_sequence(1, HEADS, tokens, DV),
         ],
         compiler_params=pltpu.CompilerParams(vmem_limit_bytes=40 * 2**20),
+        cost_estimate=takes(5),
         name="mixer",
     )(rank, scalars, seg, p, taps, gain)
 
@@ -838,8 +934,168 @@
             by_sequence(tokens, MIXW), whole_block(CONV, CHANNELS), whole_block(1, DV), whole_block(8, 128),
         ],
         compiler_params=pltpu.CompilerParams(vmem_limit_bytes=40 * 2**20),
+        cost_estimate=takes(5),
         name="mixer_back",
     )(rank, scalars, seg, p, taps, gain, inverse, update, dz)
+
+
+def adam_kernel(filled, scalars, grad_ref, one_ref, two_ref, master_ref, *refs):
+    grad_out, one_out, two_out, master_out, weight_out = refs[filled:]
+    beta_one, beta_two, rate = scalars[0], scalars[1], scalars[2]
+    grad = grad_ref[...].astype(F32)
+    one = beta_one * one_ref[...] + (1 - beta_one) * grad
+    two = beta_two * two_ref[...] + (1 - beta_two) * grad * grad
+    master = master_ref[...]
+    change = (one / scalars[3]) / (jnp.sqrt(two / scalars[4]) + EPS_ADAM) + DECAY_WEIGHT * master
+    master = master - rate * change
+    grad_out[...] = grad
+    one_out[...] = one
+    two_out[...] = two
+    master_out[...] = master
+    weight_out[...] = master.astype(BF)
+
+
+def adam(scalars, grads, state, done, first, width, count):
+    rows = grads.shape[0]
+    at_first = first // width
+    grad_first = at_first if grads.shape[1] > first else 0
+    shape = jax.ShapeDtypeStruct
+    there = pl.BlockSpec((rows, width), lambda at: (0, at + at_first))
+    filled = () if done is None else tuple(done)
+    return pl.pallas_call(
+        functools.partial(adam_kernel, len(filled)),
+        grid=(count,),
+        out_shape=(shape((rows, COLS), F32),) * 4 + (shape((rows, COLS), BF),),
+        in_specs=[smem_spec(), pl.BlockSpec((rows, width), lambda at: (0, at + grad_first))]
+        + [there] * 3 + [any_spec()] * len(filled),
+        out_specs=[there] * 5,
+        input_output_aliases={5 + at: at for at in range(len(filled))},
+        compiler_params=pltpu.CompilerParams(vmem_limit_bytes=40 * 2**20),
+        cost_estimate=takes(5),
+        name="adam",
+    )(scalars, grads, *state, *filled)
+
+
+def weight_grad_kernel(left_ref, right_ref, *refs):
+    total = dot(left_ref[...], right_ref[...], TN)
+    for ref in refs[:-1]:
+        total = total + ref[...].astype(F32)
+    refs[-1][...] = total.astype(BF)
+
+
+def weight_grad(left, right, at, width, adds=()):
+    tokens, count = right.shape
+    tile = 768 if count % 768 == 0 else count
+
+    def add_spec(row, column):
+        return pl.BlockSpec((width, tile), lambda step: (row, step + column // tile))
+
+    return pl.pallas_call(
+        weight_grad_kernel,
+        grid=(count // tile,),
+        out_shape=jax.ShapeDtypeStruct((width, count), BF),
+        in_specs=[
+            pl.BlockSpec((tokens, width), lambda step: (0, at)),
+            pl.BlockSpec((tokens, tile), lambda step: (0, step)),
+        ]
+        + [add_spec(row, column) for _, row, column in adds],
+        out_specs=pl.BlockSpec((width, tile), lambda step: (0, step)),
+        compiler_params=pltpu.CompilerParams(vmem_limit_bytes=40 * 2**20),
+        cost_estimate=takes(1),
+        name="weight_grad",
+    )(left, right, *[array for array, _, _ in adds])
+
+
+def input_back_kernel(grad_ref, w_ref, x_ref, scale_ref, out_ref, gain_ref):
+    grad = dot(grad_ref[...], w_ref[...], NT)
+    out_ref[...] = grad.astype(BF)
+    unit = x_ref[...].astype(F32) * scale_ref[:, :1]
+    gain_ref[...] = jnp.sum(grad * unit, axis=0, keepdims=True)
+
+
+def input_back(grad, w, x, scale):
+    tokens, count = grad.shape
+    tile = 512
+    shape = jax.ShapeDtypeStruct
+    return pl.pallas_call(
+        input_back_kernel,
+        grid=(D // tile,),
+        out_shape=(shape((tokens, D), BF), shape((1, D), F32)),
+        in_specs=[
+            whole_block(tokens, count),
+            pl.BlockSpec((tile, count), lambda step: (step, 0)),
+            pl.BlockSpec((tokens, tile), lambda step: (0, step)),
+            whole_block(tokens, 128),
+        ],
+        out_specs=[
+            pl.BlockSpec((tokens, tile), lambda step: (0, step)), pl.BlockSpec((1, tile), lambda step: (0, step)),
+        ],
+        compiler_params=pltpu.CompilerParams(vmem_limit_bytes=48 * 2**20),
+        cost_estimate=takes(1),
+        name="input_back",
+    )(grad, w, x, scale)
+
+
+def project_kernel(x_ref, w_ref, normed_ref, p_ref, gains_ref, scale_ref, gain):
+    @pl.when(pl.program_id(0) == 0)
+    def _():
+        row = lax.broadcasted_iota(jnp.int32, (8, EXTRA), 0)
+        col = lax.broadcasted_iota(jnp.int32, (8, EXTRA), 1)
+        pick = (col == row + 2 * H).astype(BF)
+        gain[...] = dot(pick, w_ref[:, MIXW - EXTRA :], NT)
+        gains_ref[...] = gain[...]
+
+    x = x_ref[...].astype(F32)
+    scale = norm_scale(x, EPS_NORM)
+    scale_ref[...] = jnp.broadcast_to(scale, scale_ref.shape)
+    normed = (x * scale * gain[:1]).astype(BF)
+    normed_ref[...] = normed
+    p_ref[...] = dot(normed, w_ref[...], NN)
+
+
+def project(x, w):
+    count = x.shape[0]
+    rows = 256
+    shape = jax.ShapeDtypeStruct
+    return pl.pallas_call(
+        project_kernel,
+        grid=(count // rows,),
+        out_shape=(shape((count, D), BF), shape((count, MIXW), F32), shape((8, D), F32), shape((count, 128), F32)),
+        in_specs=[by_sequence(rows, D), whole_block(D, MIXW)],
+        out_specs=[by_sequence(rows, D), by_sequence(rows, MIXW), whole_block(8, D), by_sequence(rows, 128)],
+        scratch_shapes=[pltpu.VMEM((8, D), F32)],
+        compiler_params=pltpu.CompilerParams(vmem_limit_bytes=40 * 2**20),
+        cost_estimate=takes(1),
+        name="project",
+    )(x, w)
+
+
+def finish_kernel(copies, at_ref, hidden_ref, feed_ref, grad_ref, x_ref, d_hidden_ref, gain_ref, out_ref, in_grad_ref):
+    out = (hidden_ref[...] + feed_ref[...].astype(F32)).astype(BF)
+    back, _ = norm_back(grad_ref[...].astype(F32), x_ref[...].astype(F32), gain_ref[...], EPS_NORM)
+    in_grad = (d_hidden_ref[...] + back).astype(BF)
+    width = D // (4 * copies)
+    for core in range(2):
+        for copy in range(copies):
+            for x in range(2):
+                block = (x * 2 + (at_ref[0] + core) % 2) * copies + (at_ref[1] + copy) % copies
+                to = pl.ds(pl.multiple_of(block * width, 128), width)
+                at = ((core * copies + copy) * 2 + x) * width
+                out_ref[:, to] = out[:, at : at + width]
+                in_grad_ref[:, to] = in_grad[:, at : at + width]
+
+
+def finish(place, copies, hidden, feed, grad, x, d_hidden, gain):
+    shape = jax.ShapeDtypeStruct(x.shape, BF)
+    return pl.pallas_call(
+        functools.partial(finish_kernel, copies),
+        out_shape=(shape, shape),
+        in_specs=[smem_spec()] + [vmem_spec()] * 6,
+        out_specs=[vmem_spec()] * 2,
+        compiler_params=pltpu.CompilerParams(vmem_limit_bytes=40 * 2**20),
+        cost_estimate=takes(1),
+        name="finish",
+    )(place, hidden, feed, grad, x, d_hidden, gain)
 
 
 def turn(blocks, shift, axis):
@@ -865,10 +1121,6 @@
         whole = jnp.moveaxis(whole, axis + 2, axis)
         whole = turn(turn(whole, 2 - self.core, axis + 1), self.copies - self.dp, axis + 2)
         return whole.reshape(values.shape)
-
-
-def dot(left, right, axes):
-    return lax.dot_general(left, right, (axes, ((), ())), preferred_element_type=F32)
 
 
 def on_device(inputs, cotangent, segment_ids, weights, master, moment_one, moment_two,
@@ -896,52 +1148,54 @@
         pairs_to(lambda r, g, shift=shift: ((r + 4 * shift) % replicas) * 4 + g) for shift in range(1, copies)
     ]
 
-    x = order.relative(inputs, 1)
-    dy = order.relative(cotangent, 1)
+    in_place = (D // (4 * copies)) % 128 == 0
+    x, dy = (inputs, cotangent) if in_place else (order.relative(inputs, 1), order.relative(cotangent, 1))
     seg = jnp.broadcast_to(segment_ids[None, :], (8, tokens))
-    mix_blocks, out_block, gate_block, down_block, x_all, seg_all = spread(copies, weights, x, seg)
+    mix_blocks, out_block, gate_block, down_block, x_all, seg_all, x, dy = spread(copies, weights, x, dy, seg)
+    cubes = [
+        [(copy * 4 + j % 4) * 4 + (j // 4) * 2 + side for j in range(RANKS)]
+        for copy in range(copies)
+        for side in range(2)
+    ]
+    dy_all = lax.all_gather(dy, axes, axis_index_groups=cubes, axis=0, tiled=True)
     x_all = x_all.reshape(group_tokens, D)
     w_mix = mix_blocks.reshape(D, MIXW)
 
-    def collect(block):
-        block = block.reshape(block_rows, block.shape[2])
-        mine = [block]
-        for shift in range(1, copies):
-            mine.append(lax.ppermute(block, axes, copy_pairs[copies - shift - 1]))
-        theirs = [lax.ppermute(one, axes, core_pairs) for one in mine]
+    def from_copies(blocks):
+        block = blocks[0].reshape(block_rows, blocks.shape[3])
+        return [lax.ppermute(block, axes, copy_pairs[copies - shift - 1]) for shift in range(1, copies)]
+
+    def collect(blocks, landed):
+        mine = [blocks[0].reshape(block_rows, blocks.shape[3])] + landed
+        theirs = [blocks[1].reshape(block_rows, blocks.shape[3])]
+        theirs = theirs + [lax.ppermute(one, axes, core_pairs) for one in landed]
         return jnp.concatenate(mine + theirs, axis=0)
 
-    w_out = collect(out_block)
-    w_gates = collect(gate_block)
-    w_down = collect(down_block)
-
-    pieces = [dy]
-    for mask in range(1, RANKS):
-        def to_rank(r, g, mask=mask):
-            there = ((g // 2) * 4 + r % 4) ^ mask
-            return ((r // 4) * 4 + there % 4) * 4 + (there // 4) * 2 + g % 2
-        pieces.append(lax.ppermute(dy, axes, pairs_to(to_rank)))
-    dy_all = jnp.zeros((RANKS, tokens, D), BF)
-    for mask in range(RANKS):
-        there = ((rank // 4) ^ (mask // 4)) * 4 + ((rank // 2 % 2) ^ (mask // 2 % 2)) * 2 + ((rank % 2) ^ (mask % 2))
-        dy_all = lax.dynamic_update_slice(dy_all, pieces[mask][None], (there, 0, 0))
-    dy_all = dy_all.reshape(group_tokens, D)
-
-    extra_rel = w_mix[:, MIXW - EXTRA :]
-    gain_one = extra_rel[:, 2 * H].astype(F32)[None]
-    gain_two = extra_rel[:, 2 * H + 1].astype(F32)[None]
-    extra = order.plain(extra_rel, 0).astype(F32)
+    together = lax.optimization_barrier
+    out_landed = from_copies(out_block)
+    gate_landed = from_copies(gate_block)
+    down_landed = from_copies(down_block)
+    normed, p, gains, x_scale = project(x_all, w_mix)
+    gain_one, gain_two = gains[:1], gains[1:2]
+    extra = order.plain(w_mix[:, MIXW - EXTRA :], 0).astype(F32)
     conv_cols = CONV * (2 * KD + VD) // D
-    kernel = extra[:, 2 * H + 2 : 2 * H + 2 + conv_cols].reshape(CONV, 2 * KD + VD)
+    conv_at = 2 * H + 2
+
+    tap_rows = D // CONV
+    table = extra[:, conv_at : conv_at + conv_cols].reshape(CONV, tap_rows, conv_cols)
+    ranges = ((0, QW), (KD, QW), (2 * KD, VW))
+
+    def own_channels(first, width):
+        return first // conv_cols + rank * (width // conv_cols), width // conv_cols
+
     taps = jnp.concatenate(
         [
-            lax.dynamic_slice_in_dim(kernel, rank * QW, QW, 1),
-            lax.dynamic_slice_in_dim(kernel, KD + rank * QW, QW, 1),
-            lax.dynamic_slice_in_dim(kernel, 2 * KD + rank * VW, VW, 1),
+            lax.dynamic_slice_in_dim(table, *own_channels(first, width), 1).reshape(CONV, width)
+            for first, width in ranges
         ],
         axis=1,
     )
-    column = extra[:, 2 * H + 2 + conv_cols]
+    column = extra[: 2 * H + DV, conv_at + conv_cols]
     scalars = jnp.concatenate(
         [
             jnp.exp(lax.dynamic_slice_in_dim(column, rank * HEADS, HEADS, 0)),
@@ -950,105 +1204,165 @@
     )
     out_gain = column[2 * H : 2 * H + DV][None]
     rank_arg = jnp.reshape(rank, (1,)).astype(jnp.int32)
-
-    tokens_all = x_all.astype(F32)
-    normed = (tokens_all * norm_scale(tokens_all, EPS_NORM) * gain_one).astype(BF)
-    p = dot(normed, w_mix, NN)
     gated, inverse, update = mixer(rank_arg, scalars, seg_all, p, taps, out_gain, tokens)
+    w_out = collect(out_block, out_landed)
     partial = dot(gated, w_out, NT).astype(BF)
     hidden, normed_two = branch(copies, partial.reshape(RANKS, tokens, D), x, gain_two)
     normed_two = normed_two.reshape(group_tokens, D)
-
+    normed_two, gate_landed, down_landed = together((normed_two, gate_landed, down_landed))
+    w_gates = collect(gate_block, gate_landed)
+    w_down = collect(down_block, down_landed)
     gate_up = dot(normed_two, w_gates, NN)
     gate_part, up_part = gate_up[:, :FW], gate_up[:, FW:]
     tile_count = jnp.where(rank < FULL_RANKS, FT, FT - 1)
     real = (jnp.arange(FW) < tile_count * 128)[None]
     sigmoid_gate = jax.nn.sigmoid(gate_part)
     activated = jnp.where(real, gate_part * sigmoid_gate * up_part, 0.0).astype(BF)
+    half = copies * block_rows
+
+    def block_of(values, at):
+        return values[:, at * block_rows : (at + 1) * block_rows]
+
+    def first_half(left, right):
+        theirs = dot(left[:, half:], right, TN).astype(BF)
+        return theirs, lax.ppermute(theirs, axes, core_pairs)
+
+    def away_rows(left, right, got):
+        return [
+            (dot(block_of(left, at), right, TN) + got[at * block_rows : (at + 1) * block_rows].astype(F32)).astype(BF)
+            for at in range(1, copies)
+        ]
+
+    def to_copies(away):
+        return [lax.ppermute(one, axes, pairs) for one, pairs in zip(away, copy_pairs)]
+
+    def for_copies(left, right, got):
+        away = away_rows(left, right, got)
+        return away, to_copies(away)
+
+    down_half, down_got = first_half(dy_all, activated)
+    down_half, activated = together((down_half, activated))
     feed = dot(activated, w_down, NT).astype(BF)
     d_act = dot(dy_all, w_down, NN)
     d_gate = d_act * up_part * sigmoid_gate * (1 + gate_part * (1 - sigmoid_gate))
     d_up = d_act * gate_part * sigmoid_gate
     real_two = jnp.concatenate([real, real], axis=1)
     d_gate_up = jnp.where(real_two, jnp.concatenate([d_gate, d_up], axis=1), 0.0).astype(BF)
+    gate_half, gate_got = first_half(normed_two, d_gate_up)
+    down_away, down_landed = for_copies(dy_all, activated, down_got)
+    gate_half, down_away, d_gate_up = together((gate_half, down_away, d_gate_up))
     d_normed_two = dot(d_gate_up, w_gates, NT).astype(BF)
+    d_gate_part, d_up_part = d_gate_up[:, :FW], d_gate_up[:, FW:]
+    gate_away = away_rows(normed_two, d_gate_part, gate_got[:, :FW])
+    up_away = away_rows(normed_two, d_up_part, gate_got[:, FW:])
+    gate_away, up_away, d_normed_two = together((gate_away, up_away, d_normed_two))
     d_hidden, gain_two_grad, d_hidden_all = hidden_back(
         copies, d_normed_two.reshape(RANKS, tokens, D), hidden, dy, gain_two
     )
     d_hidden_all = d_hidden_all.reshape(group_tokens, D)
+    d_hidden_all, up_away, gate_away, down_landed, feed = together((d_hidden_all, up_away, gate_away, down_landed, feed))
+    feed = lax.psum_scatter(feed, axes, axis_index_groups=cubes, scatter_dimension=0, tiled=True)
+    up_landed = to_copies(up_away)
+    gate_landed = to_copies(gate_away)
+    out_half, out_got = first_half(d_hidden_all, gated)
+    out_half, d_hidden_all = together((out_half, d_hidden_all))
     d_gated = dot(d_hidden_all, w_out, NN)
+    out_away = away_rows(d_hidden_all, gated, out_got)
+    out_away, d_gated = together((out_away, d_gated))
+    out_landed = to_copies(out_away)
     d_mix, d_taps, d_out_gain, d_scalars = mixer_back(
         rank_arg, scalars, seg_all, p, taps, out_gain, inverse, update, d_gated, tokens
     )
-    d_normed = dot(d_mix, w_mix, NT).astype(BF)
-    out_rel, in_grad_rel, gain_one_grad = ends(
-        copies, d_normed.reshape(RANKS, tokens, D), feed.reshape(RANKS, tokens, D), hidden, d_hidden, x, gain_one
+    d_mix, up_landed = together((d_mix, up_landed))
+    d_wide = d_mix[:, : MIXW - EXTRA]
+    mix_half = weight_grad(normed, d_wide, 1, half)
+    mix_got = lax.ppermute(mix_half, axes, core_pairs)
+    mix_half, d_mix = together((mix_half, d_mix))
+    d_normed, gain_one_grad = input_back(d_mix, w_mix, x_all, x_scale)
+    gain_one_grad = gain_one_grad[0]
+    d_normed, gain_one_grad, mix_got, gate_landed, out_landed = together(
+        (d_normed, gain_one_grad, mix_got, gate_landed, out_landed)
     )
-    output = order.plain(out_rel, 1)
-    input_grad = order.plain(in_grad_rel, 1)
-
-    def reduce_rows(left, right):
-        half = copies * block_rows
-        theirs = dot(left[:, half:], right, TN).astype(BF)
-        got = lax.ppermute(theirs, axes, core_pairs)
-        away = [
-            (dot(left[:, at * block_rows : (at + 1) * block_rows], right, TN)
-             + got[at * block_rows : (at + 1) * block_rows].astype(F32)).astype(BF)
-            for at in range(1, copies)
-        ]
-        total = dot(left[:, :block_rows], right, TN) + got[:block_rows].astype(F32)
-        for shift in range(1, copies):
-            total = total + lax.ppermute(away[shift - 1], axes, copy_pairs[shift - 1]).astype(F32)
-        return total.astype(BF).reshape(RANKS, rows, right.shape[1])
-
-    down_rows = reduce_rows(dy_all, activated)
-    gate_rows = reduce_rows(normed_two, d_gate_up)
-    out_rows = reduce_rows(d_hidden_all, gated)
-    mix_rows = reduce_rows(normed, d_mix)
-    grads_rest = home(copies, 5, (1, 2, 3), (out_rows, gate_rows, down_rows))
-    grads_mix = home(copies, 6, (0,), (mix_rows,))
-
-    pair_grad = dot(normed, d_mix[:, MIXW - EXTRA :], TN)
-    lanes = jnp.arange(EXTRA)[None]
-    rel_grad = (
-        pair_grad
-        + jnp.where(lanes == 2 * H, gain_one_grad.reshape(D, 1), 0.0)
-        + jnp.where(lanes == 2 * H + 1, gain_two_grad.reshape(D, 1), 0.0)
+    mix_away = [
+        weight_grad(normed, d_wide, at, block_rows, ((mix_got, at, 0),)) for at in range(1, copies)
+    ]
+    mix_landed = to_copies(mix_away)
+    d_input = lax.psum_scatter(d_normed, axes, axis_index_groups=cubes, scatter_dimension=0, tiled=True)
+    mix_away, d_gate_part, d_up_part, activated, gated = together(
+        (mix_away, d_gate_part, d_up_part, activated, gated)
     )
-    tap_grad = jnp.zeros((CONV, 2 * KD + VD), F32)
-    tap_grad = lax.dynamic_update_slice(tap_grad, d_taps[:, :QW], (0, rank * QW))
-    tap_grad = lax.dynamic_update_slice(tap_grad, d_taps[:, QW : 2 * QW], (0, KD + rank * QW))
-    tap_grad = lax.dynamic_update_slice(tap_grad, d_taps[:, 2 * QW :], (0, 2 * KD + rank * VW))
+
+    def own_rows(left, right, got, column, landed):
+        total = weight_grad(left, right, 0, block_rows, ((got, 0, column),) + tuple((one, 0, 0) for one in landed))
+        return total.reshape(RANKS, rows, right.shape[1])
+
+    up_rows = own_rows(normed_two, d_up_part, gate_got, FW, up_landed)
+    gate_rows = own_rows(normed_two, d_gate_part, gate_got, 0, gate_landed)
+    down_rows = own_rows(dy_all, activated, down_got, 0, down_landed)
+    out_rows = own_rows(d_hidden_all, gated, out_got, 0, out_landed)
+    out_rows, d_taps, d_scalars, d_out_gain, gain_two_grad = together(
+        (out_rows, d_taps, d_scalars, d_out_gain, gain_two_grad)
+    )
+    tap_grad = jnp.zeros((CONV, tap_rows, conv_cols), F32)
+    at = 0
+    for first, width in ranges:
+        start, count = own_channels(first, width)
+        piece = d_taps[:, at : at + width].reshape(CONV, count, conv_cols)
+        tap_grad = lax.dynamic_update_slice(tap_grad, piece, (0, start, 0))
+        at = at + width
     small = jnp.zeros((D,), F32)
     small = lax.dynamic_update_slice(small, d_scalars[0, :HEADS], (rank * HEADS,))
     small = lax.dynamic_update_slice(small, d_scalars[0, HEADS : 2 * HEADS], (H + rank * HEADS,))
     small = lax.dynamic_update_slice(small, d_out_gain[0], (2 * H,))
     core_grad = jnp.concatenate(
         [
-            jnp.zeros((D, 2 * H + 2), F32),
+            jnp.zeros((D, conv_at), F32),
             tap_grad.reshape(D, conv_cols),
             small[:, None],
-            jnp.zeros((D, EXTRA - 2 * H - 3 - conv_cols), F32),
+            jnp.zeros((D, EXTRA - conv_at - 1 - conv_cols), F32),
         ],
         axis=1,
     )
-    extra_grad = order.plain(rel_grad, 0) + core_grad
-    extra_grad = jnp.swapaxes(extra_grad.reshape(4, replicas, rows, EXTRA), 0, 1).reshape(D, EXTRA)
-    extra_rows = lax.psum_scatter(extra_grad, axes, scatter_dimension=0, tiled=True)
-
-    grads = jnp.concatenate([grads_mix.astype(F32), grads_rest.astype(F32), extra_rows], axis=1)
+    lanes = jnp.arange(EXTRA)[None]
+    extra_grad = (
+        dot(normed, d_mix[:, MIXW - EXTRA :], TN)
+        + jnp.where(lanes == 2 * H, gain_one_grad[:, None], 0.0)
+        + jnp.where(lanes == 2 * H + 1, gain_two_grad.reshape(D, 1), 0.0)
+        + order.relative(core_grad, 0)
+    )
+    extra_got = lax.ppermute(extra_grad[half:], axes, core_pairs)
+    extra_sum = extra_grad[:half] + extra_got
+    extra_landed = [
+        lax.ppermute(extra_sum[at * block_rows : (at + 1) * block_rows], axes, pairs)
+        for at, pairs in zip(range(1, copies), copy_pairs)
+    ]
+    extra_sum, out_rows = together((extra_sum, out_rows))
+    grads_rest = home_rest(copies, (out_rows, gate_rows, up_rows, down_rows))
+    if in_place:
+        output, input_grad = finish(
+            jnp.stack([core, dp]).astype(jnp.int32), copies, hidden, feed, d_input, x, d_hidden, gain_one
+        )
+    else:
+        output = order.plain((hidden + feed.astype(F32)).astype(BF), 1)
+        back, _ = norm_back(d_input.astype(F32), x.astype(F32), gain_one, EPS_NORM)
+        input_grad = order.plain((d_hidden + back).astype(BF), 1)
+    extra_rows = extra_sum[:block_rows]
+    for one in extra_landed:
+        extra_rows = extra_rows + one
+    step_float = step[0].astype(F32)
+    adam_scalars = jnp.stack(
+        [beta_one[0], beta_two[0], learn_rate[0], 1 - beta_one[0] ** step_float, 1 - beta_two[0] ** step_float]
+    )
+    state = (moment_one, moment_two, master)
+    done = adam(adam_scalars, grads_rest, state, None, MIX_END, 2048, 4)
+    done = adam(adam_scalars, grads_rest, state, done, MIX_END + 4 * 2048, 2560, 5)
+    done, extra_rows, output, input_grad, normed = together((done, extra_rows, output, input_grad, normed))
+    mix_rows = own_rows(normed, d_wide, mix_got, 0, mix_landed)
+    grads_mix, extra_rows = home(copies, mix_rows, extra_rows.reshape(RANKS, rows, EXTRA))
+    done = adam(adam_scalars, extra_rows, state, done, EXTRA_START, EXTRA, 1)
+    done = adam(adam_scalars, grads_mix, state, done, 0, 2048, 6)
     gain_grads = extra_rows[:, 2 * H : 2 * H + 2]
-    step_size = learn_rate[0]
-    first_beta = beta_one[0]
-    second_beta = beta_two[0]
-    step_float = step[0].astype(F32)
-    moment_one_new = first_beta * moment_one + (1 - first_beta) * grads
-    moment_two_new = second_beta * moment_two + (1 - second_beta) * grads * grads
-    first_hat = moment_one_new / (1 - first_beta**step_float)
-    second_hat = moment_two_new / (1 - second_beta**step_float)
-    master_new = master - step_size * (first_hat / (jnp.sqrt(second_hat) + EPS_ADAM) + DECAY_WEIGHT * master)
-    return (output, input_grad, grads, moment_one_new, moment_two_new, master_new,
-            master_new.astype(BF), gain_grads)
+    return (output, input_grad) + tuple(done) + (gain_grads,)
 
 
 def solution(mesh):

time: 1100 us -> 804 us (0.73)
  waiting for transfers between devices: 244 us -> 50.6 us
  other arithmetic: 74.7 us -> 7.26 us
  matrix products: 118 us -> 73.9 us
  local copies, waits for them, and re-layouts: 47.1 us -> 79.5 us
  Pallas kernels: 558 us -> 539 us
    ppermute x24 -> x17, waiting for transfers between devices: 196 us -> 50.5 us  [the longest x5 44.9 us: to_copies(): lax.ppermute(one, axes, pairs)]
    convert_element_type x11 -> x1, other arithmetic: 50.6 us -> 0.24 us  [on_device(): extra = order.plain(w_mix[:, MIXW - EXTRA:], 0).astype(F32)]
    unnamed x89 -> x165, local copies, waits for them, and re-layouts: 5.86 us -> 55.6 us
    pallas_call x4 -> x17, Pallas kernels: 226 us -> 275 us  [the longest x1 101 us: branch(): pl.pallas_call(functools.partial(branch_kernel, copies, row_parts(tokens,...]
    reduce_scatter x1 -> x2, waiting for transfers between devices: 48.3 us -> 0.01 us  [the longest x1 0.01 us: on_device(): lax.psum_scatter(feed, axes, axis_index_groups=cubes, scatter_dimension=0...]
    dot_general x21 -> x14, matrix products: 118 us -> 73.9 us  [dot(): lax.dot_general(left, right, (axes, ((), ())), preferred_element_type=F32)]
    pallas_call x1, Pallas kernels: 62.2 us -> 29.1 us  [mixer(): pl.pallas_call(mixer_kernel, grid=(count,), out_shape=(shape((p.shape[0],...]
    pallas_call x1, Pallas kernels: 155 us -> 124 us  [spread(): pl.pallas_call(functools.partial(spread_kernel, copies, ((0, tokens // 2)...]
  transfers between devices with their start and end apart: 25 -> 20, of which waited for: 7 -> 4; matrix products, arithmetic and copies ran while one was open for 14% -> 13% of each run, Pallas kernels for 38% -> 47%
where the time goes in v2:
time: 804 us; the launch traced here: 795 us
  Pallas kernels  539 us (67%)
  local copies, waits for them, and re-layouts  79.5 us (10%)
  matrix products  73.9 us (9%)
  waiting for transfers between devices  50.6 us (6%)
  starting transfers between devices  27.5 us (3%)
  between operations  17.9 us (2%)
    pallas_call x1, Pallas kernels, spread(): pl.pallas_call(functools.partial(spread_kernel, copies, ((0, tokens // 2)...  124 us
    pallas_call x1, Pallas kernels, branch(): pl.pallas_call(functools.partial(branch_kernel, copies, row_parts(tokens,...  101 us
    pallas_call x1, Pallas kernels, hidden_back(): pl.pallas_call(functools.partial(hidden_back_kernel, copies, row_parts(to...  78.9 us
    dot_general x14, matrix products, dot(): lax.dot_general(left, right, (axes, ((), ())), preferred_element_type=F32)  73.9 us
    pallas_call x1, Pallas kernels, home_rest(): pl.pallas_call(functools.partial(home_rest_kernel, copies), out_shape=jax...  72.4 us
    unnamed x165, local copies, waits for them, and re-layouts  55.6 us
    ppermute x5, waiting for transfers between devices, to_copies(): lax.ppermute(one, axes, pairs)  44.9 us
    pallas_call x1, Pallas kernels, mixer_back(): pl.pallas_call(mixer_back_kernel, grid=(count,), out_shape=(shape((p.shap...  31.8 us
  transfers between devices with their start and end apart: 20, of which 4 were waited for; matrix products, arithmetic and copies ran while one was open for 13% of the time, Pallas kernels for 47%

profile of v2, /device:TPU:0, one launch (start us, length us, event | category | flops | bytes accessed | tf_op | source)
XLA Modules:
  0.0 795.4 jit_solution(8499009503677003601)
XLA Ops:
  8.5 124.1 %spread.1 = (bf16[2,2,8,64,1664]{4,3,2,1,0:T(8,128)(2,1)}, bf16[2,8,64,512]{3,2,1,0:T(8,128)(2,1)}, bf16[2,8,64,1536]{3,2,1,0:T(8,128)(2,1)}, bf16[2,8,64,768]{3...) custom-call(bf16[64,33408]{1,0:T(8,128)(2,1)} %w_ref.1, ...), custom_call_target="tpu_custom_call" | custom-call | bytes 5000 | tf_op jit(solution)/shard_map/spread/pallas_call | solution.py:417
  132.6 2.4 fusion.50
  135.0 16.3 %collective-permute-start = (bf16[512,512]{1,0:T(8,128)(2,1)}, bf16[512,512]{1,0:T(8,128)(2,1)}, u32[]{:S(2)}, u32[]{:S(2)}) collective-permute-start(bf16[512,512]{1,0:T(8,128)(2,1)} %bitcast.9), channel_id=1, source_target_pairs={{0,16},{1,17},{2,18},{3,19},{4,20},{5,21},{6,22},{7,23},{8,24},{9,... | collective-permute-start | bytes 1572872 | tf_op jit(solution)/shard_map/ppermute | solution.py:1166
  151.3 2.7 fusion.49
  155.9 2.9 collective-permute-start.2
  162.7 2.2 copy-done.9
  164.9 13.8 %project.1 = (bf16[1024,2048]{1,0:T(8,128)(2,1)S(1)}, f32[1024,1664]{1,0:T(8,128)}, f32[8,2048]{1,0:T(8,128)S(1)}, f32[1024,128]{1,0:T(8,128)S(1)}) custom-call(bf16[1024,2048]{1,0:T(8,128)(2,1)S(1)} %bitcast.62, bf16[2048,1664]{1,0:T(8,128)(2,1)} %bitcast.81), custom_call_target="tpu_custom_call" | custom-call | bytes 1000 | tf_op jit(solution)/shard_map/project/pallas_call | solution.py:1060
  181.7 3.0 copy-done.8
  184.7 29.1 %mixer.1 = (bf16[1024,512]{1,0:T(8,128)(2,1)S(1)}, f32[8,2,128,128]{3,2,1,0:T(8,128)S(1)}, f32[8,2,128,256]{3,2,1,0:T(8,128)S(1)}) custom-call(s32[1]{0:T(128)} %bitcast.2.rank_ref, f32[4]{0:T(128)S(1)} %pad_maximum_fusion.9.scalars, s32[8,8,128]{2,1,0:T(8,128)S(1)} %copy-done.58, f32[1024,1664]{1,0:T(8,128)S(1)} %copy-done.8, ...), custom_call_target="tpu_custom_call" | custom-call | bytes 5000 | tf_op jit(solution)/shard_map/mixer/pallas_call | solution.py:895
  214.5 6.4 convolution_convert_fusion.1
  220.9 100.5 %branch.1 = (f32[128,2048]{1,0:T(8,128)}, bf16[8,128,2048]{2,1,0:T(8,128)(2,1)}) custom-call(bf16[8,128,2048]{2,1,0:T(8,128)(2,1)} %bitcast.83, bf16[128,2048]{1,0:T(8,128)(2,1)} %get-tuple-element.111.x_ref, f32[1,2048]{1,0:T(1,128)} %get-tuple-element.225.gain_ref), custom_call_target="tpu_custom_call" | custom-call | bytes 5000 | tf_op jit(solution)/shard_map/branch/pallas_call | solution.py:495
  322.2 3.7 collective-permute-done.5
  325.9 10.3 %fusion.12 = f32[1024,1536]{1,0:T(8,128)S(1)} fusion(bf16[1024,2048]{1,0:T(8,128)(2,1)} %bitcast.63, bf16[512,1536]{1,0:T(8,128)(2,1)S(1)} %collective-permute-done.5, bf16[512,1536]{1,0:T(8,128)(2,1)S(1)} %bitcast.86, bf16[512,1536]{1,0:T(8,128)(2,1)} %collective-permute-done.2, bf16[512,1536]{1,0:T(8,128)(2,1)} %bitcast.13), kind=kOutput, calls=%fused_computation.33 | convolution fusion | flops 6467616768 | bytes 16777216 | tf_op jit(solution)/shard_map/dot_general | solution.py:675
  336.3 2.7 copy-done.62
  340.0 5.2 fusion.6
  345.3 8.2 %add_multiply_fusion = (bf16[1024,768]{1,0:T(8,128)(2,1)S(1)}, bf16[1024,768]{1,0:T(8,128)(2,1)S(1)}) fusion(f32[1024,1536]{1,0:T(8,128)} %copy-done.62, bf16[1024,2048]{1,0:T(8,128)(2,1)S(1)} %copy-done.27, bf16[512,768]{1,0:T(8,128)(2,1)} %collective-permute-done.4, bf16[512,768]{1,0:T(8,128)(2,1)S(1)} %bitcast.91, ...), kind=kOutput, calls=%fused_computation.10 | convolution fusion | flops 3244032000 | bytes 16777216 | tf_op jit(solution)/shard_map/dot_general | solution.py:675
  355.8 4.9 convolution_convert_fusion.3
  361.0 7.1 convolution_convert_fusion.2
  368.1 3.1 add_convert_fusion.2
  371.3 12.1 %convolution_convert_fusion = bf16[1024,2048]{1,0:T(8,128)(2,1)} fusion(bf16[1024,1536]{1,0:T(8,128)(2,1)} %copy-done.60, bf16[512,1536]{1,0:T(8,128)(2,1)} %copy-done.72, bf16[512,1536]{1,0:T(8,128)(2,1)S(1)} %bitcast.87, bf16[512,1536]{1,0:T(8,128)(2,1)} %collective-permute-done.2, bf16[512,1536]{1,0:T(8,128)(2,1)} %bitcast.13), kind=kOutput, calls=%fused_computation.3 | convolution fusion | flops 6469713920 | bytes 13631488 | tf_op jit(solution)/shard_map/dot_general | solution.py:675
  383.5 4.6 add_convert_fusion
  390.0 78.9 %hidden_back.1 = (f32[128,2048]{1,0:T(8,128)}, f32[1,2048]{1,0:T(1,128)}, bf16[8,128,2048]{2,1,0:T(8,128)(2,1)}) custom-call(bf16[8,128,2048]{2,1,0:T(8,128)(2,1)} %bitcast.84, f32[128,2048]{1,0:T(8,128)} %get-tuple-element.123.h_ref.hidden_ref, bf16[128,2048]{1,0:T(8,128)(2,1)} %get-tuple-element.117.dy_ref, f32[1,2048]{1,0:T(1,128)} %get-tuple-element.225.gain_ref), custom_call_target="tpu_custom_call" | custom-call | bytes 5000 | tf_op jit(solution)/shard_map/hidden_back/pallas_call | solution.py:538
  470.4 3.0 fusion.9
  474.0 3.6 fusion.31.dz_ref
  479.8 31.8 %mixer_back.1 = (bf16[1024,1664]{1,0:T(8,128)(2,1)S(1)}, f32[4,1024]{1,0:T(4,128)S(1)}, f32[1,256]{1,0:T(1,128)S(1)}, f32[8,128]{1,0:T(8,128)S(1)}) custom-call(s32[1]{0:T(128)} %bitcast.2.rank_ref, f32[4]{0:T(128)S(1)} %pad_maximum_fusion.9.scalars, s32[8,8,128]{2,1,0:T(8,128)S(1)} %copy-done.58, f32[1024,1664]{1,0:T(8,128)} %get-tuple-element.106.p_ref, ...), custom_call_target="tpu_custom_call" | custom-call | bytes 5000 | tf_op jit(solution)/shard_map/mixer_back/pallas_call | solution.py:919
  512.6 2.8 copy-done.4
  515.4 4.3 weight_grad.7
  519.9 2.5 collective-permute-start.12
  522.9 11.3 %input_back.1 = (bf16[1024,2048]{1,0:T(8,128)(2,1)}, f32[1,2048]{1,0:T(1,128)S(1)}) custom-call(bf16[1024,1664]{1,0:T(8,128)(2,1)S(1)} %get-tuple-element.133.grad_ref, bf16[2048,1664]{1,0:T(8,128)(2,1)} %bitcast.82, bf16[1024,2048]{1,0:T(8,128)(2,1)} %bitcast.61, f32[1024,128]{1,0:T(8,128)S(1)} %copy-done.55), custom_call_target="tpu_custom_call" | custom-call | bytes 1000 | tf_op jit(solution)/shard_map/input_back/pallas_call | solution.py:1020
  534.2 35.1 %collective-permute-done.12.refs_1_ = bf16[512,768]{1,0:T(8,128)(2,1)S(1)} collective-permute-done((bf16[512,768]{1,0:T(8,128)(2,1)S(1)}, bf16[512,768]{1,0:T(8,128)(2,1)S(1)}, u32[]{:S(2)}, u32[]{:S(2)}) %collective-permute-start.12) | collective-permute-done | bytes 786464 | tf_op jit(solution)/shard_map/ppermute | solution.py:1237
  570.2 9.8 %collective-permute-done.13.refs_1_ = bf16[512,512]{1,0:T(8,128)(2,1)S(1)} collective-permute-done((bf16[512,512]{1,0:T(8,128)(2,1)S(1)}, bf16[512,512]{1,0:T(8,128)(2,1)S(1)}, u32[]{:S(2)}, u32[]{:S(2)}) %collective-permute-start.13) | collective-permute-done | bytes 524320 | tf_op jit(solution)/shard_map/ppermute | solution.py:1237
  582.6 3.9 fusion.47
  588.4 3.5 weight_grad.8
  600.1 3.4 fusion.17
  603.7 2.7 bitcast_add_fusion
  609.4 2.9 collective-permute-start.15
  616.6 2.2 copy-done.28
  619.9 2.4 weight_grad.12
  628.8 72.4 %home_rest.1.grad_ref = bf16[64,33280]{1,0:T(8,128)(2,1)} custom-call(bf16[8,64,512]{2,1,0:T(8,128)(2,1)} %bitcast.77, bf16[8,64,768]{2,1,0:T(8,128)(2,1)} %bitcast.76, bf16[8,64,768]{2,1,0:T(8,128)(2,1)} %bitcast.75, bf16[8,64,768]{2,1,0:T(8,128)(2,1)} %bitcast.74), custom_call_target="tpu_custom_call" | custom-call | bytes 5000 | tf_op jit(solution)/shard_map/home_rest/pallas_call | solution.py:662
  701.3 3.4 copy-done
  704.7 2.2 copy-done.2
  706.9 6.9 adam.4
  713.8 9.8 %adam.5 = (f32[64,33408]{1,0:T(8,128)}, f32[64,33408]{1,0:T(8,128)}, f32[64,33408]{1,0:T(8,128)}, f32[64,33408]{1,0:T(8,128)}, bf16[64,33408]{1,0:T(8,128)(2,1)}) custom-call(f32[5]{0:T(128)S(1)} %stack.14.scalars, bf16[64,33280]{1,0:T(8,128)(2,1)S(1)} %copy-done.2, ...), custom_call_target="tpu_custom_call", output_to_operand_aliasing={{0}: (5, {}), {1}: (6, {}), {2}: (7, {}), {3}: (8, {}), {4}... | custom-call | bytes 5000 | tf_op jit(solution)/shard_map/adam/pallas_call | solution.py:965
  730.1 2.4 finish.1
  734.7 3.8 weight_grad.13
  739.6 29.6 %home.1 = (bf16[64,12288]{1,0:T(8,128)(2,1)}, f32[64,128]{1,0:T(8,128)}) custom-call(bf16[8,64,1536]{2,1,0:T(8,128)(2,1)} %bitcast.69, f32[8,64,128]{2,1,0:T(8,128)} %bitcast.90), custom_call_target="tpu_custom_call" | custom-call | bytes 5000 | tf_op jit(solution)/shard_map/home/pallas_call | solution.py:639
  770.7 3.4 copy-done.1
  778.8 9.6 %adam.7 = (f32[64,33408]{1,0:T(8,128)}, f32[64,33408]{1,0:T(8,128)}, f32[64,33408]{1,0:T(8,128)}, f32[64,33408]{1,0:T(8,128)}, bf16[64,33408]{1,0:T(8,128)(2,1)}) custom-call(f32[5]{0:T(128)S(1)} %stack.14.scalars, bf16[64,12288]{1,0:T(8,128)(2,1)S(1)} %copy-done.37, ...), custom_call_target="tpu_custom_call", output_to_operand_aliasing={{0}: (5, {}), {1}: (6, {}), {2}: (7, {}), {3}: (8, {}), {4}... | custom-call | bytes 5000 | tf_op jit(solution)/shard_map/adam/pallas_call | solution.py:965
  (260 shorter events, 64.6 us)
Async XLA Ops:
  7.2 332.8 %all-gather.2.cloned.1.call-start = ((), (), s32[]{:S(2)}) async-start(), calls=%async_computation.2 | async-start | bytes 4718592 | tf_op jit(solution)/shard_map/all_gather | solution.py:1160
  132.5 21.5 %copy-start.63 = (bf16[2,8,64,1536]{3,2,1,0:T(8,128)(2,1)S(1)}, bf16[2,8,64,1536]{3,2,1,0:T(8,128)(2,1)}, u32[]{:S(2)}) copy-start(bf16[2,8,64,1536]{3,2,1,0:T(8,128)(2,1)} %get-tuple-element.114) | copy-start | bytes 9437188
  132.6 591.8 %reduce-scatter.3.cloned.1.call-start = ((), (), s32[]{:S(2)}) async-start(), calls=%async_computation.3 | async-start | bytes 4718592 | tf_op jit(solution)/shard_map/reduce_scatter | solution.py:1264
  135.0 46.6 %collective-permute-start = (bf16[512,512]{1,0:T(8,128)(2,1)}, bf16[512,512]{1,0:T(8,128)(2,1)}, u32[]{:S(2)}, u32[]{:S(2)}) collective-permute-start(bf16[512,512]{1,0:T(8,128)(2,1)} %bitcast.9), channel_id=1, source_target_pairs={{0,16},{1,17},{2,18},{3,19},{4,20},{5,21},{6,22},{7,23},{8,24},{9,... | collective-permute-start | bytes 1572872 | tf_op jit(solution)/shard_map/ppermute | solution.py:1166
  154.0 167.5 %collective-permute-start.3 = (bf16[512,768]{1,0:T(8,128)(2,1)}, bf16[512,768]{1,0:T(8,128)(2,1)}, u32[]{:S(2)}, u32[]{:S(2)}) collective-permute-start(bf16[512,768]{1,0:T(8,128)(2,1)} %bitcast.14), channel_id=1, source_target_pairs={{0,16},{1,17},{2,18},{3,19},{4,20},{5,21},{6,22},{7,23},{8,24},{9,... | collective-permute-start | bytes 2359304 | tf_op jit(solution)/shard_map/ppermute | solution.py:1166
  155.9 165.5 %collective-permute-start.2 = (bf16[512,1536]{1,0:T(8,128)(2,1)}, bf16[512,1536]{1,0:T(8,128)(2,1)}, u32[]{:S(2)}, u32[]{:S(2)}) collective-permute-start(bf16[512,1536]{1,0:T(8,128)(2,1)} %bitcast.13), channel_id=1, source_target_pairs={{0,16},{1,17},{2,18},{3,19},{4,20},{5,21},{6,22},{7,23},{8,24},{9,... | collective-permute-start | bytes 4718600 | tf_op jit(solution)/shard_map/ppermute | solution.py:1166
  164.9 16.8 %copy-start.58 = (s32[8,8,128]{2,1,0:T(8,128)S(1)}, s32[8,8,128]{2,1,0:T(8,128)}, u32[]{:S(2)}) copy-start(s32[8,8,128]{2,1,0:T(8,128)} %get-tuple-element.105.seg_ref) | copy-start | bytes 98308
  181.6 32.9 %collective-permute-start.1 = (bf16[512,512]{1,0:T(8,128)(2,1)}, bf16[512,512]{1,0:T(8,128)(2,1)S(1)}, u32[]{:S(2)}, u32[]{:S(2)}) collective-permute-start(bf16[512,512]{1,0:T(8,128)(2,1)} %collective-permute-done), channel_id=1, source_target_pairs={{0,1},{1,0},{2,3},{3,2},{4,5},{5,4},{6,7},{7,6},{8,9},{9,8},{10,11... | collective-permute-start | bytes 1572872 | tf_op jit(solution)/shard_map/ppermute | solution.py:1171
  184.7 29.8 %copy-start.70 = (bf16[1,8,64,512]{3,2,1,0:T(8,128)(2,1)S(1)}, bf16[1,8,64,512]{3,2,1,0:T(8,128)(2,1)}, u32[]{:S(2)}) copy-start(bf16[1,8,64,512]{3,2,1,0:T(8,128)(2,1)} %get-tuple-element.220) | copy-start | bytes 1572868
  213.8 7.1 copy-start.34
  213.8 7.1 copy-start.38
  213.8 7.1 copy-start.43
  214.5 6.4 copy-start.75
  220.9 105.0 %copy-start.66 = (bf16[1,8,64,1536]{3,2,1,0:T(8,128)(2,1)S(1)}, bf16[1,8,64,1536]{3,2,1,0:T(8,128)(2,1)}, u32[]{:S(2)}) copy-start(bf16[1,8,64,1536]{3,2,1,0:T(8,128)(2,1)} %get-tuple-element.216) | copy-start | bytes 4718596
  321.5 4.4 collective-permute-start.5
  321.6 23.7 %collective-permute-start.4 = (bf16[512,768]{1,0:T(8,128)(2,1)}, bf16[512,768]{1,0:T(8,128)(2,1)}, u32[]{:S(2)}, u32[]{:S(2)}) collective-permute-start(bf16[512,768]{1,0:T(8,128)(2,1)} %collective-permute-done.3), channel_id=1, source_target_pairs={{0,1},{1,0},{2,3},{3,2},{4,5},{5,4},{6,7},{7,6},{8,9},{9,8},{10,11... | collective-permute-start | bytes 2359304 | tf_op jit(solution)/shard_map/ppermute | solution.py:1171
  325.9 10.3 %copy-start.72 = (bf16[512,1536]{1,0:T(8,128)(2,1)}, bf16[512,1536]{1,0:T(8,128)(2,1)S(1)}, u32[]{:S(2)}) copy-start(bf16[512,1536]{1,0:T(8,128)(2,1)S(1)} %collective-permute-done.5) | copy-start | bytes 4718596
  339.9 5.3 copy-start.22
  339.9 5.4 copy-start.68
  340.0 5.4 copy-start.27
  345.2 22.9 %collective-permute-start.6 = (bf16[1024,768]{1,0:T(8,128)(2,1)}, bf16[1024,768]{1,0:T(8,128)(2,1)}, u32[]{:S(2)}, u32[]{:S(2)}) collective-permute-start(bf16[1024,768]{1,0:T(8,128)(2,1)} %fusion.6), channel_id=1, source_target_pairs={{0,1},{1,0},{2,3},{3,2},{4,5},{5,4},{6,7},{7,6},{8,9},{9,8},{10,11... | collective-permute-start | bytes 4718600 | tf_op jit(solution)/shard_map/ppermute | solution.py:1228
  355.8 4.9 copy-start.60
  355.8 5.3 copy-start.23
  355.8 5.3 copy-start.69
  360.6 22.8 %collective-permute-start.7 = (bf16[1024,1536]{1,0:T(8,128)(2,1)}, bf16[1024,1536]{1,0:T(8,128)(2,1)S(1)}, u32[]{:S(2)}, u32[]{:S(2)}) collective-permute-start(bf16[1024,1536]{1,0:T(8,128)(2,1)} %convolution_convert_fusion.3), channel_id=1, source_target_pairs={{0,1},{1,0},{2,3},{3,2},{4,5},{5,4},{6,7},{7,6},{8,9},{9,8},{10,11... | collective-permute-start | bytes 9437192 | tf_op jit(solution)/shard_map/ppermute | solution.py:1228
  371.2 12.2 %copy-start.11 = (bf16[8,128,2048]{2,1,0:T(8,128)(2,1)S(1)}, bf16[8,128,2048]{2,1,0:T(8,128)(2,1)}, u32[]{:S(2)}) copy-start(bf16[8,128,2048]{2,1,0:T(8,128)(2,1)} %get-tuple-element.113) | copy-start | bytes 12582916
  371.2 97.6 %collective-permute-start.8 = (bf16[512,768]{1,0:T(8,128)(2,1)S(1)}, bf16[512,768]{1,0:T(8,128)(2,1)S(1)}, u32[]{:S(2)}, u32[]{:S(2)}) collective-permute-start(bf16[512,768]{1,0:T(8,128)(2,1)S(1)} %add_convert_fusion.2), channel_id=1, source_target_pairs={{0,16},{1,17},{2,18},{3,19},{4,20},{5,21},{6,22},{7,23},{8,24},{9,... | collective-permute-start | bytes 2359304 | tf_op jit(solution)/shard_map/ppermute | solution.py:1237
  383.5 4.6 copy-start.61
  383.5 4.6 copy-start.14
  469.8 4.2 copy-start.71
  469.8 4.2 copy-start.76
  469.8 254.6 %reduce-scatter.5.cloned.1.call-start = ((), (), s32[]{:S(2)}) async-start(), calls=%async_computation.4 | async-start | bytes 4718592 | tf_op jit(solution)/shard_map/reduce_scatter | solution.py:1290
  473.4 4.2 collective-permute-start.9
  473.5 38.2 %collective-permute-start.10 = (bf16[512,768]{1,0:T(8,128)(2,1)S(1)}, bf16[512,768]{1,0:T(8,128)(2,1)S(1)}, u32[]{:S(2)}, u32[]{:S(2)}) collective-permute-start(bf16[512,768]{1,0:T(8,128)(2,1)S(1)} %copy-done.74), channel_id=1, source_target_pairs={{0,16},{1,17},{2,18},{3,19},{4,20},{5,21},{6,22},{7,23},{8,24},{9,... | collective-permute-start | bytes 2359304 | tf_op jit(solution)/shard_map/ppermute | solution.py:1237
  511.6 11.2 %copy-start.13 = (bf16[1024,1664]{1,0:T(8,128)(2,1)}, bf16[1024,1664]{1,0:T(8,128)(2,1)S(1)}, u32[]{:S(2)}) copy-start(bf16[1024,1664]{1,0:T(8,128)(2,1)S(1)} %get-tuple-element.133.grad_ref) | copy-start | bytes 10223620
  515.4 4.6 copy-start.73
  515.4 7.5 copy-start.55
  519.7 61.0 %collective-permute-start.11 = (bf16[1024,1536]{1,0:T(8,128)(2,1)S(1)}, bf16[1024,1536]{1,0:T(8,128)(2,1)S(1)}, u32[]{:S(2)}, u32[]{:S(2)}) collective-permute-start(bf16[1024,1536]{1,0:T(8,128)(2,1)S(1)} %weight_grad.7), channel_id=1, source_target_pairs={{0,1},{1,0},{2,3},{3,2},{4,5},{5,4},{6,7},{7,6},{8,9},{9,8},{10,11... | collective-permute-start | bytes 9437192 | tf_op jit(solution)/shard_map/ppermute | solution.py:1279
  519.9 49.3 %collective-permute-start.12 = (bf16[512,768]{1,0:T(8,128)(2,1)S(1)}, bf16[512,768]{1,0:T(8,128)(2,1)S(1)}, u32[]{:S(2)}, u32[]{:S(2)}) collective-permute-start(bf16[512,768]{1,0:T(8,128)(2,1)S(1)} %copy-done.73), channel_id=1, source_target_pairs={{0,16},{1,17},{2,18},{3,19},{4,20},{5,21},{6,22},{7,23},{8,24},{9,... | collective-permute-start | bytes 2359304 | tf_op jit(solution)/shard_map/ppermute | solution.py:1237
  522.4 57.5 %collective-permute-start.13 = (bf16[512,512]{1,0:T(8,128)(2,1)S(1)}, bf16[512,512]{1,0:T(8,128)(2,1)S(1)}, u32[]{:S(2)}, u32[]{:S(2)}) collective-permute-start(bf16[512,512]{1,0:T(8,128)(2,1)S(1)} %add_convert_fusion.3), channel_id=1, source_target_pairs={{0,16},{1,17},{2,18},{3,19},{4,20},{5,21},{6,22},{7,23},{8,24},{9,... | collective-permute-start | bytes 1572872 | tf_op jit(solution)/shard_map/ppermute | solution.py:1237
  591.9 140.6 %collective-permute-start.16 = (bf16[512,1536]{1,0:T(8,128)(2,1)}, bf16[512,1536]{1,0:T(8,128)(2,1)}, u32[]{:S(2)}, u32[]{:S(2)}) collective-permute-start(bf16[512,1536]{1,0:T(8,128)(2,1)} %weight_grad.8), channel_id=1, source_target_pairs={{0,16},{1,17},{2,18},{3,19},{4,20},{5,21},{6,22},{7,23},{8,24},{9,... | collective-permute-start | bytes 4718600 | tf_op jit(solution)/shard_map/ppermute | solution.py:1237
  606.5 2.0 collective-permute-start.14
  608.6 6.4 copy-start.64
  609.4 114.3 %collective-permute-start.15 = (f32[512,128]{1,0:T(8,128)}, f32[512,128]{1,0:T(8,128)S(1)}, u32[]{:S(2)}, u32[]{:S(2)}) collective-permute-start(f32[512,128]{1,0:T(8,128)} %slice.176), channel_id=1, source_target_pairs={{0,16},{1,17},{2,18},{3,19},{4,20},{5,21},{6,22},{7,23},{8,24},{9,... | collective-permute-start | bytes 786440 | tf_op jit(solution)/shard_map/ppermute | solution.py:1336
  713.8 9.8 %copy-start.65 = (f32[1024,128]{1,0:T(8,128)S(1)}, f32[1024,128]{1,0:T(8,128)}, u32[]{:S(2)}) copy-start(f32[1024,128]{1,0:T(8,128)} %copy-done.64) | copy-start | bytes 1572868
  724.4 8.1 %copy-start.18 = (bf16[1024,1536]{1,0:T(8,128)(2,1)S(1)}, bf16[1024,1536]{1,0:T(8,128)(2,1)}, u32[]{:S(2)}) copy-start(bf16[1024,1536]{1,0:T(8,128)(2,1)} %copy-done.16) | copy-start | bytes 9437188
  739.6 36.9 %slice-start = ((s8[8552448]{0:T(1024)(128)(4,1)}), s8[163840]{0:T(1024)(128)(4,1)S(1)}, s32[]{:S(2)}) async-start(s8[8552448]{0:T(1024)(128)(4,1)} %bitcast.59), calls=%async_computation.5 | async-start | bytes 327680
  774.9 4.0 copy-start.37
  (53 other events, 113.3 us)
Sparse Core Ops, SparseCore 0:
  132.7 104.4 all-gather.1
  469.9 85.5 reduce-scatter.2
  582.6 113.8 reduce-scatter.4

commit v3 on v2

--- a/solution.py
+++ b/solution.py
@@ -27,6 +27,7 @@
 EPS_ADAM = 1e-08
 DECAY_WEIGHT = 0.1
 MESH = pl.DeviceIdType.MESH
+BIG = 60 * 2**20
 
 RANKS = 8
 HEADS = H // RANKS
@@ -227,7 +228,8 @@
     return pl.ds(at, width)
 
 
-def spread_kernel(copies, parts, w_ref, x_ref, dy_ref, s_ref, mix, outward, gates, down, xall, sall, x_own, dy_own,
+def spread_kernel(copies, parts, w_ref, x_ref, dy_ref, s_ref, mix, outward, gates, down,
+                  gates_side, down_side, xall, sall, x_own, dy_own,
                   pack, pack_sem, local, send, recv, seg_send, seg_recv,
                   ag_send, ag_recv, copy_send, copy_recv, core_send, core_recv, side_send, side_recv, turned):
     place = Place(copies)
@@ -235,8 +237,9 @@
     partners = [place.copy_at(shift) for shift in range(1, copies)]
     meet(peers + partners + [place.sibling()])
     me = place.rank
-    targets = (mix.at[0, 0], outward.at[0], gates.at[0], down.at[0])
-    others = (None, outward.at[1], gates.at[1], down.at[1])
+    targets = (mix.at[0, 0], outward.at[0, 0], gates, down)
+    others = (None, None, gates_side, down_side)
+    wide = (mix, outward)
     own = []
     firsts = (0, 5, 6, 8)
     packed = []
@@ -274,22 +277,52 @@
     sent = []
     onward = []
 
-    def forward(mask):
-        block = mix.at[0, 0, place.flip(mask)] if mask else pack.at[0]
+    def forward(group, mask, block):
+        whole = wide[group]
+        there = place.flip(mask)
         for shift in range(1, copies):
             copy = remote(
-                block, mix.at[0, copies - shift, place.flip(mask)],
-                copy_send.at[shift - 1, mask], copy_recv.at[copies - shift - 1, mask],
+                block, whole.at[0, copies - shift, there],
+                copy_send.at[group, shift - 1, mask], copy_recv.at[group, copies - shift - 1, mask],
                 place.copy_at(shift),
             )
             copy.start()
             onward.append(copy)
         copy = remote(
-            block, mix.at[1, 0, place.flip(mask)], core_send.at[0, mask], core_recv.at[0, mask],
-            place.sibling(),
+            block, whole.at[1, 0, there],
+            core_send.at[group, 0, mask], core_recv.at[group, 0, mask], place.sibling(),
         )
         copy.start()
         onward.append(copy)
+
+    def got_and_forward(group, mask):
+        got(group, mask)
+        forward(group, mask, wide[group].at[0, 0, place.flip(mask)])
+
+    def from_copies(group):
+        whole = wide[group]
+        for shift in range(1, copies):
+            for mask in range(RANKS):
+                there = place.flip(mask)
+                block = whole.at[0, shift, there]
+                remote(
+                    block, block, copy_send.at[group, shift - 1, mask], copy_recv.at[group, shift - 1, mask],
+                    place.copy_at(shift),
+                ).wait_recv()
+                copy = remote(
+                    block, whole.at[1, shift, there],
+                    core_send.at[group, shift, mask], core_recv.at[group, shift, mask], place.sibling(),
+                )
+                copy.start()
+                onward.append(copy)
+
+    def from_sibling(group):
+        for shift in range(copies):
+            for mask in range(RANKS):
+                block = wide[group].at[1, shift, place.flip(mask)]
+                remote(
+                    block, block, core_send.at[group, shift, mask], core_recv.at[group, shift, mask], place.sibling()
+                ).wait_recv()
 
     for mask in range(1, RANKS):
         for copy in packed[mask]:
@@ -302,7 +335,7 @@
     for copy in packed[0]:
         copy.wait()
     own_mix.start()
-    forward(0)
+    forward(0, 0, pack.at[0])
     turns = []
     for row, (source, target) in enumerate(((x_ref, xall.at[me]), (x_ref, x_own), (dy_ref, dy_own))):
         here = []
@@ -332,34 +365,29 @@
         copy = remote(s_ref, sall.at[me], seg_send.at[mask - 1], seg_recv.at[mask - 1], place.peer(mask))
         copy.start()
         seg_flights.append(copy)
+    sent = sent + send_group(1)
     for mask in range(1, RANKS):
-        got(0, mask)
-        forward(mask)
+        got_and_forward(0, mask)
     for copy in turns[0]:
         copy.wait()
     gather = Gather(place, xall, parts, MEET_EARLY, ag_send, ag_recv)
     for part in range(len(parts)):
         gather.start(part, 0)
-    for group in range(1, 4):
+    for group in range(2, 4):
         sent = sent + send_group(group)
+    for copy in own[0]:
+        copy.wait()
+    forward(1, 0, wide[1].at[0, 0, me])
+    for mask in range(1, RANKS):
+        got_and_forward(1, mask)
     for stage in range(3):
         for part in range(len(parts)):
             gather.landed(part, stage)
             if stage < 2:
                 gather.start(part, stage + 1)
-    for shift in range(1, copies):
-        for mask in range(RANKS):
-            block = mix.at[0, shift, place.flip(mask)]
-            remote(
-                block, block, copy_send.at[shift - 1, mask], copy_recv.at[shift - 1, mask], place.copy_at(shift)
-            ).wait_recv()
-            copy = remote(
-                block, mix.at[1, shift, place.flip(mask)],
-                core_send.at[shift, mask], core_recv.at[shift, mask], place.sibling(),
-            )
-            copy.start()
-            onward.append(copy)
-    for group in range(1, 4):
+    from_copies(0)
+    from_copies(1)
+    for group in range(2, 4):
         for copy in own[group - 1]:
             copy.wait()
         for mask in range(RANKS):
@@ -367,22 +395,18 @@
                 got(group, mask)
             copy = remote(
                 targets[group].at[place.flip(mask)], others[group].at[place.flip(mask)],
-                side_send.at[group - 1, mask], side_recv.at[group - 1, mask], place.sibling(),
+                side_send.at[group - 2, mask], side_recv.at[group - 2, mask], place.sibling(),
             )
             copy.start()
             onward.append(copy)
-    for group in range(1, 4):
+    for group in range(2, 4):
         for mask in range(RANKS):
             block = others[group].at[place.flip(mask)]
             remote(
-                block, block, side_send.at[group - 1, mask], side_recv.at[group - 1, mask], place.sibling()
+                block, block, side_send.at[group - 2, mask], side_recv.at[group - 2, mask], place.sibling()
             ).wait_recv()
-    for shift in range(copies):
-        for mask in range(RANKS):
-            block = mix.at[1, shift, place.flip(mask)]
-            remote(
-                block, block, core_send.at[shift, mask], core_recv.at[shift, mask], place.sibling()
-            ).wait_recv()
+    from_sibling(0)
+    from_sibling(1)
     for copy in seg_flights:
         copy.wait()
     own_mix.wait()
@@ -418,23 +442,28 @@
         functools.partial(spread_kernel, copies, ((0, tokens // 2), (tokens // 2, tokens // 2))),
         out_shape=(
             shape((2, copies, RANKS, rows, MIXW), BF),
-            shape((2, RANKS, rows, OW), BF),
-            shape((2, RANKS, rows, 2 * FW), BF),
-            shape((2, RANKS, rows, FW), BF),
+            shape((2, copies, RANKS, rows, OW), BF),
+        )
+        + (
+            shape((RANKS, rows, 2 * FW), BF),
+            shape((RANKS, rows, FW), BF),
+        )
+        * 2
+        + (
             shape((RANKS, tokens, D), BF),
             shape((RANKS,) + seg.shape, seg.dtype),
             shape((tokens, D), BF),
             shape((tokens, D), BF),
         ),
         in_specs=[any_spec(), vmem_spec(), vmem_spec(), any_spec()],
-        out_specs=[any_spec()] * 8,
+        out_specs=[any_spec()] * 10,
         scratch_shapes=[
             pltpu.VMEM((RANKS, rows, MIXW), BF), dma(RANKS, 5), dma(11), dma(9, RANKS - 1), dma(4, RANKS - 1),
             dma(RANKS - 1), dma(RANKS - 1), dma(3, 7), dma(3, 7),
-            dma(copies - 1, RANKS), dma(copies - 1, RANKS), dma(copies, RANKS), dma(copies, RANKS),
-            dma(3, RANKS), dma(3, RANKS), dma(3, 4 * copies),
+            dma(2, copies - 1, RANKS), dma(2, copies - 1, RANKS), dma(2, copies, RANKS), dma(2, copies, RANKS),
+            dma(2, RANKS), dma(2, RANKS), dma(3, 4 * copies),
         ],
-        compiler_params=pltpu.CompilerParams(collective_id=1, has_side_effects=True),
+        compiler_params=pltpu.CompilerParams(collective_id=1, has_side_effects=True, vmem_limit_bytes=BIG),
         cost_estimate=takes(5),
         name="spread",
     )(weights, x, dy, seg)
@@ -484,9 +513,6 @@
 
 def cube_scratch(tokens):
     return [pltpu.VMEM((7, tokens, D), BF), dma(3, 7), dma(3, 7)]
-
-
-BIG = 56 * 2**20
 
 
 def branch(copies, partial, x, gain):
@@ -643,7 +669,7 @@
         out_specs=(any_spec(), vmem_spec()),
         scratch_shapes=home_scratch()
         + [pltpu.VMEM((RANKS - 1, rows, EXTRA), F32), pltpu.VMEM((rows, EXTRA), F32), dma(RANKS - 1), dma(RANKS - 1)],
-        compiler_params=pltpu.CompilerParams(collective_id=6, has_side_effects=True),
+        compiler_params=pltpu.CompilerParams(collective_id=6, has_side_effects=True, vmem_limit_bytes=BIG),
         cost_estimate=takes(5),
         name="home",
     )(array, extra)
@@ -665,7 +691,7 @@
         in_specs=[any_spec()] * 4,
         out_specs=any_spec(),
         scratch_shapes=home_scratch(),
-        compiler_params=pltpu.CompilerParams(collective_id=4, has_side_effects=True),
+        compiler_params=pltpu.CompilerParams(collective_id=4, has_side_effects=True, vmem_limit_bytes=BIG),
         cost_estimate=takes(5),
         name="home_rest",
     )(*grad_rows)
@@ -907,7 +933,7 @@
         out_specs=[
             by_sequence(tokens, VW), by_sequence(1, HEADS, tokens, tokens), by_sequence(1, HEADS, tokens, DV),
         ],
-        compiler_params=pltpu.CompilerParams(vmem_limit_bytes=40 * 2**20),
+        compiler_params=pltpu.CompilerParams(vmem_limit_bytes=BIG),
         cost_estimate=takes(5),
         name="mixer",
     )(rank, scalars, seg, p, taps, gain)
@@ -933,7 +959,7 @@
         out_specs=[
             by_sequence(tokens, MIXW), whole_block(CONV, CHANNELS), whole_block(1, DV), whole_block(8, 128),
         ],
-        compiler_params=pltpu.CompilerParams(vmem_limit_bytes=40 * 2**20),
+        compiler_params=pltpu.CompilerParams(vmem_limit_bytes=BIG),
         cost_estimate=takes(5),
         name="mixer_back",
     )(rank, scalars, seg, p, taps, gain, inverse, update, dz)
@@ -970,7 +996,7 @@
         + [there] * 3 + [any_spec()] * len(filled),
         out_specs=[there] * 5,
         input_output_aliases={5 + at: at for at in range(len(filled))},
-        compiler_params=pltpu.CompilerParams(vmem_limit_bytes=40 * 2**20),
+        compiler_params=pltpu.CompilerParams(vmem_limit_bytes=BIG),
         cost_estimate=takes(5),
         name="adam",
     )(scalars, grads, *state, *filled)
@@ -983,8 +1009,9 @@
     refs[-1][...] = total.astype(BF)
 
 
-def weight_grad(left, right, at, width, adds=()):
-    tokens, count = right.shape
+def weight_grad(left, right, at, width, adds=(), count=None):
+    tokens = right.shape[0]
+    count = right.shape[1] if count is None else count
     tile = 768 if count % 768 == 0 else count
 
     def add_spec(row, column):
@@ -1000,7 +1027,7 @@
         ]
         + [add_spec(row, column) for _, row, column in adds],
         out_specs=pl.BlockSpec((width, tile), lambda step: (0, step)),
-        compiler_params=pltpu.CompilerParams(vmem_limit_bytes=40 * 2**20),
+        compiler_params=pltpu.CompilerParams(vmem_limit_bytes=BIG),
         cost_estimate=takes(1),
         name="weight_grad",
     )(left, right, *[array for array, _, _ in adds])
@@ -1030,7 +1057,7 @@
         out_specs=[
             pl.BlockSpec((tokens, tile), lambda step: (0, step)), pl.BlockSpec((1, tile), lambda step: (0, step)),
         ],
-        compiler_params=pltpu.CompilerParams(vmem_limit_bytes=48 * 2**20),
+        compiler_params=pltpu.CompilerParams(vmem_limit_bytes=BIG),
         cost_estimate=takes(1),
         name="input_back",
     )(grad, w, x, scale)
@@ -1064,7 +1091,7 @@
         in_specs=[by_sequence(rows, D), whole_block(D, MIXW)],
         out_specs=[by_sequence(rows, D), by_sequence(rows, MIXW), whole_block(8, D), by_sequence(rows, 128)],
         scratch_shapes=[pltpu.VMEM((8, D), F32)],
-        compiler_params=pltpu.CompilerParams(vmem_limit_bytes=40 * 2**20),
+        compiler_params=pltpu.CompilerParams(vmem_limit_bytes=BIG),
         cost_estimate=takes(1),
         name="project",
     )(x, w)
@@ -1092,7 +1119,7 @@
         out_shape=(shape, shape),
         in_specs=[smem_spec()] + [vmem_spec()] * 6,
         out_specs=[vmem_spec()] * 2,
-        compiler_params=pltpu.CompilerParams(vmem_limit_bytes=40 * 2**20),
+        compiler_params=pltpu.CompilerParams(vmem_limit_bytes=BIG),
         cost_estimate=takes(1),
         name="finish",
     )(place, hidden, feed, grad, x, d_hidden, gain)
@@ -1151,7 +1178,9 @@
     in_place = (D // (4 * copies)) % 128 == 0
     x, dy = (inputs, cotangent) if in_place else (order.relative(inputs, 1), order.relative(cotangent, 1))
     seg = jnp.broadcast_to(segment_ids[None, :], (8, tokens))
-    mix_blocks, out_block, gate_block, down_block, x_all, seg_all, x, dy = spread(copies, weights, x, dy, seg)
+    mix_blocks, out_blocks, gate_block, down_block, gate_side, down_side, x_all, seg_all, x, dy = spread(
+        copies, weights, x, dy, seg
+    )
     cubes = [
         [(copy * 4 + j % 4) * 4 + (j // 4) * 2 + side for j in range(RANKS)]
         for copy in range(copies)
@@ -1160,19 +1189,19 @@
     dy_all = lax.all_gather(dy, axes, axis_index_groups=cubes, axis=0, tiled=True)
     x_all = x_all.reshape(group_tokens, D)
     w_mix = mix_blocks.reshape(D, MIXW)
+    w_out = out_blocks.reshape(D, OW)
 
     def from_copies(blocks):
-        block = blocks[0].reshape(block_rows, blocks.shape[3])
+        block = blocks.reshape(block_rows, blocks.shape[2])
         return [lax.ppermute(block, axes, copy_pairs[copies - shift - 1]) for shift in range(1, copies)]
 
-    def collect(blocks, landed):
-        mine = [blocks[0].reshape(block_rows, blocks.shape[3])] + landed
-        theirs = [blocks[1].reshape(block_rows, blocks.shape[3])]
+    def collect(blocks, side, landed):
+        mine = [blocks.reshape(block_rows, blocks.shape[2])] + landed
+        theirs = [side.reshape(block_rows, side.shape[2])]
         theirs = theirs + [lax.ppermute(one, axes, core_pairs) for one in landed]
         return jnp.concatenate(mine + theirs, axis=0)
 
     together = lax.optimization_barrier
-    out_landed = from_copies(out_block)
     gate_landed = from_copies(gate_block)
     down_landed = from_copies(down_block)
     normed, p, gains, x_scale = project(x_all, w_mix)
@@ -1205,13 +1234,12 @@
     out_gain = column[2 * H : 2 * H + DV][None]
     rank_arg = jnp.reshape(rank, (1,)).astype(jnp.int32)
     gated, inverse, update = mixer(rank_arg, scalars, seg_all, p, taps, out_gain, tokens)
-    w_out = collect(out_block, out_landed)
     partial = dot(gated, w_out, NT).astype(BF)
     hidden, normed_two = branch(copies, partial.reshape(RANKS, tokens, D), x, gain_two)
     normed_two = normed_two.reshape(group_tokens, D)
     normed_two, gate_landed, down_landed = together((normed_two, gate_landed, down_landed))
-    w_gates = collect(gate_block, gate_landed)
-    w_down = collect(down_block, down_landed)
+    w_gates = collect(gate_block, gate_side, gate_landed)
+    w_down = collect(down_block, down_side, down_landed)
     gate_up = dot(normed_two, w_gates, NN)
     gate_part, up_part = gate_up[:, :FW], gate_up[:, FW:]
     tile_count = jnp.where(rank < FULL_RANKS, FT, FT - 1)
@@ -1256,13 +1284,15 @@
     gate_away = away_rows(normed_two, d_gate_part, gate_got[:, :FW])
     up_away = away_rows(normed_two, d_up_part, gate_got[:, FW:])
     gate_away, up_away, d_normed_two = together((gate_away, up_away, d_normed_two))
+    up_landed = to_copies(up_away)
     d_hidden, gain_two_grad, d_hidden_all = hidden_back(
         copies, d_normed_two.reshape(RANKS, tokens, D), hidden, dy, gain_two
     )
     d_hidden_all = d_hidden_all.reshape(group_tokens, D)
-    d_hidden_all, up_away, gate_away, down_landed, feed = together((d_hidden_all, up_away, gate_away, down_landed, feed))
+    d_hidden_all, up_landed, gate_away, down_landed, feed = together(
+        (d_hidden_all, up_landed, gate_away, down_landed, feed)
+    )
     feed = lax.psum_scatter(feed, axes, axis_index_groups=cubes, scatter_dimension=0, tiled=True)
-    up_landed = to_copies(up_away)
     gate_landed = to_copies(gate_away)
     out_half, out_got = first_half(d_hidden_all, gated)
     out_half, d_hidden_all = together((out_half, d_hidden_all))
@@ -1273,18 +1303,16 @@
     d_mix, d_taps, d_out_gain, d_scalars = mixer_back(
         rank_arg, scalars, seg_all, p, taps, out_gain, inverse, update, d_gated, tokens
     )
-    d_mix, up_landed = together((d_mix, up_landed))
-    d_wide = d_mix[:, : MIXW - EXTRA]
-    mix_half = weight_grad(normed, d_wide, 1, half)
+    d_mix, gate_landed, out_landed = together((d_mix, gate_landed, out_landed))
+    mix_columns = MIXW - EXTRA
+    mix_half = weight_grad(normed, d_mix, 1, half, (), mix_columns)
     mix_got = lax.ppermute(mix_half, axes, core_pairs)
     mix_half, d_mix = together((mix_half, d_mix))
     d_normed, gain_one_grad = input_back(d_mix, w_mix, x_all, x_scale)
     gain_one_grad = gain_one_grad[0]
-    d_normed, gain_one_grad, mix_got, gate_landed, out_landed = together(
-        (d_normed, gain_one_grad, mix_got, gate_landed, out_landed)
-    )
+    d_normed, gain_one_grad, mix_got = together((d_normed, gain_one_grad, mix_got))
     mix_away = [
-        weight_grad(normed, d_wide, at, block_rows, ((mix_got, at, 0),)) for at in range(1, copies)
+        weight_grad(normed, d_mix, at, block_rows, ((mix_got, at, 0),), mix_columns) for at in range(1, copies)
     ]
     mix_landed = to_copies(mix_away)
     d_input = lax.psum_scatter(d_normed, axes, axis_index_groups=cubes, scatter_dimension=0, tiled=True)
@@ -1292,9 +1320,10 @@
         (mix_away, d_gate_part, d_up_part, activated, gated)
     )
 
-    def own_rows(left, right, got, column, landed):
-        total = weight_grad(left, right, 0, block_rows, ((got, 0, column),) + tuple((one, 0, 0) for one in landed))
-        return total.reshape(RANKS, rows, right.shape[1])
+    def own_rows(left, right, got, column, landed, count=None):
+        adds = ((got, 0, column),) + tuple((one, 0, 0) for one in landed)
+        total = weight_grad(left, right, 0, block_rows, adds, count)
+        return total.reshape(RANKS, rows, total.shape[1])
 
     up_rows = own_rows(normed_two, d_up_part, gate_got, FW, up_landed)
     gate_rows = own_rows(normed_two, d_gate_part, gate_got, 0, gate_landed)
@@ -1357,7 +1386,7 @@
     done = adam(adam_scalars, grads_rest, state, None, MIX_END, 2048, 4)
     done = adam(adam_scalars, grads_rest, state, done, MIX_END + 4 * 2048, 2560, 5)
     done, extra_rows, output, input_grad, normed = together((done, extra_rows, output, input_grad, normed))
-    mix_rows = own_rows(normed, d_wide, mix_got, 0, mix_landed)
+    mix_rows = own_rows(normed, d_mix, mix_got, 0, mix_landed, mix_columns)
     grads_mix, extra_rows = home(copies, mix_rows, extra_rows.reshape(RANKS, rows, EXTRA))
     done = adam(adam_scalars, extra_rows, state, done, EXTRA_START, EXTRA, 1)
     done = adam(adam_scalars, grads_mix, state, done, 0, 2048, 6)

time: 804 us -> 765 us (0.951)
  local copies, waits for them, and re-layouts: 79.5 us -> 20.7 us
  Pallas kernels: 539 us -> 591 us
  waiting for transfers between devices: 50.6 us -> 21.9 us
    unnamed x165 -> x53, local copies, waits for them, and re-layouts: 55.6 us -> 6.09 us
    ppermute x5, waiting for transfers between devices: 44.9 us -> 17 us  [to_copies(): lax.ppermute(one, axes, pairs)]
    pallas_call x1, Pallas kernels: 78.9 us -> 98 us  [hidden_back(): pl.pallas_call(functools.partial(hidden_back_kernel, copies, row_parts(to...]
    pallas_call x7, Pallas kernels: 16.9 us -> 33.2 us  [weight_grad(): pl.pallas_call(weight_grad_kernel, grid=(count // tile,), out_shape=jax.S...]
    ppermute x3 -> x2, starting transfers between devices: 19.2 us -> 17.6 us  [from_copies(): lax.ppermute(block, axes, copy_pairs[copies - shift - 1])]
  transfers between devices with their start and end apart: 20 -> 18, of which waited for: 4 -> 3; matrix products, arithmetic and copies ran while one was open for 13% -> 12% of each run, Pallas kernels for 47% -> 55%
where the time goes in v3:
time: 765 us; the launch traced here: 755 us
  Pallas kernels  591 us (77%)
  matrix products  70.2 us (9%)
  starting transfers between devices  27.7 us (4%)
  waiting for transfers between devices  21.9 us (3%)
  local copies, waits for them, and re-layouts  20.7 us (3%)
  between operations  17.5 us (2%)
    pallas_call x1, Pallas kernels, spread(): pl.pallas_call(functools.partial(spread_kernel, copies, ((0, tokens // 2)...  125 us
    pallas_call x1, Pallas kernels, hidden_back(): pl.pallas_call(functools.partial(hidden_back_kernel, copies, row_parts(to...  98 us
    pallas_call x1, Pallas kernels, branch(): pl.pallas_call(functools.partial(branch_kernel, copies, row_parts(tokens,...  97.7 us
    pallas_call x1, Pallas kernels, home_rest(): pl.pallas_call(functools.partial(home_rest_kernel, copies), out_shape=jax...  80.1 us
    dot_general x14, matrix products, dot(): lax.dot_general(left, right, (axes, ((), ())), preferred_element_type=F32)  70.2 us
    pallas_call x7, Pallas kernels, weight_grad(): pl.pallas_call(weight_grad_kernel, grid=(count // tile,), out_shape=jax.S...  33.2 us
    pallas_call x1, Pallas kernels, mixer_back(): pl.pallas_call(mixer_back_kernel, grid=(count,), out_shape=(shape((p.shap...  33.2 us
    pallas_call x4, Pallas kernels, adam(): pl.pallas_call(functools.partial(adam_kernel, len(filled)), grid=(count,)...  31.8 us
  transfers between devices with their start and end apart: 18, of which 3 were waited for; matrix products, arithmetic and copies ran while one was open for 12% of the time, Pallas kernels for 55%

profile of v3, /device:TPU:0, one launch (start us, length us, event | category | flops | bytes accessed | tf_op | source)
XLA Modules:
  0.0 755.4 jit_solution(7483137766763872558)
XLA Ops:
  8.5 125.3 %spread.1 = (bf16[2,2,8,64,1664]{4,3,2,1,0:T(8,128)(2,1)}, bf16[2,2,8,64,512]{4,3,2,1,0:T(8,128)(2,1)}, bf16[8,64,1536]{2,1,0:T(8,128)(2,1)}, bf16[8,64,768]{2,1...) custom-call(bf16[64,33408]{1,0:T(8,128)(2,1)} %w_ref.1, ...), custom_call_target="tpu_custom_call" | custom-call | bytes 5000 | tf_op jit(solution)/shard_map/spread/pallas_call | solution.py:441
  133.8 17.5 %collective-permute-start.1 = (bf16[512,768]{1,0:T(8,128)(2,1)}, bf16[512,768]{1,0:T(8,128)(2,1)}, u32[]{:S(2)}, u32[]{:S(2)}) collective-permute-start(bf16[512,768]{1,0:T(8,128)(2,1)} %bitcast.94), channel_id=1, source_target_pairs={{0,16},{1,17},{2,18},{3,19},{4,20},{5,21},{6,22},{7,23},{8,24},{9,... | collective-permute-start | bytes 2359304 | tf_op jit(solution)/shard_map/ppermute | solution.py:1196
  155.2 14.1 %project.1 = (bf16[1024,2048]{1,0:T(8,128)(2,1)}, f32[1024,1664]{1,0:T(8,128)}, f32[8,2048]{1,0:T(8,128)}, f32[1024,128]{1,0:T(8,128)}) custom-call(bf16[1024,2048]{1,0:T(8,128)(2,1)} %bitcast.63, bf16[2048,1664]{1,0:T(8,128)(2,1)} %bitcast.61), custom_call_target="tpu_custom_call" | custom-call | bytes 1000 | tf_op jit(solution)/shard_map/project/pallas_call | solution.py:1087
  170.7 30.5 %mixer.1 = (bf16[1024,512]{1,0:T(8,128)(2,1)}, f32[8,2,128,128]{3,2,1,0:T(8,128)}, f32[8,2,128,256]{3,2,1,0:T(8,128)}) custom-call(s32[1]{0:T(128)} %bitcast.2.rank_ref, f32[4]{0:T(128)} %pad_maximum_fusion.6.scalars, s32[8,8,128]{2,1,0:T(8,128)} %get-tuple-element.106.seg_ref, f32[1024,1664]{1,0:T(8,128)} %get-tuple-element.107.p_ref, ...), custom_call_target="tpu_custom_call" | custom-call | bytes 5000 | tf_op jit(solution)/shard_map/mixer/pallas_call | solution.py:921
  201.2 1.5 fusion.45
  202.8 5.6 convolution_convert_fusion.1
  208.4 97.7 %branch.1 = (f32[128,2048]{1,0:T(8,128)}, bf16[8,128,2048]{2,1,0:T(8,128)(2,1)}) custom-call(bf16[8,128,2048]{2,1,0:T(8,128)(2,1)} %bitcast.76, bf16[128,2048]{1,0:T(8,128)(2,1)} %get-tuple-element.112.x_ref, f32[1,2048]{1,0:T(1,128)} %get-tuple-element.221.gain_ref), custom_call_target="tpu_custom_call" | custom-call | bytes 5000 | tf_op jit(solution)/shard_map/branch/pallas_call | solution.py:521
  306.8 3.1 collective-permute-done.3
  309.9 10.0 %fusion.12 = f32[1024,1536]{1,0:T(8,128)S(1)} fusion(bf16[1024,2048]{1,0:T(8,128)(2,1)} %bitcast.65, bf16[512,1536]{1,0:T(8,128)(2,1)} %collective-permute-done.3, bf16[512,1536]{1,0:T(8,128)(2,1)} %bitcast.92, bf16[512,1536]{1,0:T(8,128)(2,1)} %collective-permute-done, bf16[512,1536]{1,0:T(8,128)(2,1)S(1)} %bitcast.91), kind=kOutput, calls=%fused_computation.32 | convolution fusion | flops 6467616768 | bytes 16777216 | tf_op jit(solution)/shard_map/dot_general | solution.py:701
  320.0 2.7 copy-done.3
  323.7 4.0 fusion.6
  328.1 8.0 %add_multiply_fusion = (bf16[1024,768]{1,0:T(8,128)(2,1)S(1)}, bf16[1024,768]{1,0:T(8,128)(2,1)S(1)}) fusion(f32[1024,1536]{1,0:T(8,128)S(1)} %copy-done.4, bf16[1024,2048]{1,0:T(8,128)(2,1)} %all-gather.2.cloned.1.call-done.left_ref, bf16[512,768]{1,0:T(8,128)(2,1)} %collective-permute-done.2, bf16[512,768]{1,0:T(8,128)(2,1)S(1)} %bitcast.97, ...), kind=kOutput, calls=%fused_computation.10 | convolution fusion | flops 3244032000 | bytes 16777216 | tf_op jit(solution)/shard_map/dot_general | solution.py:701
  336.7 1.6 copy-done.1
  338.3 5.3 convolution_convert_fusion.3
  343.9 3.8 add_convert_fusion.2
  347.7 1.4 collective-permute-start.7
  349.1 11.5 %convolution_convert_fusion = bf16[1024,2048]{1,0:T(8,128)(2,1)} fusion(bf16[1024,1536]{1,0:T(8,128)(2,1)S(1)} %fusion, bf16[512,1536]{1,0:T(8,128)(2,1)} %collective-permute-done.3, bf16[512,1536]{1,0:T(8,128)(2,1)} %bitcast.93, bf16[512,1536]{1,0:T(8,128)(2,1)} %collective-permute-done, bf16[512,1536]{1,0:T(8,128)(2,1)} %bitcast.90), kind=kOutput, calls=%fused_computation.3 | convolution fusion | flops 6469713920 | bytes 13631488 | tf_op jit(solution)/shard_map/dot_general | solution.py:701
  360.7 2.0 add_convert_fusion
  362.7 1.9 add_convert_fusion.1
  364.6 1.5 collective-permute-start.6
  366.1 6.9 convolution_convert_fusion.2
  373.0 98.0 %hidden_back.1 = (f32[128,2048]{1,0:T(8,128)}, f32[1,2048]{1,0:T(1,128)}, bf16[8,128,2048]{2,1,0:T(8,128)(2,1)}) custom-call(bf16[8,128,2048]{2,1,0:T(8,128)(2,1)} %bitcast.77, f32[128,2048]{1,0:T(8,128)} %get-tuple-element.126.h_ref.hidden_ref, bf16[128,2048]{1,0:T(8,128)(2,1)} %get-tuple-element.118.dy_ref, f32[1,2048]{1,0:T(1,128)} %get-tuple-element.221.gain_ref), custom_call_target="tpu_custom_call" | custom-call | bytes 5000 | tf_op jit(solution)/shard_map/hidden_back/pallas_call | solution.py:564
  471.3 3.3 fusion.9
  475.4 3.6 fusion.47.dz_ref
  479.1 1.5 add_convert_fusion.3
  480.6 2.2 collective-permute-start.10
  482.8 33.2 %mixer_back.1 = (bf16[1024,1664]{1,0:T(8,128)(2,1)}, f32[4,1024]{1,0:T(4,128)}, f32[1,256]{1,0:T(1,128)}, f32[8,128]{1,0:T(8,128)}) custom-call(s32[1]{0:T(128)} %bitcast.2.rank_ref, f32[4]{0:T(128)} %pad_maximum_fusion.6.scalars, s32[8,8,128]{2,1,0:T(8,128)} %get-tuple-element.106.seg_ref, f32[1024,1664]{1,0:T(8,128)} %get-tuple-element.107.p_ref, ...), custom_call_target="tpu_custom_call" | custom-call | bytes 5000 | tf_op jit(solution)/shard_map/mixer_back/pallas_call | solution.py:945
  516.0 17.0 %collective-permute-done.10.refs_1_ = bf16[512,512]{1,0:T(8,128)(2,1)S(1)} collective-permute-done((bf16[512,512]{1,0:T(8,128)(2,1)}, bf16[512,512]{1,0:T(8,128)(2,1)S(1)}, u32[]{:S(2)}, u32[]{:S(2)}) %collective-permute-start.10) | collective-permute-done | bytes 524320 | tf_op jit(solution)/shard_map/ppermute | solution.py:1265
  533.0 7.2 weight_grad.7
  540.2 12.6 %input_back.1 = (bf16[1024,2048]{1,0:T(8,128)(2,1)}, f32[1,2048]{1,0:T(1,128)}) custom-call(bf16[1024,1664]{1,0:T(8,128)(2,1)} %get-tuple-element.137.right_ref.grad_ref, bf16[2048,1664]{1,0:T(8,128)(2,1)} %bitcast.62, bf16[1024,2048]{1,0:T(8,128)(2,1)} %bitcast.64, f32[1024,128]{1,0:T(8,128)} %get-tuple-element.138.scale_ref), custom_call_target="tpu_custom_call" | custom-call | bytes 1000 | tf_op jit(solution)/shard_map/input_back/pallas_call | solution.py:1047
  552.9 1.9 fusion.44
  554.8 5.0 weight_grad.8
  559.8 2.3 collective-permute-start.14
  562.1 3.4 weight_grad.9
  570.9 1.7 fusion.17
  573.1 2.7 bitcast_add_fusion
  576.2 1.7 collective-permute-done.12
  582.5 4.1 weight_grad.12
  586.6 4.1 weight_grad.11
  590.8 4.1 weight_grad.10
  594.9 80.1 %home_rest.1.grad_ref = bf16[64,33280]{1,0:T(8,128)(2,1)} custom-call(bf16[8,64,512]{2,1,0:T(8,128)(2,1)} %bitcast.81, bf16[8,64,768]{2,1,0:T(8,128)(2,1)} %bitcast.80, bf16[8,64,768]{2,1,0:T(8,128)(2,1)} %bitcast.79, bf16[8,64,768]{2,1,0:T(8,128)(2,1)} %bitcast.78), custom_call_target="tpu_custom_call" | custom-call | bytes 5000 | tf_op jit(solution)/shard_map/home_rest/pallas_call | solution.py:688
  675.0 7.6 %adam.4 = (f32[64,33408]{1,0:T(8,128)}, f32[64,33408]{1,0:T(8,128)}, f32[64,33408]{1,0:T(8,128)}, f32[64,33408]{1,0:T(8,128)}, bf16[64,33408]{1,0:T(8,128)(2,1)}) custom-call(f32[5]{0:T(128)} %stack.14.scalars, bf16[64,33280]{1,0:T(8,128)(2,1)} %home_rest.1.grad_ref, f32[64,33408]{1,0:T(8,128)} %one_ref.7, f32[64,33408]{1,0:T(8,128)} %two_ref.7, ...), custom_call_target="tpu_custom_call" | custom-call | bytes 5000 | tf_op jit(solution)/shard_map/adam/pallas_call | solution.py:991
  682.6 11.8 %adam.5 = (f32[64,33408]{1,0:T(8,128)}, f32[64,33408]{1,0:T(8,128)}, f32[64,33408]{1,0:T(8,128)}, f32[64,33408]{1,0:T(8,128)}, bf16[64,33408]{1,0:T(8,128)(2,1)}) custom-call(f32[5]{0:T(128)} %stack.14.scalars, bf16[64,33280]{1,0:T(8,128)(2,1)} %home_rest.1.grad_ref, ...), custom_call_target="tpu_custom_call", output_to_operand_aliasing={{0}: (5, {}), {1}: (6, {}), {2}: (7, {}), {3}: (8, {}), {4}... | custom-call | bytes 5000 | tf_op jit(solution)/shard_map/adam/pallas_call | solution.py:991
  695.1 3.9 finish.1
  699.0 5.3 weight_grad.13
  704.2 30.3 %home.1 = (bf16[64,12288]{1,0:T(8,128)(2,1)}, f32[64,128]{1,0:T(8,128)}) custom-call(bf16[8,64,1536]{2,1,0:T(8,128)(2,1)} %bitcast.71, f32[8,64,128]{2,1,0:T(8,128)} %bitcast.85), custom_call_target="tpu_custom_call" | custom-call | bytes 5000 | tf_op jit(solution)/shard_map/home/pallas_call | solution.py:665
  736.0 1.5 adam.6
  737.5 10.9 %adam.7 = (f32[64,33408]{1,0:T(8,128)}, f32[64,33408]{1,0:T(8,128)}, f32[64,33408]{1,0:T(8,128)}, f32[64,33408]{1,0:T(8,128)}, bf16[64,33408]{1,0:T(8,128)(2,1)}) custom-call(f32[5]{0:T(128)} %stack.14.scalars, bf16[64,12288]{1,0:T(8,128)(2,1)} %get-tuple-element.181.grad_ref, ...), custom_call_target="tpu_custom_call", output_to_operand_aliasing={{0}: (5, {}), {1}: (6, {}), {2}: (7, {}), {3}: (8, {}), {4}... | custom-call | bytes 5000 | tf_op jit(solution)/shard_map/adam/pallas_call | solution.py:991
  (139 shorter events, 20.8 us)
Async XLA Ops:
  7.2 316.5 %all-gather.2.cloned.1.call-start = ((), (), s32[]{:S(2)}) async-start(), calls=%async_computation.2 | async-start | bytes 4718592 | tf_op jit(solution)/shard_map/all_gather | solution.py:1189
  133.8 561.3 %reduce-scatter.3.cloned.1.call-start = ((), (), s32[]{:S(2)}) async-start(), calls=%async_computation.3 | async-start | bytes 4718592 | tf_op jit(solution)/shard_map/reduce_scatter | solution.py:1295
  133.8 172.3 %collective-permute-start.1 = (bf16[512,768]{1,0:T(8,128)(2,1)}, bf16[512,768]{1,0:T(8,128)(2,1)}, u32[]{:S(2)}, u32[]{:S(2)}) collective-permute-start(bf16[512,768]{1,0:T(8,128)(2,1)} %bitcast.94), channel_id=1, source_target_pairs={{0,16},{1,17},{2,18},{3,19},{4,20},{5,21},{6,22},{7,23},{8,24},{9,... | collective-permute-start | bytes 2359304 | tf_op jit(solution)/shard_map/ppermute | solution.py:1196
  151.4 154.7 %collective-permute-start = (bf16[512,1536]{1,0:T(8,128)(2,1)}, bf16[512,1536]{1,0:T(8,128)(2,1)}, u32[]{:S(2)}, u32[]{:S(2)}) collective-permute-start(bf16[512,1536]{1,0:T(8,128)(2,1)} %bitcast.89), channel_id=1, source_target_pairs={{0,16},{1,17},{2,18},{3,19},{4,20},{5,21},{6,22},{7,23},{8,24},{9,... | collective-permute-start | bytes 4718600 | tf_op jit(solution)/shard_map/ppermute | solution.py:1196
  170.1 0.6 copy-start.13
  170.7 32.0 %copy-start.16 = (bf16[2,2,8,64,512]{4,3,2,1,0:T(8,128)(2,1)S(1)}, bf16[2,2,8,64,512]{4,3,2,1,0:T(8,128)(2,1)}, u32[]{:S(2)}) copy-start(bf16[2,2,8,64,512]{4,3,2,1,0:T(8,128)(2,1)} %get-tuple-element.111) | copy-start | bytes 6291460
  208.4 101.6 %copy-start.18 = (bf16[8,64,1536]{2,1,0:T(8,128)(2,1)S(1)}, bf16[8,64,1536]{2,1,0:T(8,128)(2,1)}, u32[]{:S(2)}) copy-start(bf16[8,64,1536]{2,1,0:T(8,128)(2,1)} %get-tuple-element.115) | copy-start | bytes 4718596
  306.1 3.8 collective-permute-start.3
  306.3 21.7 %collective-permute-start.2 = (bf16[512,768]{1,0:T(8,128)(2,1)}, bf16[512,768]{1,0:T(8,128)(2,1)}, u32[]{:S(2)}, u32[]{:S(2)}) collective-permute-start(bf16[512,768]{1,0:T(8,128)(2,1)} %collective-permute-done.1), channel_id=1, source_target_pairs={{0,1},{1,0},{2,3},{3,2},{4,5},{5,4},{6,7},{7,6},{8,9},{9,8},{10,11... | collective-permute-start | bytes 2359304 | tf_op jit(solution)/shard_map/ppermute | solution.py:1201
  320.0 2.7 copy-start.3
  323.6 4.1 copy-start.5
  323.6 4.3 copy-start.19
  323.6 4.3 copy-start.21
  323.7 4.4 copy-start.4
  327.8 16.2 %collective-permute-start.4 = (bf16[1024,768]{1,0:T(8,128)(2,1)S(1)}, bf16[1024,768]{1,0:T(8,128)(2,1)S(1)}, u32[]{:S(2)}, u32[]{:S(2)}) collective-permute-start(bf16[1024,768]{1,0:T(8,128)(2,1)S(1)} %fusion.6), channel_id=1, source_target_pairs={{0,1},{1,0},{2,3},{3,2},{4,5},{5,4},{6,7},{7,6},{8,9},{9,8},{10,11... | collective-permute-start | bytes 4718600 | tf_op jit(solution)/shard_map/ppermute | solution.py:1256
  336.1 2.2 copy-start.1
  338.3 5.6 copy-start.6
  343.6 17.1 %collective-permute-start.5 = (bf16[1024,1536]{1,0:T(8,128)(2,1)}, bf16[1024,1536]{1,0:T(8,128)(2,1)S(1)}, u32[]{:S(2)}, u32[]{:S(2)}) collective-permute-start(bf16[1024,1536]{1,0:T(8,128)(2,1)} %convolution_convert_fusion.3), channel_id=1, source_target_pairs={{0,1},{1,0},{2,3},{3,2},{4,5},{5,4},{6,7},{7,6},{8,9},{9,8},{10,11... | collective-permute-start | bytes 9437192 | tf_op jit(solution)/shard_map/ppermute | solution.py:1256
  343.9 3.8 copy-start.9
  347.7 123.3 %collective-permute-start.7 = (bf16[512,768]{1,0:T(8,128)(2,1)}, bf16[512,768]{1,0:T(8,128)(2,1)}, u32[]{:S(2)}, u32[]{:S(2)}) collective-permute-start(bf16[512,768]{1,0:T(8,128)(2,1)} %add_convert_fusion.2), channel_id=1, source_target_pairs={{0,16},{1,17},{2,18},{3,19},{4,20},{5,21},{6,22},{7,23},{8,24},{9,... | collective-permute-start | bytes 2359304 | tf_op jit(solution)/shard_map/ppermute | solution.py:1265
  360.7 2.0 copy-start.2
  362.7 3.5 copy-start.7
  362.7 3.5 copy-start.20
  362.7 3.5 copy-start.22
  364.6 106.4 %collective-permute-start.6 = (bf16[512,768]{1,0:T(8,128)(2,1)}, bf16[512,768]{1,0:T(8,128)(2,1)}, u32[]{:S(2)}, u32[]{:S(2)}) collective-permute-start(bf16[512,768]{1,0:T(8,128)(2,1)} %add_convert_fusion), channel_id=1, source_target_pairs={{0,16},{1,17},{2,18},{3,19},{4,20},{5,21},{6,22},{7,23},{8,24},{9,... | collective-permute-start | bytes 2359304 | tf_op jit(solution)/shard_map/ppermute | solution.py:1265
  471.0 224.1 %reduce-scatter.5.cloned.1.call-start = ((), (), s32[]{:S(2)}) async-start(), calls=%async_computation.4 | async-start | bytes 4718592 | tf_op jit(solution)/shard_map/reduce_scatter | solution.py:1318
  471.2 3.5 copy-start.8
  471.3 4.1 copy-start.17
  474.6 4.5 copy-start.10
  474.6 4.5 collective-permute-start.8
  474.6 41.4 %collective-permute-start.9 = (bf16[512,768]{1,0:T(8,128)(2,1)}, bf16[512,768]{1,0:T(8,128)(2,1)}, u32[]{:S(2)}, u32[]{:S(2)}) collective-permute-start(bf16[512,768]{1,0:T(8,128)(2,1)} %add_convert_fusion.1), channel_id=1, source_target_pairs={{0,16},{1,17},{2,18},{3,19},{4,20},{5,21},{6,22},{7,23},{8,24},{9,... | collective-permute-start | bytes 2359304 | tf_op jit(solution)/shard_map/ppermute | solution.py:1265
  479.1 1.5 copy-start.11
  480.6 52.4 %collective-permute-start.10 = (bf16[512,512]{1,0:T(8,128)(2,1)}, bf16[512,512]{1,0:T(8,128)(2,1)S(1)}, u32[]{:S(2)}, u32[]{:S(2)}) collective-permute-start(bf16[512,512]{1,0:T(8,128)(2,1)} %add_convert_fusion.3), channel_id=1, source_target_pairs={{0,16},{1,17},{2,18},{3,19},{4,20},{5,21},{6,22},{7,23},{8,24},{9,... | collective-permute-start | bytes 1572872 | tf_op jit(solution)/shard_map/ppermute | solution.py:1265
  533.0 7.2 copy-start.12
  540.2 12.6 %collective-permute-start.11 = (bf16[1024,1536]{1,0:T(8,128)(2,1)}, bf16[1024,1536]{1,0:T(8,128)(2,1)}, u32[]{:S(2)}, u32[]{:S(2)}) collective-permute-start(bf16[1024,1536]{1,0:T(8,128)(2,1)} %weight_grad.7), channel_id=1, source_target_pairs={{0,1},{1,0},{2,3},{3,2},{4,5},{5,4},{6,7},{7,6},{8,9},{9,8},{10,11... | collective-permute-start | bytes 9437192 | tf_op jit(solution)/shard_map/ppermute | solution.py:1309
  559.8 139.2 %collective-permute-start.14 = (bf16[512,1536]{1,0:T(8,128)(2,1)}, bf16[512,1536]{1,0:T(8,128)(2,1)}, u32[]{:S(2)}, u32[]{:S(2)}) collective-permute-start(bf16[512,1536]{1,0:T(8,128)(2,1)} %weight_grad.8), channel_id=1, source_target_pairs={{0,16},{1,17},{2,18},{3,19},{4,20},{5,21},{6,22},{7,23},{8,24},{9,... | collective-permute-start | bytes 4718600 | tf_op jit(solution)/shard_map/ppermute | solution.py:1265
  562.1 4.6 copy-start.15
  562.1 6.1 copy-start.14
  570.9 2.2 copy-start
  570.9 2.2 copy-start.23
  570.9 2.2 copy-start.24
  575.9 2.0 collective-permute-start.12
  577.9 116.4 %collective-permute-start.13 = (f32[512,128]{1,0:T(8,128)S(1)}, f32[512,128]{1,0:T(8,128)S(1)}, u32[]{:S(2)}, u32[]{:S(2)}) collective-permute-start(f32[512,128]{1,0:T(8,128)S(1)} %slice.145), channel_id=1, source_target_pairs={{0,16},{1,17},{2,18},{3,19},{4,20},{5,21},{6,22},{7,23},{8,24},{9,... | collective-permute-start | bytes 786440 | tf_op jit(solution)/shard_map/ppermute | solution.py:1365
Sparse Core Ops, SparseCore 0:
  133.9 123.5 all-gather.1
  471.1 85.0 reduce-scatter.2
  558.6 120.3 reduce-scatter.4

commit v4 on v3

--- a/solution.py
+++ b/solution.py
@@ -707,14 +707,20 @@
 
 
 def mul(left, right, axes):
-    left_high, left_low = halves(left)
-    right_high, right_low = halves(right)
-    return dot(left_high, right_high, axes) + (dot(left_high, right_low, axes) + dot(left_low, right_high, axes))
+    (left_axis,), (right_axis,) = axes
+    both = jnp.concatenate(halves(right), axis=1 - right_axis)
+    total = dot(
+        jnp.concatenate(halves(left), axis=left_axis), jnp.concatenate([both, both], axis=right_axis), axes
+    )
+    width = right.shape[1 - right_axis]
+    return total[:, :width] + total[:, width:]
 
 
 def mul_mask(mask, right, axes):
-    right_high, right_low = halves(right)
-    return dot(mask, right_high, axes) + dot(mask, right_low, axes)
+    (left_axis,), (right_axis,) = axes
+    return dot(
+        jnp.concatenate([mask, mask], axis=left_axis), jnp.concatenate(halves(right), axis=right_axis), axes
+    )
 
 
 NN = ((1,), (0,))
@@ -817,21 +823,36 @@
         self.gate = p_ref[:, g_at : g_at + DV]
 
 
-def mixer_kernel(rank_ref, scalars, seg_ref, p_ref, taps_ref, gain_ref, z_ref, inv_ref, upd_ref):
-    seq = Sequence(seg_ref[0, :1])
+TOGETHER = 4
+TOGETHER_BACK = 2
+
+
+def in_turns(bodies):
+    bodies = list(bodies)
+    while bodies:
+        bodies = [body for body in bodies if next(body, None) is not None]
+
+
+def mixer_kernel(tokens, rank_ref, scalars, seg_ref, p_ref, taps_ref, gain_ref, z_ref, inv_ref, upd_ref):
     rank = rank_ref[0]
-    ones = [Head(seq, head, rank, scalars, p_ref, taps_ref) for head in range(HEADS)]
-    inverses = unit_lower_inverses([one.lower for one in ones], seq.row, seq.col)
+    places = [(at, head) for at in range(TOGETHER) for head in range(HEADS)]
+    seqs = [Sequence(seg_ref[at, :1]) for at in range(TOGETHER)]
+    ones = [
+        Head(seqs[at], head, rank, scalars, p_ref.at[pl.ds(at * tokens, tokens)], taps_ref) for at, head in places
+    ]
+    inverses = unit_lower_inverses([one.lower for one in ones], seqs[0].row, seqs[0].col)
     updates = [mul(inverse, one.beta * one.v, NN) for inverse, one in zip(inverses, ones)]
     outs = [mul(one.attend, update, NN) for one, update in zip(ones, updates)]
-    for head, (one, inverse, update, out) in enumerate(zip(ones, inverses, updates, outs)):
+    for (at, head), one, inverse, update, out in zip(places, ones, inverses, updates, outs):
         normed = out * norm_scale(out, EPS_GATED) * gain_ref[...]
-        z_ref[:, head * DV : (head + 1) * DV] = (normed * (one.gate * jax.nn.sigmoid(one.gate))).astype(BF)
-        inv_ref[0, head] = inverse
-        upd_ref[0, head] = update
-
-
-def mixer_back_kernel(rank_ref, scalars, seg_ref, p_ref, taps_ref, gain_ref, inv_ref, upd_ref, dz_ref,
+        z_ref[pl.ds(at * tokens, tokens), head * DV : (head + 1) * DV] = (
+            normed * (one.gate * jax.nn.sigmoid(one.gate))
+        ).astype(BF)
+        inv_ref[at, head] = inverse
+        upd_ref[at, head] = update
+
+
+def mixer_back_kernel(tokens, rank_ref, scalars, seg_ref, p_ref, taps_ref, gain_ref, inv_ref, upd_ref, dz_ref,
                       dp_ref, dtaps_ref, dgain_ref, dscal_ref):
     @pl.when(pl.program_id(0) == 0)
     def _():
@@ -839,64 +860,94 @@
         dgain_ref[...] = jnp.zeros_like(dgain_ref)
         dscal_ref[...] = jnp.zeros_like(dscal_ref)
 
-    seq = Sequence(seg_ref[0, :1])
     rank = rank_ref[0]
-    pair_grad = jnp.zeros((seq.tokens, EXTRA), F32)
-    lane = lax.broadcasted_iota(jnp.int32, (seq.tokens, EXTRA), 1)
+    lane = lax.broadcasted_iota(jnp.int32, (tokens, EXTRA), 1)
     scal_row = lax.broadcasted_iota(jnp.int32, (8, 128), 0)
     scal_col = lax.broadcasted_iota(jnp.int32, (8, 128), 1)
-    scal = jnp.zeros((8, 128), F32)
-    for head in range(HEADS):
-        one = Head(seq, head, rank, scalars, p_ref, taps_ref)
-        inverse = inv_ref[0, head]
-        update = upd_ref[0, head]
+    pair_grads = [jnp.zeros((tokens, EXTRA), F32) for _ in range(TOGETHER_BACK)]
+    scal = [jnp.zeros((8, 128), F32)]
+    sums = {}
+
+    def add_to(key, value):
+        sums[key] = sums[key] + value if key in sums else value
+
+    def body(at, seq, head):
+        mine = pl.ds(at * tokens, tokens)
+        one = Head(seq, head, rank, scalars, p_ref.at[mine], taps_ref)
+        yield True
+        inverse = inv_ref[at, head]
+        update = upd_ref[at, head]
         out = mul(one.attend, update, NN)
-        dz = dz_ref[:, head * DV : (head + 1) * DV]
+        yield True
+        dz = dz_ref[mine, head * DV : (head + 1) * DV]
         scale = norm_scale(out, EPS_GATED)
         normed = out * scale
         sig = jax.nn.sigmoid(one.gate)
         gate = one.gate * sig
         d_gate = dz * normed * gain_ref[...] * (sig * (1 + one.gate * (1 - sig)))
-        dp_ref[:, one.g_at : one.g_at + DV] = d_gate.astype(BF)
-        dgain_ref[...] += jnp.sum(dz * normed * gate, axis=0, keepdims=True)
+        dp_ref[mine, one.g_at : one.g_at + DV] = d_gate.astype(BF)
+        add_to("gain", jnp.sum(dz * normed * gate, axis=0, keepdims=True))
         d_normed = dz * gain_ref[...] * gate
         d_out = scale * (d_normed - normed * jnp.mean(d_normed * normed, axis=1, keepdims=True))
+        yield True
+        d_update = mul(one.attend, d_out, TN)
+        yield True
         d_attend = jnp.where(seq.inclusive, mul(d_out, update, NT), 0.0)
-        d_update = mul(one.attend, d_out, TN)
+        yield True
         d_scaled = mul(inverse, d_update, TN)
+        yield True
+        d_qk = d_attend * one.pairs
+        d_q = mul(d_qk, one.k, NN)
+        yield True
         d_lower = jnp.where(seq.strict, -mul(d_scaled, update, NT), 0.0)
+        yield True
+        d_k = mul(d_qk, one.q, TN)
         d_v = one.beta * d_scaled
         d_beta = jnp.sum(d_scaled * one.v, axis=1, keepdims=True) + jnp.sum(
             d_lower * one.strict_pairs * one.kk, axis=1, keepdims=True
         )
         d_gap = d_attend * one.attend + d_lower * one.lower
-        d_qk = d_attend * one.pairs
         d_kk = d_lower * (one.beta * one.strict_pairs)
-        d_q = mul(d_qk, one.k, NN)
-        d_k = mul(d_qk, one.q, TN) + mul(d_kk, one.k, NN) + mul(d_kk, one.k, TN)
+        yield True
+        d_k = d_k + mul(d_kk, one.k, NN) + mul(d_kk, one.k, TN)
+        yield True
         reach = mul_mask(seq.lower, d_gap, TN)
+        yield True
         d_decay = jnp.sum(jnp.where(seq.row > seq.col, reach, 0.0), axis=1, keepdims=True)
         d_a = d_decay * (-one.rate) * jax.nn.sigmoid(one.a)
         d_b = d_beta * one.beta * (1 - one.beta)
-        pair_grad = pair_grad + jnp.where(lane == one.lane_a, d_a, 0.0) + jnp.where(lane == one.lane_b, d_b, 0.0)
+        pair_grads[at] = (
+            pair_grads[at] + jnp.where(lane == one.lane_a, d_a, 0.0) + jnp.where(lane == one.lane_b, d_b, 0.0)
+        )
         sum_rate = jnp.sum(d_decay * one.decay, axis=0, keepdims=True)
         sum_a = jnp.sum(d_a, axis=0, keepdims=True)
-        scal = scal + jnp.where((scal_row == 0) & (scal_col == head), sum_rate, 0.0)
-        scal = scal + jnp.where((scal_row == 0) & (scal_col == HEADS + head), sum_a, 0.0)
+        scal[0] = scal[0] + jnp.where((scal_row == 0) & (scal_col == head), sum_rate, 0.0)
+        scal[0] = scal[0] + jnp.where((scal_row == 0) & (scal_col == HEADS + head), sum_a, 0.0)
         dq_unit = d_q * DK**-0.5
         dc_q = one.q_scale * (dq_unit - one.q_unit * jnp.sum(dq_unit * one.q_unit, axis=1, keepdims=True))
         dc_k = one.k_scale * (d_k - one.k * jnp.sum(d_k * one.k, axis=1, keepdims=True))
-        for grad, pre, sig, raw, taps, at, width in (
+        for grad, pre, sig, raw, taps, first, width in (
             (dc_q, one.pre[0], one.sig[0], one.raw[0], one.taps[0], one.q_at, DK),
             (dc_k, one.pre[1], one.sig[1], one.raw[1], one.taps[1], one.k_at, DK),
             (d_v, one.pre[2], one.sig[2], one.raw[2], one.taps[2], one.v_at, DV),
         ):
             d_pre = grad * (sig * (1 + pre * (1 - sig)))
             d_raw, d_taps = seq.conv_back(taps, raw, d_pre)
-            dp_ref[:, at : at + width] = d_raw.astype(BF)
-            dtaps_ref[:, at : at + width] += d_taps
-    dp_ref[:, 2 * QW + 2 * VW :] = pair_grad.astype(BF)
-    dscal_ref[...] += scal
+            dp_ref[mine, first : first + width] = d_raw.astype(BF)
+            add_to((first, width), d_taps)
+            yield True
+
+    seqs = [Sequence(seg_ref[at, :1]) for at in range(TOGETHER_BACK)]
+    in_turns(body(at, seqs[at], head) for at in range(TOGETHER_BACK) for head in range(HEADS))
+    for key, value in sums.items():
+        if key == "gain":
+            dgain_ref[...] += value
+        else:
+            first, width = key
+            dtaps_ref[:, first : first + width] += value
+    for at in range(TOGETHER_BACK):
+        dp_ref[pl.ds(at * tokens, tokens), 2 * QW + 2 * VW :] = pair_grads[at].astype(BF)
+    dscal_ref[...] += scal[0]
 
 
 def smem_spec():
@@ -919,19 +970,20 @@
     count = p.shape[0] // tokens
     shape = jax.ShapeDtypeStruct
     return pl.pallas_call(
-        mixer_kernel,
-        grid=(count,),
+        functools.partial(mixer_kernel, tokens),
+        grid=(count // TOGETHER,),
         out_shape=(
             shape((p.shape[0], VW), BF),
             shape((count, HEADS, tokens, tokens), F32),
             shape((count, HEADS, tokens, DV), F32),
         ),
         in_specs=[
-            smem_spec(), smem_spec(), by_sequence(1, 8, tokens), by_sequence(tokens, MIXW),
+            smem_spec(), smem_spec(), by_sequence(TOGETHER, 8, tokens), by_sequence(TOGETHER * tokens, MIXW),
             whole_block(CONV, CHANNELS), whole_block(1, DV),
         ],
         out_specs=[
-            by_sequence(tokens, VW), by_sequence(1, HEADS, tokens, tokens), by_sequence(1, HEADS, tokens, DV),
+            by_sequence(TOGETHER * tokens, VW), by_sequence(TOGETHER, HEADS, tokens, tokens),
+            by_sequence(TOGETHER, HEADS, tokens, DV),
         ],
         compiler_params=pltpu.CompilerParams(vmem_limit_bytes=BIG),
         cost_estimate=takes(5),
@@ -943,8 +995,8 @@
     count = p.shape[0] // tokens
     shape = jax.ShapeDtypeStruct
     return pl.pallas_call(
-        mixer_back_kernel,
-        grid=(count,),
+        functools.partial(mixer_back_kernel, tokens),
+        grid=(count // TOGETHER_BACK,),
         out_shape=(
             shape((p.shape[0], MIXW), BF),
             shape((CONV, CHANNELS), F32),
@@ -952,12 +1004,14 @@
             shape((8, 128), F32),
         ),
         in_specs=[
-            smem_spec(), smem_spec(), by_sequence(1, 8, tokens), by_sequence(tokens, MIXW),
+            smem_spec(), smem_spec(), by_sequence(TOGETHER_BACK, 8, tokens), by_sequence(TOGETHER_BACK * tokens, MIXW),
             whole_block(CONV, CHANNELS), whole_block(1, DV),
-            by_sequence(1, HEADS, tokens, tokens), by_sequence(1, HEADS, tokens, DV), by_sequence(tokens, VW),
+            by_sequence(TOGETHER_BACK, HEADS, tokens, tokens), by_sequence(TOGETHER_BACK, HEADS, tokens, DV),
+            by_sequence(TOGETHER_BACK * tokens, VW),
         ],
         out_specs=[
-            by_sequence(tokens, MIXW), whole_block(CONV, CHANNELS), whole_block(1, DV), whole_block(8, 128),
+            by_sequence(TOGETHER_BACK * tokens, MIXW), whole_block(CONV, CHANNELS), whole_block(1, DV),
+            whole_block(8, 128),
         ],
         compiler_params=pltpu.CompilerParams(vmem_limit_bytes=BIG),
         cost_estimate=takes(5),
@@ -1082,7 +1136,7 @@
 
 def project(x, w):
     count = x.shape[0]
-    rows = 256
+    rows = 512 if count % 512 == 0 else 256
     shape = jax.ShapeDtypeStruct
     return pl.pallas_call(
         project_kernel,
@@ -1270,7 +1324,6 @@
 
     down_half, down_got = first_half(dy_all, activated)
     down_half, activated = together((down_half, activated))
-    feed = dot(activated, w_down, NT).astype(BF)
     d_act = dot(dy_all, w_down, NN)
     d_gate = d_act * up_part * sigmoid_gate * (1 + gate_part * (1 - sigmoid_gate))
     d_up = d_act * gate_part * sigmoid_gate
@@ -1289,9 +1342,11 @@
         copies, d_normed_two.reshape(RANKS, tokens, D), hidden, dy, gain_two
     )
     d_hidden_all = d_hidden_all.reshape(group_tokens, D)
-    d_hidden_all, up_landed, gate_away, down_landed, feed = together(
-        (d_hidden_all, up_landed, gate_away, down_landed, feed)
+    d_hidden_all, up_landed, gate_away, down_landed, activated = together(
+        (d_hidden_all, up_landed, gate_away, down_landed, activated)
     )
+    feed = dot(activated, w_down, NT).astype(BF)
+    feed, d_hidden_all = together((feed, d_hidden_all))
     feed = lax.psum_scatter(feed, axes, axis_index_groups=cubes, scatter_dimension=0, tiled=True)
     gate_landed = to_copies(gate_away)
     out_half, out_got = first_half(d_hidden_all, gated)
@@ -1303,35 +1358,30 @@
     d_mix, d_taps, d_out_gain, d_scalars = mixer_back(
         rank_arg, scalars, seg_all, p, taps, out_gain, inverse, update, d_gated, tokens
     )
-    d_mix, gate_landed, out_landed = together((d_mix, gate_landed, out_landed))
+
+    def own_rows(left, right, got, column, landed, count=None):
+        adds = ((got, 0, column),) + tuple((one, 0, 0) for one in landed)
+        total = weight_grad(left, right, 0, block_rows, adds, count)
+        return total.reshape(RANKS, rows, total.shape[1])
+
     mix_columns = MIXW - EXTRA
     mix_half = weight_grad(normed, d_mix, 1, half, (), mix_columns)
     mix_got = lax.ppermute(mix_half, axes, core_pairs)
-    mix_half, d_mix = together((mix_half, d_mix))
-    d_normed, gain_one_grad = input_back(d_mix, w_mix, x_all, x_scale)
-    gain_one_grad = gain_one_grad[0]
-    d_normed, gain_one_grad, mix_got = together((d_normed, gain_one_grad, mix_got))
+    mix_half, d_mix, gate_landed, out_landed = together((mix_half, d_mix, gate_landed, out_landed))
     mix_away = [
         weight_grad(normed, d_mix, at, block_rows, ((mix_got, at, 0),), mix_columns) for at in range(1, copies)
     ]
     mix_landed = to_copies(mix_away)
+    mix_away, d_mix, d_gate_part, d_up_part, activated, gated, d_taps, d_scalars, d_out_gain, gain_two_grad = together(
+        (mix_away, d_mix, d_gate_part, d_up_part, activated, gated, d_taps, d_scalars, d_out_gain, gain_two_grad)
+    )
+    d_normed, gain_one_grad = input_back(d_mix, w_mix, x_all, x_scale)
+    gain_one_grad = gain_one_grad[0]
     d_input = lax.psum_scatter(d_normed, axes, axis_index_groups=cubes, scatter_dimension=0, tiled=True)
-    mix_away, d_gate_part, d_up_part, activated, gated = together(
-        (mix_away, d_gate_part, d_up_part, activated, gated)
-    )
-
-    def own_rows(left, right, got, column, landed, count=None):
-        adds = ((got, 0, column),) + tuple((one, 0, 0) for one in landed)
-        total = weight_grad(left, right, 0, block_rows, adds, count)
-        return total.reshape(RANKS, rows, total.shape[1])
-
     up_rows = own_rows(normed_two, d_up_part, gate_got, FW, up_landed)
+    down_rows = own_rows(dy_all, activated, down_got, 0, down_landed)
     gate_rows = own_rows(normed_two, d_gate_part, gate_got, 0, gate_landed)
-    down_rows = own_rows(dy_all, activated, down_got, 0, down_landed)
     out_rows = own_rows(d_hidden_all, gated, out_got, 0, out_landed)
-    out_rows, d_taps, d_scalars, d_out_gain, gain_two_grad = together(
-        (out_rows, d_taps, d_scalars, d_out_gain, gain_two_grad)
-    )
     tap_grad = jnp.zeros((CONV, tap_rows, conv_cols), F32)
     at = 0
     for first, width in ranges:
@@ -1367,14 +1417,6 @@
     ]
     extra_sum, out_rows = together((extra_sum, out_rows))
     grads_rest = home_rest(copies, (out_rows, gate_rows, up_rows, down_rows))
-    if in_place:
-        output, input_grad = finish(
-            jnp.stack([core, dp]).astype(jnp.int32), copies, hidden, feed, d_input, x, d_hidden, gain_one
-        )
-    else:
-        output = order.plain((hidden + feed.astype(F32)).astype(BF), 1)
-        back, _ = norm_back(d_input.astype(F32), x.astype(F32), gain_one, EPS_NORM)
-        input_grad = order.plain((d_hidden + back).astype(BF), 1)
     extra_rows = extra_sum[:block_rows]
     for one in extra_landed:
         extra_rows = extra_rows + one
@@ -1385,9 +1427,18 @@
     state = (moment_one, moment_two, master)
     done = adam(adam_scalars, grads_rest, state, None, MIX_END, 2048, 4)
     done = adam(adam_scalars, grads_rest, state, done, MIX_END + 4 * 2048, 2560, 5)
-    done, extra_rows, output, input_grad, normed = together((done, extra_rows, output, input_grad, normed))
+    done, extra_rows, normed = together((done, extra_rows, normed))
     mix_rows = own_rows(normed, d_mix, mix_got, 0, mix_landed, mix_columns)
     grads_mix, extra_rows = home(copies, mix_rows, extra_rows.reshape(RANKS, rows, EXTRA))
+    grads_mix, d_input, feed = together((grads_mix, d_input, feed))
+    if in_place:
+        output, input_grad = finish(
+            jnp.stack([core, dp]).astype(jnp.int32), copies, hidden, feed, d_input, x, d_hidden, gain_one
+        )
+    else:
+        output = order.plain((hidden + feed.astype(F32)).astype(BF), 1)
+        back, _ = norm_back(d_input.astype(F32), x.astype(F32), gain_one, EPS_NORM)
+        input_grad = order.plain((d_hidden + back).astype(BF), 1)
     done = adam(adam_scalars, extra_rows, state, done, EXTRA_START, EXTRA, 1)
     done = adam(adam_scalars, grads_mix, state, done, 0, 2048, 6)
     gain_grads = extra_rows[:, 2 * H : 2 * H + 2]

time: 765 us -> 797 us (1.042)
  waiting for transfers between devices: 21.9 us -> 60.7 us
  Pallas kernels: 591 us -> 583 us
    ppermute x5, waiting for transfers between devices: 17 us -> 55.6 us  [to_copies(): lax.ppermute(one, axes, pairs)]
    pallas_call x2, Pallas kernels: 63.7 us -> 36.1 us  [the longest x1 21.1 us: mixer_back(): pl.pallas_call(functools.partial(mixer_back_kernel, tokens), grid=(count...]
    pallas_call x1, Pallas kernels: 97.7 us -> 113 us  [branch(): pl.pallas_call(functools.partial(branch_kernel, copies, row_parts(tokens,...]
  transfers between devices with their start and end apart: 18 -> 18, of which waited for: 3 -> 4; matrix products, arithmetic and copies ran while one was open for 12% -> 11% of each run, Pallas kernels for 55% -> 56%
where the time goes in v4:
time: 797 us; the launch traced here: 786 us
  Pallas kernels  583 us (73%)
  matrix products  69.9 us (9%)
  waiting for transfers between devices  60.7 us (8%)
  starting transfers between devices  28.4 us (4%)
  local copies, waits for them, and re-layouts  20.7 us (3%)
  between operations  17.3 us (2%)
    pallas_call x1, Pallas kernels, spread(): pl.pallas_call(functools.partial(spread_kernel, copies, ((0, tokens // 2)...  125 us
    pallas_call x1, Pallas kernels, branch(): pl.pallas_call(functools.partial(branch_kernel, copies, row_parts(tokens,...  113 us
    pallas_call x1, Pallas kernels, hidden_back(): pl.pallas_call(functools.partial(hidden_back_kernel, copies, row_parts(to...  103 us
    pallas_call x1, Pallas kernels, home_rest(): pl.pallas_call(functools.partial(home_rest_kernel, copies), out_shape=jax...  78.8 us
    dot_general x14, matrix products, dot(): lax.dot_general(left, right, (axes, ((), ())), preferred_element_type=F32)  69.9 us
    ppermute x5, waiting for transfers between devices, to_copies(): lax.ppermute(one, axes, pairs)  55.6 us
    pallas_call x7, Pallas kernels, weight_grad(): pl.pallas_call(weight_grad_kernel, grid=(count // tile,), out_shape=jax.S...  33.1 us
    pallas_call x4, Pallas kernels, adam(): pl.pallas_call(functools.partial(adam_kernel, len(filled)), grid=(count,)...  31.8 us
  transfers between devices with their start and end apart: 18, of which 4 were waited for; matrix products, arithmetic and copies ran while one was open for 11% of the time, Pallas kernels for 56%

profile of v4, /device:TPU:0, one launch (start us, length us, event | category | flops | bytes accessed | tf_op | source)
XLA Modules:
  0.0 786.3 jit_solution(15319603877554791066)
XLA Ops:
  7.2 1.2 broadcast_in_dim.91.s_ref
  8.5 125.3 %spread.1 = (bf16[2,2,8,64,1664]{4,3,2,1,0:T(8,128)(2,1)}, bf16[2,2,8,64,512]{4,3,2,1,0:T(8,128)(2,1)}, bf16[8,64,1536]{2,1,0:T(8,128)(2,1)}, bf16[8,64,768]{2,1...) custom-call(bf16[64,33408]{1,0:T(8,128)(2,1)} %w_ref.1, ...), custom_call_target="tpu_custom_call" | custom-call | bytes 5000 | tf_op jit(solution)/shard_map/spread/pallas_call | solution.py:441
  133.8 17.5 %collective-permute-start.1 = (bf16[512,768]{1,0:T(8,128)(2,1)}, bf16[512,768]{1,0:T(8,128)(2,1)}, u32[]{:S(2)}, u32[]{:S(2)}) collective-permute-start(bf16[512,768]{1,0:T(8,128)(2,1)} %bitcast.94), channel_id=1, source_target_pairs={{0,16},{1,17},{2,18},{3,19},{4,20},{5,21},{6,22},{7,23},{8,24},{9,... | collective-permute-start | bytes 2359304 | tf_op jit(solution)/shard_map/ppermute | solution.py:1250
  155.2 14.5 %project.1 = (bf16[1024,2048]{1,0:T(8,128)(2,1)}, f32[1024,1664]{1,0:T(8,128)}, f32[8,2048]{1,0:T(8,128)}, f32[1024,128]{1,0:T(8,128)}) custom-call(bf16[1024,2048]{1,0:T(8,128)(2,1)} %bitcast.62, bf16[2048,1664]{1,0:T(8,128)(2,1)} %bitcast.60), custom_call_target="tpu_custom_call" | custom-call | bytes 1000 | tf_op jit(solution)/shard_map/project/pallas_call | solution.py:1141
  171.0 15.0 %mixer.1 = (bf16[1024,512]{1,0:T(8,128)(2,1)}, f32[8,2,128,128]{3,2,1,0:T(8,128)}, f32[8,2,128,256]{3,2,1,0:T(8,128)}) custom-call(s32[1]{0:T(128)} %bitcast.2.rank_ref, f32[4]{0:T(128)} %pad_maximum_fusion.6.scalars, s32[8,8,128]{2,1,0:T(8,128)} %get-tuple-element.103.seg_ref, f32[1024,1664]{1,0:T(8,128)} %get-tuple-element.105.p_ref, ...), custom_call_target="tpu_custom_call" | custom-call | bytes 5000 | tf_op jit(solution)/shard_map/mixer/pallas_call | solution.py:972
  186.1 1.5 fusion.44
  187.6 5.6 convolution_convert_fusion.1
  193.2 113.2 %branch.1 = (f32[128,2048]{1,0:T(8,128)}, bf16[8,128,2048]{2,1,0:T(8,128)(2,1)}) custom-call(bf16[8,128,2048]{2,1,0:T(8,128)(2,1)} %bitcast.75, bf16[128,2048]{1,0:T(8,128)(2,1)} %get-tuple-element.108.x_ref, f32[1,2048]{1,0:T(1,128)} %get-tuple-element.219.gain_ref), custom_call_target="tpu_custom_call" | custom-call | bytes 5000 | tf_op jit(solution)/shard_map/branch/pallas_call | solution.py:521
  307.2 3.1 collective-permute-done.3
  310.3 9.8 %fusion.14 = f32[1024,1536]{1,0:T(8,128)S(1)} fusion(bf16[1024,2048]{1,0:T(8,128)(2,1)} %bitcast.64, bf16[512,1536]{1,0:T(8,128)(2,1)} %collective-permute-done.3, bf16[512,1536]{1,0:T(8,128)(2,1)} %bitcast.92, bf16[512,1536]{1,0:T(8,128)(2,1)} %collective-permute-done, bf16[512,1536]{1,0:T(8,128)(2,1)S(1)} %bitcast.91), kind=kOutput, calls=%fused_computation.35 | convolution fusion | flops 6467616768 | bytes 16777216 | tf_op jit(solution)/shard_map/dot_general | solution.py:701
  320.1 2.7 copy-done.3
  323.8 4.1 fusion.8
  328.2 8.0 %add_multiply_fusion = (bf16[1024,768]{1,0:T(8,128)(2,1)S(1)}, bf16[1024,768]{1,0:T(8,128)(2,1)S(1)}) fusion(f32[1024,1536]{1,0:T(8,128)S(1)} %copy-done.4, bf16[1024,2048]{1,0:T(8,128)(2,1)} %all-gather.2.cloned.1.call-done.left_ref, bf16[512,768]{1,0:T(8,128)(2,1)} %collective-permute-done.2, bf16[512,768]{1,0:T(8,128)(2,1)S(1)} %bitcast.98, ...), kind=kOutput, calls=%fused_computation.10 | convolution fusion | flops 3244032000 | bytes 16777216 | tf_op jit(solution)/shard_map/dot_general | solution.py:701
  336.9 1.6 copy-done.1
  338.4 5.1 convolution_convert_fusion.3
  343.8 3.7 add_convert_fusion.2
  348.0 11.5 %convolution_convert_fusion = bf16[1024,2048]{1,0:T(8,128)(2,1)} fusion(bf16[1024,1536]{1,0:T(8,128)(2,1)S(1)} %fusion, bf16[512,1536]{1,0:T(8,128)(2,1)} %collective-permute-done.3, bf16[512,1536]{1,0:T(8,128)(2,1)} %bitcast.93, bf16[512,1536]{1,0:T(8,128)(2,1)} %collective-permute-done, bf16[512,1536]{1,0:T(8,128)(2,1)} %bitcast.90), kind=kOutput, calls=%fused_computation.3 | convolution fusion | flops 6469713920 | bytes 13631488 | tf_op jit(solution)/shard_map/dot_general | solution.py:701
  359.5 2.0 add_convert_fusion
  361.5 2.0 add_convert_fusion.1
  363.5 2.5 collective-permute-start.6
  366.0 102.9 %hidden_back.1 = (f32[128,2048]{1,0:T(8,128)}, f32[1,2048]{1,0:T(1,128)}, bf16[8,128,2048]{2,1,0:T(8,128)(2,1)}) custom-call(bf16[8,128,2048]{2,1,0:T(8,128)(2,1)} %bitcast.76, f32[128,2048]{1,0:T(8,128)} %get-tuple-element.110.h_ref.hidden_ref, bf16[128,2048]{1,0:T(8,128)(2,1)} %get-tuple-element.118.dy_ref, f32[1,2048]{1,0:T(1,128)} %get-tuple-element.219.gain_ref), custom_call_target="tpu_custom_call" | custom-call | bytes 5000 | tf_op jit(solution)/shard_map/hidden_back/pallas_call | solution.py:564
  468.9 7.8 convolution_convert_fusion.2
  477.2 3.3 fusion.11
  481.0 3.6 fusion.46.dz_ref
  485.7 21.1 %mixer_back.1 = (bf16[1024,1664]{1,0:T(8,128)(2,1)}, f32[4,1024]{1,0:T(4,128)}, f32[1,256]{1,0:T(1,128)}, f32[8,128]{1,0:T(8,128)}) custom-call(s32[1]{0:T(128)} %bitcast.2.rank_ref, f32[4]{0:T(128)} %pad_maximum_fusion.6.scalars, s32[8,8,128]{2,1,0:T(8,128)} %get-tuple-element.103.seg_ref, f32[1024,1664]{1,0:T(8,128)} %get-tuple-element.105.p_ref, ...), custom_call_target="tpu_custom_call" | custom-call | bytes 5000 | tf_op jit(solution)/shard_map/mixer_back/pallas_call | solution.py:997
  506.8 7.0 weight_grad.7
  514.9 2.0 collective-permute-start.10
  516.8 1.9 fusion.43
  518.7 34.3 %collective-permute-done.9.refs_1_ = bf16[512,768]{1,0:T(8,128)(2,1)} collective-permute-done((bf16[512,768]{1,0:T(8,128)(2,1)}, bf16[512,768]{1,0:T(8,128)(2,1)}, u32[]{:S(2)}, u32[]{:S(2)}) %collective-permute-start.9) | collective-permute-done | bytes 786464 | tf_op jit(solution)/shard_map/ppermute | solution.py:1319
  553.0 21.3 %collective-permute-done.10.refs_1_ = bf16[512,512]{1,0:T(8,128)(2,1)} collective-permute-done((bf16[512,512]{1,0:T(8,128)(2,1)S(1)}, bf16[512,512]{1,0:T(8,128)(2,1)}, u32[]{:S(2)}, u32[]{:S(2)}) %collective-permute-start.10) | collective-permute-done | bytes 524320 | tf_op jit(solution)/shard_map/ppermute | solution.py:1319
  574.3 5.0 weight_grad.8
  579.3 12.5 %input_back.1 = (bf16[1024,2048]{1,0:T(8,128)(2,1)}, f32[1,2048]{1,0:T(1,128)}) custom-call(bf16[1024,1664]{1,0:T(8,128)(2,1)} %get-tuple-element.142.right_ref.grad_ref, bf16[2048,1664]{1,0:T(8,128)(2,1)} %bitcast.61, bf16[1024,2048]{1,0:T(8,128)(2,1)} %bitcast.63, f32[1024,128]{1,0:T(8,128)} %get-tuple-element.143.scale_ref), custom_call_target="tpu_custom_call" | custom-call | bytes 1000 | tf_op jit(solution)/shard_map/input_back/pallas_call | solution.py:1101
  597.4 1.7 fusion.19
  599.6 2.7 fusion.2
  602.4 1.9 collective-permute-done.12
  604.4 3.0 collective-permute-start.13
  611.4 4.1 weight_grad.12
  615.5 4.2 weight_grad.11
  619.7 4.1 weight_grad.10
  623.8 3.4 weight_grad.9
  627.2 78.8 %home_rest.1.grad_ref = bf16[64,33280]{1,0:T(8,128)(2,1)} custom-call(bf16[8,64,512]{2,1,0:T(8,128)(2,1)} %bitcast.80, bf16[8,64,768]{2,1,0:T(8,128)(2,1)} %bitcast.79, bf16[8,64,768]{2,1,0:T(8,128)(2,1)} %bitcast.78, bf16[8,64,768]{2,1,0:T(8,128)(2,1)} %bitcast.77), custom_call_target="tpu_custom_call" | custom-call | bytes 5000 | tf_op jit(solution)/shard_map/home_rest/pallas_call | solution.py:688
  706.0 7.6 adam.4
  713.6 11.8 %adam.5 = (f32[64,33408]{1,0:T(8,128)}, f32[64,33408]{1,0:T(8,128)}, f32[64,33408]{1,0:T(8,128)}, f32[64,33408]{1,0:T(8,128)}, bf16[64,33408]{1,0:T(8,128)(2,1)}) custom-call(f32[5]{0:T(128)} %stack.17.scalars, bf16[64,33280]{1,0:T(8,128)(2,1)} %home_rest.1.grad_ref, ...), custom_call_target="tpu_custom_call", output_to_operand_aliasing={{0}: (5, {}), {1}: (6, {}), {2}: (7, {}), {3}: (8, {}), {4}... | custom-call | bytes 5000 | tf_op jit(solution)/shard_map/adam/pallas_call | solution.py:1045
  726.1 5.3 weight_grad.13
  731.4 30.5 %home.1 = (bf16[64,12288]{1,0:T(8,128)(2,1)}, f32[64,128]{1,0:T(8,128)}) custom-call(bf16[8,64,1536]{2,1,0:T(8,128)(2,1)} %bitcast.70, f32[8,64,128]{2,1,0:T(8,128)} %bitcast.84), custom_call_target="tpu_custom_call" | custom-call | bytes 5000 | tf_op jit(solution)/shard_map/home/pallas_call | solution.py:665
  763.4 1.5 adam.6
  764.8 3.9 finish.1
  768.7 10.9 %adam.7 = (f32[64,33408]{1,0:T(8,128)}, f32[64,33408]{1,0:T(8,128)}, f32[64,33408]{1,0:T(8,128)}, f32[64,33408]{1,0:T(8,128)}, bf16[64,33408]{1,0:T(8,128)(2,1)}) custom-call(f32[5]{0:T(128)} %stack.17.scalars, bf16[64,12288]{1,0:T(8,128)(2,1)} %get-tuple-element.179.grad_ref, ...), custom_call_target="tpu_custom_call", output_to_operand_aliasing={{0}: (5, {}), {1}: (6, {}), {2}: (7, {}), {3}: (8, {}), {4}... | custom-call | bytes 5000 | tf_op jit(solution)/shard_map/adam/pallas_call | solution.py:1045
  (131 shorter events, 21.1 us)
Async XLA Ops:
  7.2 316.7 %all-gather.2.cloned.1.call-start = ((), (), s32[]{:S(2)}) async-start(), calls=%async_computation.2 | async-start | bytes 4718592 | tf_op jit(solution)/shard_map/all_gather | solution.py:1243
  133.8 631.1 %reduce-scatter.5.cloned.1.call-start = ((), (), s32[]{:S(2)}) async-start(), calls=%async_computation.4 | async-start | bytes 4718592 | tf_op jit(solution)/shard_map/reduce_scatter | solution.py:1350
  133.8 172.6 %collective-permute-start.1 = (bf16[512,768]{1,0:T(8,128)(2,1)}, bf16[512,768]{1,0:T(8,128)(2,1)}, u32[]{:S(2)}, u32[]{:S(2)}) collective-permute-start(bf16[512,768]{1,0:T(8,128)(2,1)} %bitcast.94), channel_id=1, source_target_pairs={{0,16},{1,17},{2,18},{3,19},{4,20},{5,21},{6,22},{7,23},{8,24},{9,... | collective-permute-start | bytes 2359304 | tf_op jit(solution)/shard_map/ppermute | solution.py:1250
  151.4 155.1 %collective-permute-start = (bf16[512,1536]{1,0:T(8,128)(2,1)}, bf16[512,1536]{1,0:T(8,128)(2,1)}, u32[]{:S(2)}, u32[]{:S(2)}) collective-permute-start(bf16[512,1536]{1,0:T(8,128)(2,1)} %bitcast.89), channel_id=1, source_target_pairs={{0,16},{1,17},{2,18},{3,19},{4,20},{5,21},{6,22},{7,23},{8,24},{9,... | collective-permute-start | bytes 4718600 | tf_op jit(solution)/shard_map/ppermute | solution.py:1250
  170.4 0.6 copy-start.11
  171.0 16.5 %copy-start.14 = (bf16[2,2,8,64,512]{4,3,2,1,0:T(8,128)(2,1)S(1)}, bf16[2,2,8,64,512]{4,3,2,1,0:T(8,128)(2,1)}, u32[]{:S(2)}) copy-start(bf16[2,2,8,64,512]{4,3,2,1,0:T(8,128)(2,1)} %get-tuple-element.107) | copy-start | bytes 6291460
  193.2 117.1 %copy-start.16 = (bf16[8,64,1536]{2,1,0:T(8,128)(2,1)S(1)}, bf16[8,64,1536]{2,1,0:T(8,128)(2,1)}, u32[]{:S(2)}) copy-start(bf16[8,64,1536]{2,1,0:T(8,128)(2,1)} %get-tuple-element.115) | copy-start | bytes 4718596
  306.5 3.8 collective-permute-start.3
  306.6 21.5 %collective-permute-start.2 = (bf16[512,768]{1,0:T(8,128)(2,1)}, bf16[512,768]{1,0:T(8,128)(2,1)}, u32[]{:S(2)}, u32[]{:S(2)}) collective-permute-start(bf16[512,768]{1,0:T(8,128)(2,1)} %collective-permute-done.1), channel_id=1, source_target_pairs={{0,1},{1,0},{2,3},{3,2},{4,5},{5,4},{6,7},{7,6},{8,9},{9,8},{10,11... | collective-permute-start | bytes 2359304 | tf_op jit(solution)/shard_map/ppermute | solution.py:1255
  320.1 2.7 copy-start.3
  323.8 4.1 copy-start.5
  323.8 4.3 copy-start.17
  323.8 4.3 copy-start.18
  323.8 4.4 copy-start.4
  327.9 15.9 %collective-permute-start.4 = (bf16[1024,768]{1,0:T(8,128)(2,1)S(1)}, bf16[1024,768]{1,0:T(8,128)(2,1)S(1)}, u32[]{:S(2)}, u32[]{:S(2)}) collective-permute-start(bf16[1024,768]{1,0:T(8,128)(2,1)S(1)} %fusion.8), channel_id=1, source_target_pairs={{0,1},{1,0},{2,3},{3,2},{4,5},{5,4},{6,7},{7,6},{8,9},{9,8},{10,11... | collective-permute-start | bytes 4718600 | tf_op jit(solution)/shard_map/ppermute | solution.py:1310
  336.2 2.2 copy-start.1
  338.4 5.4 copy-start.6
  343.5 16.0 %collective-permute-start.5 = (bf16[1024,1536]{1,0:T(8,128)(2,1)}, bf16[1024,1536]{1,0:T(8,128)(2,1)S(1)}, u32[]{:S(2)}, u32[]{:S(2)}) collective-permute-start(bf16[1024,1536]{1,0:T(8,128)(2,1)} %convolution_convert_fusion.3), channel_id=1, source_target_pairs={{0,1},{1,0},{2,3},{3,2},{4,5},{5,4},{6,7},{7,6},{8,9},{9,8},{10,11... | collective-permute-start | bytes 9437192 | tf_op jit(solution)/shard_map/ppermute | solution.py:1310
  343.8 3.7 copy-start.8
  347.5 121.3 %collective-permute-start.7 = (bf16[512,768]{1,0:T(8,128)(2,1)}, bf16[512,768]{1,0:T(8,128)(2,1)}, u32[]{:S(2)}, u32[]{:S(2)}) collective-permute-start(bf16[512,768]{1,0:T(8,128)(2,1)} %add_convert_fusion.2), channel_id=1, source_target_pairs={{0,16},{1,17},{2,18},{3,19},{4,20},{5,21},{6,22},{7,23},{8,24},{9,... | collective-permute-start | bytes 2359304 | tf_op jit(solution)/shard_map/ppermute | solution.py:1319
  359.5 2.0 copy-start.2
  363.5 105.4 %collective-permute-start.6 = (bf16[512,768]{1,0:T(8,128)(2,1)}, bf16[512,768]{1,0:T(8,128)(2,1)}, u32[]{:S(2)}, u32[]{:S(2)}) collective-permute-start(bf16[512,768]{1,0:T(8,128)(2,1)} %add_convert_fusion), channel_id=1, source_target_pairs={{0,16},{1,17},{2,18},{3,19},{4,20},{5,21},{6,22},{7,23},{8,24},{9,... | collective-permute-start | bytes 2359304 | tf_op jit(solution)/shard_map/ppermute | solution.py:1319
  476.7 288.1 %reduce-scatter.3.cloned.1.call-start = ((), (), s32[]{:S(2)}) async-start(), calls=%async_computation.3 | async-start | bytes 4718592 | tf_op jit(solution)/shard_map/reduce_scatter | solution.py:1380
  477.2 3.4 copy-start.7
  477.2 3.8 copy-start.15
  480.5 4.2 copy-start.9
  480.5 4.2 collective-permute-start.8
  484.7 1.0 copy-start.10
  513.8 60.5 %collective-permute-start.11 = (bf16[1024,1536]{1,0:T(8,128)(2,1)}, bf16[1024,1536]{1,0:T(8,128)(2,1)}, u32[]{:S(2)}, u32[]{:S(2)}) collective-permute-start(bf16[1024,1536]{1,0:T(8,128)(2,1)} %weight_grad.7), channel_id=1, source_target_pairs={{0,1},{1,0},{2,3},{3,2},{4,5},{5,4},{6,7},{7,6},{8,9},{9,8},{10,11... | collective-permute-start | bytes 9437192 | tf_op jit(solution)/shard_map/ppermute | solution.py:1369
  513.9 39.1 %collective-permute-start.9 = (bf16[512,768]{1,0:T(8,128)(2,1)}, bf16[512,768]{1,0:T(8,128)(2,1)}, u32[]{:S(2)}, u32[]{:S(2)}) collective-permute-start(bf16[512,768]{1,0:T(8,128)(2,1)} %add_convert_fusion.1), channel_id=1, source_target_pairs={{0,16},{1,17},{2,18},{3,19},{4,20},{5,21},{6,22},{7,23},{8,24},{9,... | collective-permute-start | bytes 2359304 | tf_op jit(solution)/shard_map/ppermute | solution.py:1319
  514.9 59.5 %collective-permute-start.10 = (bf16[512,512]{1,0:T(8,128)(2,1)S(1)}, bf16[512,512]{1,0:T(8,128)(2,1)}, u32[]{:S(2)}, u32[]{:S(2)}) collective-permute-start(bf16[512,512]{1,0:T(8,128)(2,1)S(1)} %add_convert_fusion.3), channel_id=1, source_target_pairs={{0,16},{1,17},{2,18},{3,19},{4,20},{5,21},{6,22},{7,23},{8,24},{9,... | collective-permute-start | bytes 1572872 | tf_op jit(solution)/shard_map/ppermute | solution.py:1319
  591.8 1.4 copy-start.13
  591.8 2.9 copy-start.12
  591.9 134.2 %collective-permute-start.14 = (bf16[512,1536]{1,0:T(8,128)(2,1)}, bf16[512,1536]{1,0:T(8,128)(2,1)}, u32[]{:S(2)}, u32[]{:S(2)}) collective-permute-start(bf16[512,1536]{1,0:T(8,128)(2,1)} %weight_grad.8), channel_id=1, source_target_pairs={{0,16},{1,17},{2,18},{3,19},{4,20},{5,21},{6,22},{7,23},{8,24},{9,... | collective-permute-start | bytes 4718600 | tf_op jit(solution)/shard_map/ppermute | solution.py:1319
  597.4 2.2 copy-start
  597.4 2.2 copy-start.19
  597.4 2.2 copy-start.20
  602.3 2.0 collective-permute-start.12
  604.4 121.0 %collective-permute-start.13 = (f32[512,128]{1,0:T(8,128)S(1)}, f32[512,128]{1,0:T(8,128)S(1)}, u32[]{:S(2)}, u32[]{:S(2)}) collective-permute-start(f32[512,128]{1,0:T(8,128)S(1)} %slice.145), channel_id=1, source_target_pairs={{0,16},{1,17},{2,18},{3,19},{4,20},{5,21},{6,22},{7,23},{8,24},{9,... | collective-permute-start | bytes 786440 | tf_op jit(solution)/shard_map/ppermute | solution.py:1415
Sparse Core Ops, SparseCore 0:
  133.9 128.7 all-gather.1
  476.8 87.0 reduce-scatter.4
  592.0 118.2 reduce-scatter.2
